TPU v7x, 32 devices: a whole 2x2x4 slice. The times are simulated.
32 devices in a mesh: grp: 4 (over y, core), tok: 8 (over z, x).
Axes of the slice: x: 2, y: 2, z: 4, core: 2. Of those that a mesh axis runs over, the one named last changes fastest.
Arguments:
- pre_q: bfloat16 [2048, 4096], P(('grp', 'tok')), may hold values from -64 to 64
- pre_kv: bfloat16 [2048, 2048], P(('grp', 'tok')), may hold values from -8 to 8
- pre_segment: int32 [4, 512], P('grp'), may hold values from 0 to 1, never falling along the last dimension, each value on 1 to 384 neighbouring positions
- dec_q: bfloat16 [32, 4096], P(('grp', 'tok')), may hold values from -64 to 64
- cache: bfloat16 [32, 512, 2048], P(('grp', 'tok')), may hold values from -8 to 8
- cache_len: int32 [32], P(('grp', 'tok')), may hold values from 1 to 512, 8192 in all
- slot_request: int32 [32], replicated, may hold values from 0 to 31, each once
- resid: bfloat16 [2080, 4096], P('grp', 'tok'), may hold values from -64 to 64
- wo: bfloat16 [4096, 4096], P(None, 'tok'), may hold values from -0.5 to 0.5
- tenant: int32 [4, 520], P('grp'), may hold values from 0 to 3, never falling along the last dimension, each value on 1 to 260 neighbouring positions
- norm_gain: float32 [4, 4096], replicated, may hold values from 0.25 to 1.75
- w_gate: bfloat16 [4096, 12288], P(None, 'tok'), may hold values from -0.09375 to 0.09375
- w_up: bfloat16 [4096, 12288], P(None, 'tok'), may hold values from -0.09375 to 0.09375
- w_down: bfloat16 [12288, 4096], P('tok'), may hold values from -0.0546875 to 0.0546875
Outputs:
- out: bfloat16 [2080, 4096], P('grp', 'tok')
All inputs are finite; a program needn't handle non-finite values. No bound on the sum of `cache_len` on one device may be relied on, other than what follows from the above.
Results may differ from a plain program's by a relative error of at most 0.011.
Values may be sent and summed in bfloat16 or wider, within the bound.
No kernel may reach another device: no remote copies, remote signals or barrier semaphores. Data moves between devices by JAX's collectives and lax.ppermute only.
A program may use at most 128 MiB of HBM per device.

v0:
```python
import math

import jax
import jax.numpy as jnp
from jax import lax
from jax.sharding import PartitionSpec as P

D = 4096
H = 32
KVH = 8
HD = 128


epsilon = 1e-05


def shards(
    pre_q,
    pre_kv,
    pre_segment,
    dec_q,
    cache,
    cache_len,
    slot_request,
    resid,
    wo,
    tenant,
    norm_gain,
    w_gate,
    w_up,
    w_down,
):
    group = H // KVH
    width = KVH * HD
    tok_index = lax.axis_index("tok")
    local_rows = pre_q.shape[0]
    segment = pre_segment[0]
    query_pos = tok_index * local_rows + jnp.arange(local_rows)
    query_seg = lax.dynamic_slice_in_dim(segment, tok_index * local_rows, local_rows)
    queries = pre_q.reshape(local_rows, KVH, group, HD)
    piece = lax.all_gather(pre_kv, "tok", axis=0, tiled=True)
    running = jnp.full((KVH, group, local_rows), -jnp.inf, jnp.float32)
    totals = jnp.zeros((KVH, group, local_rows), jnp.float32)
    summed = jnp.zeros((KVH, group, local_rows, HD), jnp.float32)
    count = piece.shape[0]
    keys = piece[:, :width].reshape(count, KVH, HD)
    values = piece[:, width:].reshape(count, KVH, HD)
    key_pos = jnp.arange(count)
    allowed = (key_pos[None, :] <= query_pos[:, None]) & (segment[None, :] == query_seg[:, None])
    scores = jnp.einsum(
        "qkgd,nkd->kgqn", queries, keys, preferred_element_type=jnp.float32
    ) / math.sqrt(HD)
    scores = jnp.where(allowed, scores, -jnp.inf)
    highest = jnp.max(scores, axis=-1)
    anchor = jnp.where(jnp.isfinite(highest), highest, 0.0)
    weights = jnp.exp(scores - anchor[..., None]).astype(jnp.bfloat16)
    factor = jnp.exp(running - anchor)
    totals = totals * factor + jnp.sum(weights.astype(jnp.float32), axis=-1)
    summed = summed * factor[..., None] + jnp.einsum(
        "kgqn,nkd->kgqd", weights, values, preferred_element_type=jnp.float32
    )
    running, totals, summed = (highest, totals, summed)
    prefill_out = (
        (summed / totals[..., None])
        .transpose(2, 0, 1, 3)
        .reshape(local_rows, D)
        .astype(jnp.bfloat16)
    )
    all_queries = lax.all_gather(dec_q, ("grp", "tok"), axis=0, tiled=True)
    slot = lax.axis_index(("grp", "tok"))
    request = slot_request[slot]
    query_row = lax.dynamic_slice_in_dim(all_queries, request, 1, 0).reshape(KVH, group, HD)
    positions = cache.shape[1]
    entries = cache[0].reshape(positions, 2, KVH, HD)
    slot_scores = jnp.einsum(
        "kgd,pkd->kgp", query_row, entries[:, 0], preferred_element_type=jnp.float32
    ) / math.sqrt(HD)
    visible = jnp.arange(positions) < cache_len[0]
    slot_scores = jnp.where(visible, slot_scores, -jnp.inf)
    slot_top = jnp.max(slot_scores, axis=-1, keepdims=True)
    slot_weights = jnp.exp(slot_scores - slot_top).astype(jnp.bfloat16)
    slot_total = jnp.sum(slot_weights.astype(jnp.float32), axis=-1)
    slot_mixed = jnp.einsum(
        "kgp,pkd->kgd", slot_weights, entries[:, 1], preferred_element_type=jnp.float32
    )
    decode_out = (slot_mixed / slot_total[..., None]).reshape(1, D).astype(jnp.bfloat16)
    attended = jnp.concatenate([prefill_out, decode_out], axis=0)
    projected = jnp.dot(
        lax.all_gather(attended, "tok", axis=0, tiled=True), wo, preferred_element_type=jnp.float32
    )
    mixed_in = (resid.astype(jnp.float32) + projected).astype(jnp.bfloat16)
    owners = tenant[0]
    one_hot = (owners[:, None] == jnp.arange(norm_gain.shape[0])[None, :]).astype(jnp.float32)
    gathered = lax.all_gather(mixed_in, "tok", axis=1, tiled=True)
    wide = gathered.astype(jnp.float32)
    mean_square = jnp.sum(wide * wide, axis=-1) / D
    gains = jnp.dot(one_hot, norm_gain, precision=lax.Precision.HIGHEST)
    normed = (wide * lax.rsqrt(mean_square + epsilon)[:, None] * gains).astype(jnp.bfloat16)
    gate_part = jnp.dot(normed, w_gate, preferred_element_type=jnp.float32)
    lift_part = jnp.dot(normed, w_up, preferred_element_type=jnp.float32)
    hidden = (jax.nn.silu(gate_part) * lift_part).astype(jnp.bfloat16)
    terms = jnp.dot(hidden, w_down, preferred_element_type=jnp.float32)
    result = mixed_in.astype(jnp.float32) + lax.psum_scatter(
        terms.astype(jnp.bfloat16), "tok", scatter_dimension=1, tiled=True
    ).astype(jnp.float32)
    return result.astype(jnp.bfloat16)


def solution(mesh):
    in_specs = (
        P(("grp", "tok"), None),
        P(("grp", "tok"), None),
        P("grp", None),
        P(("grp", "tok"), None),
        P(("grp", "tok"), None, None),
        P(("grp", "tok")),
        P(),
        P("grp", "tok"),
        P(None, "tok"),
        P("grp", None),
        P(),
        P(None, "tok"),
        P(None, "tok"),
        P("tok", None),
    )
    out_specs = P("grp", "tok")
    return jax.shard_map(shards, mesh=mesh, in_specs=in_specs, out_specs=out_specs, check_vma=False)
```

profile of v0, /device:TPU:0, one launch (start us, length us, event | category | flops | bytes accessed | tf_op | source)
XLA Modules:
  0.0 404.8 jit_solution(13078534104000024754)
XLA Ops:
  6.5 0.7 all-gather.6.cloned.1.call-update
  7.3 1.2 dynamic_slice.10
  10.5 2.2 reshape.58
  12.7 2.9 copy.30
  16.2 74.2 %all-gather = bf16[32,1,4096]{2,1,0:T(2,128)(2,1)S(1)} all-gather(bf16[1,1,4096]{2,1,0:T(2,128)(2,1)S(1)} %bitcast.70), channel_id=1, replica_groups=mesh['grp'=4,'tok'=8] {'grp','tok'}, dimensions={0}, use_global_device_ids=true | all-gather | bytes 270336 | tf_op jit(solution)/shard_map/all_gather | solution.py:69
  91.5 1.7 fusion.23
  93.2 0.5 copy.39
  93.8 0.5 copy.40
  94.3 1.9 fusion.3
  96.3 1.3 convert_reduce_fusion
  97.6 1.5 fusion.9
  99.0 0.4 copy.29
  99.9 0.9 maximum_bitcast_fusion
  100.8 76.7 %all-gather.10.cloned.1.call-done = bf16[8,65,4096]{2,1,0:T(8,128)(2,1)} async-done(((bf16[1,65,4096]{2,1,0:T(8,128)(2,1)}), bf16[8,65,4096]{2,1,0:T(8,128)(2,1)}) %all-gather.10.cloned.1.call-update) | async-done | bytes 4259856 | tf_op jit(solution)/shard_map/all_gather | solution.py:89
  177.5 5.7 %reshape.64 = bf16[520,4096]{1,0:T(8,128)(2,1)} reshape(bf16[8,65,4096]{2,1,0:T(8,128)(2,1)} %all-gather.10.cloned.1.call-done) | data formatting | bytes 8519680
  183.2 6.7 %fusion.8 = bf16[520,512]{1,0:T(8,128)(2,1)} fusion(bf16[520,4096]{1,0:T(8,128)(2,1)} %reshape.64, bf16[4096,512]{1,0:T(8,128)(2,1)} %param.22, bf16[520,512]{1,0:T(8,128)(2,1)S(1)} %copy-done.8), kind=kOutput, calls=%fused_computation.17 | convolution fusion | flops 2181836800 | bytes 9519104 | tf_op jit(solution)/shard_map/dot_general | solution.py:88
  190.0 74.0 %all-gather.8.cloned.1.call-done = bf16[520,4096]{1,0:T(8,128)(2,1)} async-done(((bf16[520,512]{1,0:T(8,128)(2,1)}), bf16[520,4096]{1,0:T(8,128)(2,1)}) %all-gather.8.cloned.1.call-update) | async-done | bytes 4259856 | tf_op jit(solution)/shard_map/all_gather | solution.py:94
  264.0 3.3 fusion
  267.5 4.0 fusion.2
  271.5 2.0 copy-done.3
  273.4 9.3 %fusion.24 = f32[520,1536]{1,0:T(8,128)S(1)} fusion(bf16[520,4096]{1,0:T(8,128)(2,1)S(1)} %fusion.2, bf16[4096,1536]{1,0:T(8,128)(2,1)} %param.25), kind=kOutput, calls=%fused_computation.51 | convolution fusion | flops 6543114240 | bytes 20037632 | tf_op jit(solution)/shard_map/dot_general | solution.py:99
  282.8 24.8 %convolution_convert_fusion = bf16[520,4096]{1,0:T(8,128)(2,1)} fusion(bf16[1536,4096]{1,0:T(8,128)(2,1)} %param.27, bf16[520,4096]{1,0:T(8,128)(2,1)} %copy-done.3, bf16[4096,1536]{1,0:T(8,128)(2,1)} %param.26, f32[520,1536]{1,0:T(8,128)S(1)} %fusion.24), kind=kOutput, calls=%fused_computation.5 | convolution fusion | flops 13093150720 | bytes 36880384 | tf_op jit(solution)/shard_map/dot_general | solution.py:102
  307.6 88.6 %reduce-scatter.2.cloned.1.call-done = bf16[520,512]{1,0:T(8,128)(2,1)} async-done(((bf16[520,4096]{1,0:T(8,128)(2,1)}), bf16[520,512]{1,0:T(8,128)(2,1)}) %reduce-scatter.2.cloned.1.call-update) | async-done | bytes 532496 | tf_op jit(solution)/shard_map/reduce_scatter | solution.py:103
  396.3 2.0 add_convert_fusion
  (38 shorter events, 1.9 us)
Async XLA Ops:
  6.5 260.7 %copy-start = (f32[4,4096]{1,0:T(4,128)S(1)}, f32[4,4096]{1,0:T(4,128)}, u32[]{:S(2)}) copy-start(f32[4,4096]{1,0:T(4,128)} %param.24) | copy-start | bytes 196612
  6.5 9.6 %copy-start.5 = (bf16[1,4096]{1,0:T(2,128)(2,1)S(1)}, bf16[1,4096]{1,0:T(2,128)(2,1)}, u32[]{:S(2)}) copy-start(bf16[1,4096]{1,0:T(2,128)(2,1)} %param.17) | copy-start | bytes 24580
  6.5 85.0 %all-gather.6.cloned.1.call-start = ((), (), s32[]{:S(2)}) async-start(), calls=%async_computation.1 | async-start | bytes 2359296 | tf_op jit(solution)/shard_map/all_gather | solution.py:41
  7.3 84.0 %copy-start.7 = (s32[1,512]{1,0:T(1,128)S(1)}, s32[1,512]{1,0:T(1,128)}, u32[]{:S(2)}) copy-start(s32[1,512]{1,0:T(1,128)} %param.16) | copy-start | bytes 6148
  7.3 170.2 %all-gather.10.cloned.1.call-start = ((), (), s32[]{:S(2)}) async-start(), calls=%async_computation.4 | async-start | bytes 5308416 | tf_op jit(solution)/shard_map/all_gather | solution.py:89
  100.8 82.5 %copy-start.8 = (bf16[520,512]{1,0:T(8,128)(2,1)S(1)}, bf16[520,512]{1,0:T(8,128)(2,1)}, u32[]{:S(2)}) copy-start(bf16[520,512]{1,0:T(8,128)(2,1)} %param.21) | copy-start | bytes 1597444
  100.8 163.2 %all-gather.8.cloned.1.call-start = ((), (), s32[]{:S(2)}) async-start(), calls=%async_computation.2 | async-start | bytes 4792320 | tf_op jit(solution)/shard_map/all_gather | solution.py:94
  183.2 6.7 %copy-start.6 = (s32[1,520]{1,0:T(1,128)S(1)}, s32[1,520]{1,0:T(1,128)}, u32[]{:S(2)}) copy-start(s32[1,520]{1,0:T(1,128)} %param.23) | copy-start | bytes 6244
  189.9 206.4 %reduce-scatter.2.cloned.1.call-start = ((), (), s32[]{:S(2)}) async-start(), calls=%async_computation.3 | async-start | bytes 4792320 | tf_op jit(solution)/shard_map/reduce_scatter | solution.py:103
  264.0 3.5 copy-start.2
  271.4 2.0 copy-start.3
  282.8 115.5 %copy-start.1 = (f32[4,4096]{1,0:T(4,128)S(1)}, f32[4,4096]{1,0:T(4,128)}, u32[]{:S(2)}) copy-start(f32[4,4096]{1,0:T(4,128)} %param.24) | copy-start | bytes 196612
  307.6 88.7 %copy-start.4 = (bf16[520,512]{1,0:T(8,128)(2,1)S(1)}, bf16[520,512]{1,0:T(8,128)(2,1)}, u32[]{:S(2)}) copy-start(bf16[520,512]{1,0:T(8,128)(2,1)} %fusion.8) | copy-start | bytes 1597444
Sparse Core Ops, SparseCore 0:
  9.5 54.7 all-gather.5
  100.9 76.5 all-gather.9
  190.0 73.8 all-gather.7
  307.8 88.4 reduce-scatter.1
where the time goes:
time: 405 us
  waiting for transfers between devices  240 us (59%)
  blocking collectives  74.2 us (18%)
  matrix products  49 us (12%)
  local copies, waits for them, and re-layouts  18 us (4%)
  between operations  15.8 us (4%)
  other arithmetic  7.53 us (2%)
    reduce_scatter x1, waiting for transfers between devices, shards(): lax.psum_scatter(terms.astype(jnp.bfloat16), 'tok', scatter_dimension=1,...  88.6 us
    all_gather x1, waiting for transfers between devices, shards(): lax.all_gather(attended, 'tok', axis=0, tiled=True)  76.7 us
    all_gather x1, blocking collectives, shards(): all_queries = lax.all_gather(dec_q, ('grp', 'tok'), axis=0, tiled=True)  74.2 us
    all_gather x1, waiting for transfers between devices, shards(): gathered = lax.all_gather(mixed_in, 'tok', axis=1, tiled=True)  74 us
    dot_general x1, matrix products, shards(): terms = jnp.dot(hidden, w_down, preferred_element_type=jnp.float32)  24.8 us
    unnamed x22, local copies, waits for them, and re-layouts  11.9 us
    dot_general x1, matrix products, shards(): gate_part = jnp.dot(normed, w_gate, preferred_element_type=jnp.float32)  9.33 us
  transfers between devices with their start and end apart: 4, of which 3 were waited for; matrix products, arithmetic and copies ran while one was open for 2% of the time, Pallas kernels for 0%

commit v1 on v0

v1 whole, which is shorter than its diff:
```python
import functools
import math

import jax
import jax.numpy as jnp
from jax import lax
from jax.experimental import pallas as pl
from jax.experimental.pallas import tpu as pltpu
from jax.sharding import PartitionSpec as P

D = 4096
H = 32
KVH = 8
HD = 128
GROUP = H // KVH
WIDTH = KVH * HD
EPS = 1e-05
NEG = -1e30
Z_CHIPS = 4

ANY = pl.BlockSpec(memory_space=pl.ANY)
VMEM = pl.BlockSpec(memory_space=pltpu.VMEM)
SMEM = pl.BlockSpec(memory_space=pltpu.SMEM)
F32 = jnp.float32
BF16 = jnp.bfloat16


def ring_order(n):
    columns = n // Z_CHIPS
    if n % Z_CHIPS or columns % 2:
        return list(range(n))
    order = [z * columns for z in range(Z_CHIPS)]
    for i, z in enumerate(reversed(range(Z_CHIPS))):
        xs = range(1, columns) if i % 2 == 0 else range(columns - 1, 0, -1)
        order += [z * columns + x for x in xs]
    return order


def params(mib):
    return pltpu.CompilerParams(vmem_limit_bytes=mib * 2**20)


def cost(flops, moved, exps=0):
    return pl.CostEstimate(flops=int(flops), bytes_accessed=int(moved), transcendentals=int(exps))


def copies(pairs, sems):
    out = [pltpu.make_async_copy(src, dst, sems.at[i]) for i, (src, dst) in enumerate(pairs)]
    for c in out:
        c.start()
    return out


def row_parts(parts, owners, target, rows):
    n = len(parts) - 1
    half = n // 2
    pairs = []
    for i, part in enumerate(parts):
        d = i if i <= half else i - 1
        start = owners[d] * rows
        if i == half:
            pairs.append((part, target.at[pl.ds(pl.multiple_of(start, 16), rows // 2)]))
        elif i == half + 1:
            pairs.append((part, target.at[pl.ds(pl.multiple_of(start + rows // 2, 16), rows // 2)]))
        else:
            pairs.append((part, target.at[pl.ds(pl.multiple_of(start, 16), rows)]))
    return pairs


def attention_kernel(n, first, rows, owners, here, q_ref, segcol_ref, seg_ref, *rest):
    parts, (out_ref, kv, sems) = rest[: n + 1], rest[n + 1 :]
    total = kv.shape[0]
    moving = copies(row_parts(parts, owners, kv, total // n), sems)
    key_pos = lax.broadcasted_iota(jnp.int32, (rows, total), 1)
    query_pos = lax.broadcasted_iota(jnp.int32, (rows, total), 0) + (here[0] + first)
    seen = (key_pos <= query_pos) & (segcol_ref[first : first + rows, :] == seg_ref[...])
    bias = jnp.where(seen, 0.0, NEG).astype(F32)
    bias = jnp.concatenate([bias] * GROUP, axis=0)
    for c in moving:
        c.wait()
    for k in range(KVH):
        q = jnp.concatenate(
            [q_ref[first : first + rows, (k * GROUP + g) * HD : (k * GROUP + g + 1) * HD] for g in range(GROUP)],
            axis=0,
        )
        s = lax.dot_general(
            q, kv[:, k * HD : (k + 1) * HD], (((1,), (1,)), ((), ())), preferred_element_type=F32
        )
        s = s * (1.0 / math.sqrt(HD)) + bias
        w = jnp.exp(s - jnp.max(s, axis=-1, keepdims=True)).astype(BF16)
        t = jnp.sum(w.astype(F32), axis=-1, keepdims=True)
        o = jnp.dot(w, kv[:, WIDTH + k * HD : WIDTH + (k + 1) * HD], preferred_element_type=F32) / t
        for g in range(GROUP):
            out_ref[:, (k * GROUP + g) * HD : (k * GROUP + g + 1) * HD] = o[g * rows : (g + 1) * rows].astype(BF16)


def attention(n, first, rows, owners, here, q, segcol, seg, parts):
    total = seg.shape[1]
    return pl.pallas_call(
        functools.partial(attention_kernel, n, first, rows),
        out_shape=jax.ShapeDtypeStruct((rows, D), BF16),
        in_specs=[SMEM, SMEM, VMEM, VMEM, VMEM] + [ANY] * (n + 1),
        out_specs=VMEM,
        scratch_shapes=[pltpu.VMEM((total, 2 * WIDTH), BF16), pltpu.SemaphoreType.DMA((n + 1,))],
        compiler_params=params(20),
        cost_estimate=cost(4 * rows * H * HD * total, 4 * total * WIDTH, rows * H * total),
        name="prefill_attention",
    )(owners, here, q, segcol, seg, *parts)


def decode_kernel(length, q_ref, cache_ref, out_ref):
    positions = cache_ref.shape[1]
    head = lax.broadcasted_iota(jnp.int32, (H, positions), 0) // GROUP
    q = q_ref[...]
    s = jnp.zeros((H, positions), F32)
    for k in range(KVH):
        one = lax.dot_general(
            q, cache_ref[0, :, k * HD : (k + 1) * HD], (((1,), (1,)), ((), ())), preferred_element_type=F32
        )
        s = jnp.where(head == k, one, s)
    spot = lax.broadcasted_iota(jnp.int32, (H, positions), 1)
    s = jnp.where(spot < length[0], s * (1.0 / math.sqrt(HD)), NEG)
    w = jnp.exp(s - jnp.max(s, axis=-1, keepdims=True)).astype(BF16).astype(F32)
    t = jnp.sum(w, axis=-1, keepdims=True)
    o = jnp.zeros((H, HD), F32)
    for k in range(KVH):
        mine = jnp.where(head == k, w, 0.0).astype(BF16)
        o = o + jnp.dot(
            mine, cache_ref[0, :, WIDTH + k * HD : WIDTH + (k + 1) * HD], preferred_element_type=F32
        )
    out_ref[...] = (o / t).astype(BF16)


def decode(length, q, cache):
    return pl.pallas_call(
        decode_kernel,
        out_shape=jax.ShapeDtypeStruct((H, HD), BF16),
        in_specs=[SMEM, VMEM, VMEM],
        out_specs=VMEM,
        compiler_params=params(20),
        cost_estimate=cost(4 * H * WIDTH * cache.shape[1], 2 * cache.size, H * cache.shape[1]),
        name="decode_attention",
    )(length, q, cache)


def project_kernel(n, rows, extra, owners, *rest):
    if extra:
        dec_ref, perm_ref, rest = rest[0], rest[1], rest[2:]
    parts, (wo_ref, resid_ref, out_ref, x, w, sems, wsems) = rest[: n + 1], rest[n + 1 :]
    moving = copies(row_parts(parts, owners, x, rows), sems)
    steps = 4
    deep = D // steps
    slabs = [pl.ds(i * deep, deep) for i in range(steps)]
    weights = copies([(wo_ref.at[s], w.at[s]) for s in slabs], wsems)
    if extra:
        x[n * rows :, :] = jnp.dot(perm_ref[...], dec_ref[...], preferred_element_type=F32).astype(BF16)
    for c in moving:
        c.wait()
    total = resid_ref[...].astype(F32)
    for i in range(steps):
        weights[i].wait()
        cut = slice(i * deep, (i + 1) * deep)
        total = total + jnp.dot(x[:, cut], w[cut, :], preferred_element_type=F32)
    out_ref[...] = total.astype(BF16)


def project(n, rows, owners, parts, wo, resid, dec=None, perm=None):
    m, cols = resid.shape
    extra = dec is not None
    return pl.pallas_call(
        functools.partial(project_kernel, n, rows, extra),
        out_shape=jax.ShapeDtypeStruct((m, cols), BF16),
        in_specs=[SMEM] + [VMEM] * (2 * extra) + [ANY] * (n + 2) + [VMEM],
        out_specs=VMEM,
        scratch_shapes=[
            pltpu.VMEM((m, D), BF16),
            pltpu.VMEM((D, cols), BF16),
            pltpu.SemaphoreType.DMA((n + 1,)),
            pltpu.SemaphoreType.DMA((4,)),
        ],
        compiler_params=params(20),
        cost_estimate=cost(2 * m * D * cols, 2 * D * (m + cols)),
        name="out_projection",
    )(owners, *([dec, perm] if extra else []), *parts, wo, resid)


def norm_kernel(n, cut, owners, tenants_ref, gain_ref, *rest):
    parts, (out_ref, x, sems) = rest[: n + 1], rest[n + 1 :]
    m = x.shape[0]
    cols = D // n
    half = n // 2
    pairs = []
    for i, part in enumerate(parts):
        d = i if i <= half else i - 1
        at = pl.ds(pl.multiple_of(owners[d] * cols, 128), cols)
        if i == half:
            pairs.append((part, x.at[pl.ds(0, cut), at]))
        elif i == half + 1:
            pairs.append((part, x.at[pl.ds(cut, m - cut), at]))
        else:
            pairs.append((part, x.at[:, at]))
    for c in copies(pairs, sems):
        c.wait()
    square = jnp.zeros((m, 1), F32)
    for j in range(n):
        wide = x[:, j * cols : (j + 1) * cols].astype(F32)
        square = square + jnp.sum(wide * wide, axis=-1, keepdims=True)
    scale = lax.rsqrt(square / D + EPS)
    tenants = tenants_ref[...]
    for j in range(n):
        at = slice(j * cols, (j + 1) * cols)
        gain = jnp.broadcast_to(gain_ref[0:1, at], (m, cols))
        for t in range(1, gain_ref.shape[0]):
            gain = jnp.where(tenants == t, gain_ref[t : t + 1, at], gain)
        out_ref[:, at] = (x[:, at].astype(F32) * scale * gain).astype(BF16)


def normalize(n, cut, owners, tenants, gain, parts):
    m = tenants.shape[0]
    return pl.pallas_call(
        functools.partial(norm_kernel, n, cut),
        out_shape=jax.ShapeDtypeStruct((m, D), BF16),
        in_specs=[SMEM, VMEM, VMEM] + [ANY] * (n + 1),
        out_specs=VMEM,
        scratch_shapes=[pltpu.VMEM((m, D), BF16), pltpu.SemaphoreType.DMA((n + 1,))],
        compiler_params=params(20),
        cost_estimate=cost(12 * m * D, 4 * m * D),
        name="tenant_norm",
    )(owners, tenants, gain, *parts)


def swiglu_kernel(x_ref, gate_ref, up_ref, out_ref):
    x = x_ref[...]
    gate = jnp.dot(x, gate_ref[...], preferred_element_type=F32)
    lift = jnp.dot(x, up_ref[...], preferred_element_type=F32)
    out_ref[...] = (gate / (1.0 + jnp.exp(-gate)) * lift).astype(BF16)


def swiglu(x, w_gate, w_up, first, count, tile):
    m = x.shape[0]
    weight = pl.BlockSpec((D, tile), lambda i: (0, first + i))
    return pl.pallas_call(
        swiglu_kernel,
        out_shape=jax.ShapeDtypeStruct((m, count * tile), BF16),
        grid=(count,),
        in_specs=[pl.BlockSpec((m, D), lambda i: (0, 0)), weight, weight],
        out_specs=pl.BlockSpec((m, tile), lambda i: (0, i)),
        compiler_params=params(24),
        cost_estimate=cost(4 * m * D * count * tile, 4 * D * count * tile + 2 * m * D),
        name="gate_up",
    )(x, w_gate, w_up)


def down_kernel(stage, pieces, cut, blocks, *rest):
    hidden, rest = rest[:pieces], rest[pieces:]
    two = stage in ("second", "middle")
    got = 0 if stage == "first" else 2
    w_ref, rest = rest[0], rest[1:]
    arrived, rest = rest[:got], rest[got:]
    if stage == "last":
        own, rest = rest[0], rest[1:]
        outs, (w, sems) = rest[:1], rest[1:]
    else:
        outs, (w, sems) = rest[:2], rest[2:]
    cols = w.shape[-1]
    count = 2 if two else 1
    weights = copies(
        [
            (w_ref.at[:, pl.ds(pl.multiple_of(blocks[i] * cols, 128), cols)], w.at[i])
            for i in range(count)
        ],
        sems,
    )

    def block(i):
        weights[i].wait()
        total = None
        for j, h in enumerate(hidden):
            deep = h.shape[1]
            part = jnp.dot(h[...], w[i, j * deep : (j + 1) * deep, :], preferred_element_type=F32)
            total = part if total is None else total + part
        return total

    if stage == "first":
        total = block(0)
        outs[0][...] = total[:cut].astype(BF16)
        outs[1][...] = total[cut:].astype(BF16)
    elif stage == "second":
        total = block(0)
        outs[0][:cut] = (total[:cut] + arrived[0][...].astype(F32)).astype(BF16)
        outs[0][cut:] = total[cut:].astype(BF16)
        total = block(1)
        outs[1][:cut] = total[:cut].astype(BF16)
        outs[1][cut:] = (total[cut:] + arrived[1][...].astype(F32)).astype(BF16)
    elif stage == "middle":
        for i in range(2):
            outs[i][...] = (block(i) + arrived[i][...].astype(F32)).astype(BF16)
    else:
        total = block(0) + arrived[0][...].astype(F32) + arrived[1][...].astype(F32)
        outs[0][...] = (total + own[...].astype(F32)).astype(BF16)


def down(stage, cut, blocks, hidden, w_down, arrived, cols, own=None):
    m = hidden[0].shape[0]
    deep = w_down.shape[0]
    two = stage in ("second", "middle")
    if stage == "first":
        shapes = [(cut, cols), (m - cut, cols)]
    elif two:
        shapes = [(m, cols)] * 2
    else:
        shapes = [(m, cols)]
    given = list(arrived) + ([own] if stage == "last" else [])
    out = pl.pallas_call(
        functools.partial(down_kernel, stage, len(hidden), cut),
        out_shape=[jax.ShapeDtypeStruct(s, BF16) for s in shapes],
        in_specs=[SMEM] + [VMEM] * len(hidden) + [ANY] + [VMEM] * len(given),
        out_specs=[VMEM] * len(shapes),
        scratch_shapes=[pltpu.VMEM((1 + two, deep, cols), BF16), pltpu.SemaphoreType.DMA((1 + two,))],
        compiler_params=params(20),
        cost_estimate=cost(2 * m * deep * cols * (1 + two), 2 * (1 + two) * deep * cols),
        name="down_" + stage,
    )(blocks, *hidden, w_down, *given)
    return out


class Ring:
    def __init__(self, n, order, cut):
        self.n, self.half, self.cut = n, n // 2, cut
        self.fw = [(order[i], order[(i + 1) % n]) for i in range(n)]
        self.bw = [(b, a) for a, b in self.fw]

    def send(self, forward, backward):
        return lax.ppermute(forward, "tok", self.fw), lax.ppermute(backward, "tok", self.bw)

    def gather(self, own, whole_last=False):
        f = b = own
        ahead, behind = [], []
        for step in range(1, self.half):
            f, b = self.send(f, b)
            ahead.append(f)
            behind.append(b)
        if whole_last:
            last = [lax.ppermute(f, "tok", self.fw)]
        else:
            last = list(self.send(f[: self.cut], b[self.cut :]))
        return [own] + ahead + last + behind[::-1]


def shards(
    pre_q,
    pre_kv,
    pre_segment,
    dec_q,
    cache,
    cache_len,
    slot_request,
    resid,
    wo,
    tenant,
    norm_gain,
    w_gate,
    w_up,
    w_down,
):
    n, groups = lax.axis_size("tok"), lax.axis_size("grp")
    tok, grp = lax.axis_index("tok"), lax.axis_index("grp")
    local = pre_q.shape[0]
    rows = local // 2
    cols = wo.shape[1]
    order = ring_order(n)
    order_of = jnp.array(order, jnp.int32)
    place_of = jnp.array([order.index(i) for i in range(n)], jnp.int32)
    place = place_of[tok]
    owners = order_of[(place - jnp.arange(n, dtype=jnp.int32)) % n]
    here = jnp.reshape(tok * local, (1,)).astype(jnp.int32)

    parts = Ring(n, order, local // 2).gather(pre_kv)
    asked = jnp.concatenate(Ring(n, order, 0).gather(dec_q, whole_last=True), axis=0)
    choices = []
    for j in range(groups):
        request = slot_request[(grp ^ j) * n + tok]
        row = lax.dynamic_slice_in_dim(asked, (place - place_of[request % n]) % n, 1, 0)
        if j:
            row = lax.ppermute(row, "grp", [(g, g ^ j) for g in range(groups)])
        choices.append(row)
    mine = slot_request[grp * n + tok] // n
    query = lax.dynamic_slice_in_dim(jnp.concatenate(choices, axis=0), mine ^ grp, 1, 0)

    segcol = lax.dynamic_slice_in_dim(pre_segment, tok * local, local, 1).reshape(local, 1)
    spare = -(-n // 16) * 16
    own_att = [
        attention(n, c * rows, rows, owners, here, pre_q, segcol, pre_segment, parts) for c in range(2)
    ]
    own_dec = decode(cache_len, query.reshape(H, HD), cache).reshape(1, D)

    def split(a, fill):
        a = a.reshape(n, local + 1, -1)
        first = a[:, :rows].reshape(n * rows, -1)
        second = a[:, rows:local].reshape(n * rows, -1)
        tail = jnp.concatenate([a[:, local], jnp.full((spare - n, a.shape[-1]), fill, a.dtype)], axis=0)
        return first, jnp.concatenate([second, tail], axis=0)

    resids = split(resid, 0)
    tenants = split(tenant[0][:, None], 0)

    dec_parts = Ring(n, order, 0).gather(own_dec, whole_last=True)
    dec_all = jnp.concatenate(dec_parts + [jnp.zeros((spare - n, D), BF16)], axis=0)
    perm = (jnp.arange(spare)[:, None] == jnp.concatenate([owners, jnp.full((spare - n,), -1, jnp.int32)])[None, :])
    perm = perm.astype(BF16)

    results = []
    for c in range(2):
        ring = Ring(n, order, rows // 2)
        att = ring.gather(own_att[c])
        extra = (dec_all, perm) if c else ()
        mixed = project(n, rows, owners, att, wo, resids[c], *extra)
        m = mixed.shape[0]
        cut = (m // 32) * 16
        ring = Ring(n, order, cut)
        everywhere = ring.gather(mixed)
        normed = normalize(n, cut, owners, tenants[c], norm_gain, everywhere)
        tile = 256
        tiles = w_gate.shape[1] // tile
        per = 2
        hidden = [swiglu(normed, w_gate, w_up, i, min(per, tiles - i), tile) for i in range(0, tiles, per)]
        half = n // 2

        def target(d):
            return order_of[(place + d) % n]

        sent = down("first", cut, jnp.stack([target(half)]), hidden, w_down, (), cols)
        for step in range(1, half):
            got = ring.send(*sent)
            d = half - step
            blocks = jnp.stack([target(d), target(-d)])
            sent = down("second" if step == 1 else "middle", cut, blocks, hidden, w_down, got, cols)
        got = ring.send(*sent)
        results.append(
            down("last", cut, jnp.stack([target(0)]), hidden, w_down, got, cols, own=mixed)[0]
        )

    first = results[0].reshape(n, rows, cols)
    second = results[1][: n * rows].reshape(n, rows, cols)
    tail = results[1][n * rows : n * rows + n].reshape(n, 1, cols)
    return jnp.concatenate([first, second, tail], axis=1).reshape(n * (local + 1), cols)


def solution(mesh):
    in_specs = (
        P(("grp", "tok"), None),
        P(("grp", "tok"), None),
        P("grp", None),
        P(("grp", "tok"), None),
        P(("grp", "tok"), None, None),
        P(("grp", "tok")),
        P(),
        P("grp", "tok"),
        P(None, "tok"),
        P("grp", None),
        P(),
        P(None, "tok"),
        P(None, "tok"),
        P("tok", None),
    )
    out_specs = P("grp", "tok")
    return jax.shard_map(shards, mesh=mesh, in_specs=in_specs, out_specs=out_specs, check_vma=False)
```

time: 405 us -> 283 us (0.70)
  waiting for transfers between devices: 240 us -> 69.7 us
  blocking collectives: 74.2 us -> 0 us
  starting transfers between devices: 0.13 us -> 73.3 us
  Pallas kernels: 0 us -> 60.6 us
  matrix products: 49 us -> 0 us
  local copies, waits for them, and re-layouts: 18 us -> 53.2 us
  between operations: 15.8 us -> 20.3 us
    all_gather x3 -> x0, waiting for transfers between devices: 151 us -> none  [the longest x1 76.7 us: shards(): lax.all_gather(attended, 'tok', axis=0, tiled=True)]
    reduce_scatter x1 -> x0, waiting for transfers between devices: 88.6 us -> none  [shards(): lax.psum_scatter(terms.astype(jnp.bfloat16), 'tok', scatter_dimension=1,...]
    all_gather x1 -> x0, blocking collectives: 74.2 us -> none  [shards(): all_queries = lax.all_gather(dec_q, ('grp', 'tok'), axis=0, tiled=True)]
    ppermute x0 -> x73, starting transfers between devices: none -> 73.3 us  [the longest x34 40.4 us: send(): lax.ppermute(backward, 'tok', self.bw)]
    ppermute x0 -> x73, waiting for transfers between devices: none -> 69.7 us  [the longest x34 35.7 us: send(): lax.ppermute(backward, 'tok', self.bw)]
    pallas_call x0 -> x23, Pallas kernels: none -> 60.6 us  [the longest x10 20.5 us: down(): pl.pallas_call(functools.partial(down_kernel, stage, len(hidden), cut), o...]
    dot_general x7 -> x0, matrix products: 48.6 us -> none  [the longest x1 24.8 us: shards(): terms = jnp.dot(hidden, w_down, preferred_element_type=jnp.float32)]
    unnamed x22 -> x101, local copies, waits for them, and re-layouts: 11.9 us -> 35.1 us
  transfers between devices with their start and end apart: 4 -> 73, of which waited for: 3 -> 28; matrix products, arithmetic and copies ran while one was open for 2% -> 8% of each run, Pallas kernels for 0% -> 20%
where the time goes in v1:
time: 283 us; the launch traced here: 282 us
  starting transfers between devices  73.3 us (26%)
  waiting for transfers between devices  69.7 us (25%)
  Pallas kernels  60.6 us (21%)
  local copies, waits for them, and re-layouts  53.2 us (19%)
  between operations  20.3 us (7%)
  other arithmetic  5.02 us (2%)
    ppermute x34, starting transfers between devices, send(): lax.ppermute(backward, 'tok', self.bw)  40.4 us
    ppermute x34, waiting for transfers between devices, send(): lax.ppermute(backward, 'tok', self.bw)  35.7 us
    unnamed x101, local copies, waits for them, and re-layouts  35.1 us
    ppermute x34, starting transfers between devices, send(): lax.ppermute(forward, 'tok', self.fw)  29.2 us
    ppermute x34, waiting for transfers between devices, send(): lax.ppermute(forward, 'tok', self.fw)  28.3 us
    pallas_call x10, Pallas kernels, down(): pl.pallas_call(functools.partial(down_kernel, stage, len(hidden), cut), o...  20.5 us
    pallas_call x6, Pallas kernels, swiglu(): pl.pallas_call(swiglu_kernel, out_shape=jax.ShapeDtypeStruct((m, count *...  19.3 us
    pallas_call x2, Pallas kernels, attention(): pl.pallas_call(functools.partial(attention_kernel, n, first, rows), out_s...  6.91 us
  transfers between devices with their start and end apart: 73, of which 28 were waited for; matrix products, arithmetic and copies ran while one was open for 8% of the time, Pallas kernels for 20%

profile of v1, /device:TPU:0, one launch (start us, length us, event | category | flops | bytes accessed | tf_op | source)
XLA Modules:
  0.0 282.0 jit_solution(14888177948469452577)
XLA Ops:
  3.0 6.5 %collective-permute-done.4.rest_8_ = bf16[64,2048]{1,0:T(8,128)(2,1)S(1)} collective-permute-done((bf16[64,2048]{1,0:T(8,128)(2,1)}, bf16[64,2048]{1,0:T(8,128)(2,1)S(1)}, u32[]{:S(2)}, u32[]{:S(2)}) %collective-permute-start.4) | collective-permute-done | bytes 262176 | tf_op jit(solution)/shard_map/ppermute | solution.py:334
  11.6 5.5 %collective-permute-done.5.rest_7_ = bf16[64,2048]{1,0:T(8,128)(2,1)S(1)} collective-permute-done((bf16[64,2048]{1,0:T(8,128)(2,1)S(1)}, bf16[64,2048]{1,0:T(8,128)(2,1)S(1)}, u32[]{:S(2)}, u32[]{:S(2)}) %collective-permute-start.5) | collective-permute-done | bytes 262176 | tf_op jit(solution)/shard_map/ppermute | solution.py:334
  39.5 3.5 %prefill_attention.2.rest_0_ = bf16[32,4096]{1,0:T(8,128)(2,1)S(1)} custom-call(s32[8]{0:T(128)S(1)} %gather_fusion, s32[1]{0:T(128)} %bitcast.2.here, bf16[64,4096]{1,0:T(8,128)(2,1)S(1)} %copy-done.11, s32[64,1]{1,0:T(8,128)S(1)} %copy.30.segcol_ref, s32[1,512]{1,0:T(1,128)S(1)} %copy-done.40, bf16[64,2048]{1,0:T(8,128)(2,1)S(1)} %copy-done.12, ...), custom_call_target="tpu_custom_call" | custom-call | flops 268435456 | bytes 2097152 | tf_op jit(solution)/shard_map/prefill_attention/pallas_call | solution.py:99
  50.2 3.5 %prefill_attention.3.rest_2_ = bf16[32,4096]{1,0:T(8,128)(2,1)S(1)} custom-call(s32[8]{0:T(128)S(1)} %gather_fusion, s32[1]{0:T(128)} %bitcast.2.here, bf16[64,4096]{1,0:T(8,128)(2,1)S(1)} %copy-done.11, s32[64,1]{1,0:T(8,128)S(1)} %copy-done.23, s32[1,512]{1,0:T(1,128)S(1)} %copy-done.40, bf16[64,2048]{1,0:T(8,128)(2,1)S(1)} %copy-done.12, ...), custom_call_target="tpu_custom_call" | custom-call | flops 268435456 | bytes 2097152 | tf_op jit(solution)/shard_map/prefill_attention/pallas_call | solution.py:99
  56.4 5.6 %collective-permute-done.32 = bf16[1,4096]{1,0:T(2,128)(2,1)S(1)} collective-permute-done((bf16[1,4096]{1,0:T(2,128)(2,1)S(1)}, bf16[1,4096]{1,0:T(2,128)(2,1)S(1)}, u32[]{:S(2)}, u32[]{:S(2)}) %collective-permute-start.32) | collective-permute-done | bytes 8224 | tf_op jit(solution)/shard_map/ppermute | solution.py:334
  66.2 3.3 %collective-permute-done.33 = bf16[1,4096]{1,0:T(2,128)(2,1)S(1)} collective-permute-done((bf16[1,4096]{1,0:T(2,128)(2,1)S(1)}, bf16[1,4096]{1,0:T(2,128)(2,1)S(1)}, u32[]{:S(2)}, u32[]{:S(2)}) %collective-permute-start.33) | collective-permute-done | bytes 8224 | tf_op jit(solution)/shard_map/ppermute | solution.py:334
  73.7 3.3 %collective-permute-done.34 = bf16[1,4096]{1,0:T(2,128)(2,1)S(1)} collective-permute-done((bf16[1,4096]{1,0:T(2,128)(2,1)S(1)}, bf16[1,4096]{1,0:T(2,128)(2,1)S(1)}, u32[]{:S(2)}, u32[]{:S(2)}) %collective-permute-start.34) | collective-permute-done | bytes 8224 | tf_op jit(solution)/shard_map/ppermute | solution.py:334
  91.9 3.3 %collective-permute-done.41 = bf16[1,4096]{1,0:T(2,128)(2,1)S(1)} collective-permute-done((bf16[1,4096]{1,0:T(2,128)(2,1)S(1)}, bf16[1,4096]{1,0:T(2,128)(2,1)S(1)}, u32[]{:S(2)}, u32[]{:S(2)}) %collective-permute-start.41) | collective-permute-done | bytes 8224 | tf_op jit(solution)/shard_map/ppermute | solution.py:385
  105.5 7.7 %collective-permute-done.42 = bf16[1,4096]{1,0:T(2,128)(2,1)S(1)} collective-permute-done((bf16[1,4096]{1,0:T(2,128)(2,1)S(1)}, bf16[1,4096]{1,0:T(2,128)(2,1)S(1)}, u32[]{:S(2)}, u32[]{:S(2)}) %collective-permute-start.42) | collective-permute-done | bytes 8224 | tf_op jit(solution)/shard_map/ppermute | solution.py:334
  134.4 3.6 %out_projection.2.rest_0_.rest_6_ = bf16[256,512]{1,0:T(8,128)(2,1)S(1)} custom-call(s32[8]{0:T(128)S(1)} %gather_fusion, bf16[32,4096]{1,0:T(8,128)(2,1)S(1)} %prefill_attention.2.rest_0_, bf16[32,4096]{1,0:T(8,128)(2,1)} %collective-permute-done.8.rest_1_, bf16[32,4096]{1,0:T(8,128)(2,1)} %collective-permute-done.9.rest_2_, ...), custom_call_target="tpu_custom_call" | custom-call | flops 1073741824 | bytes 6291456 | tf_op jit(solution)/shard_map/out_projection/pallas_call | solution.py:170
  145.5 3.1 %out_projection.3.rest_0_.rest_6_ = bf16[272,512]{1,0:T(8,128)(2,1)S(1)} custom-call(s32[8]{0:T(128)S(1)} %copy-done.37, bf16[16,4096]{1,0:T(8,128)(2,1)S(1)} %concatenate.24.rest_0_, bf16[16,16]{1,0:T(8,128)(2,1)S(1)} %fusion.4.rest_1_, bf16[32,4096]{1,0:T(8,128)(2,1)S(1)} %prefill_attention.3.rest_2_, ...), custom_call_target="tpu_custom_call" | custom-call | flops 1140850688 | bytes 6422528 | tf_op jit(solution)/shard_map/out_projection/pallas_call | solution.py:170
  152.8 5.5 %collective-permute-done.61.rest_8_ = bf16[272,512]{1,0:T(8,128)(2,1)S(1)} collective-permute-done((bf16[272,512]{1,0:T(8,128)(2,1)S(1)}, bf16[272,512]{1,0:T(8,128)(2,1)S(1)}, u32[]{:S(2)}, u32[]{:S(2)}) %collective-permute-start.61) | collective-permute-done | bytes 278560 | tf_op jit(solution)/shard_map/ppermute | solution.py:334
  166.2 3.7 %collective-permute-done.62.rest_7_ = bf16[272,512]{1,0:T(8,128)(2,1)S(1)} collective-permute-done((bf16[272,512]{1,0:T(8,128)(2,1)S(1)}, bf16[272,512]{1,0:T(8,128)(2,1)S(1)}, u32[]{:S(2)}, u32[]{:S(2)}) %collective-permute-start.62) | collective-permute-done | bytes 278560 | tf_op jit(solution)/shard_map/ppermute | solution.py:334
  187.3 3.5 %tenant_norm.2.x_ref = bf16[256,4096]{1,0:T(8,128)(2,1)S(1)} custom-call(s32[8]{0:T(128)S(1)} %copy-done.38, s32[256,1]{1,0:T(8,128)S(1)} %reshape.110.tenants_ref, f32[4,4096]{1,0:T(4,128)S(1)} %copy-done.32, bf16[256,512]{1,0:T(8,128)(2,1)S(1)} %out_projection.2.rest_0_.rest_6_, bf16[256,512]{1,0:T(8,128)(2,1)S(1)} %collective-permute-done.16.rest_1_, ...), custom_call_target="tpu_custom_call" | custom-call | flops 12582912 | bytes 4194304 | tf_op jit(solution)/shard_map/tenant_norm/pallas_call | solution.py:220
  190.8 4.6 %copy-done = bf16[4096,1536]{1,0:T(8,128)(2,1)S(1)} copy-done((bf16[4096,1536]{1,0:T(8,128)(2,1)S(1)}, bf16[4096,1536]{1,0:T(8,128)(2,1)}, u32[]{:S(2)}) %copy-start) | copy-done | bytes 12582936
  195.4 4.6 %copy-done.2 = bf16[4096,1536]{1,0:T(8,128)(2,1)S(1)} copy-done((bf16[4096,1536]{1,0:T(8,128)(2,1)S(1)}, bf16[4096,1536]{1,0:T(8,128)(2,1)}, u32[]{:S(2)}) %copy-start.2) | copy-done | bytes 12582936
  200.0 3.2 %gate_up.8.rest_2_ = bf16[256,512]{1,0:T(8,128)(2,1)S(1)} custom-call(bf16[256,4096]{1,0:T(8,128)(2,1)S(1)} %tenant_norm.2.x_ref, bf16[4096,1536]{1,0:T(8,128)(2,1)S(1)} %copy-done, bf16[4096,1536]{1,0:T(8,128)(2,1)S(1)} %copy-done.2), custom_call_target="tpu_custom_call" | custom-call | flops 2147483648 | bytes 10485760 | tf_op jit(solution)/shard_map/gate_up/pallas_call | solution.py:242
  203.2 3.2 %gate_up.7.rest_1_ = bf16[256,512]{1,0:T(8,128)(2,1)S(1)} custom-call(bf16[256,4096]{1,0:T(8,128)(2,1)S(1)} %tenant_norm.2.x_ref, bf16[4096,1536]{1,0:T(8,128)(2,1)S(1)} %copy-done, bf16[4096,1536]{1,0:T(8,128)(2,1)S(1)} %copy-done.2), custom_call_target="tpu_custom_call" | custom-call | flops 2147483648 | bytes 10485760 | tf_op jit(solution)/shard_map/gate_up/pallas_call | solution.py:242
  208.0 3.1 %gate_up.6.rest_0_ = bf16[256,512]{1,0:T(8,128)(2,1)S(1)} custom-call(bf16[256,4096]{1,0:T(8,128)(2,1)S(1)} %copy-done.5, bf16[4096,1536]{1,0:T(8,128)(2,1)S(1)} %copy-done, bf16[4096,1536]{1,0:T(8,128)(2,1)S(1)} %copy-done.2), custom_call_target="tpu_custom_call" | custom-call | flops 2147483648 | bytes 10485760 | tf_op jit(solution)/shard_map/gate_up/pallas_call | solution.py:242
  218.4 4.6 %copy-done.1 = bf16[4096,1536]{1,0:T(8,128)(2,1)S(1)} copy-done((bf16[4096,1536]{1,0:T(8,128)(2,1)S(1)}, bf16[4096,1536]{1,0:T(8,128)(2,1)}, u32[]{:S(2)}) %copy-start.1) | copy-done | bytes 12582936
  222.9 4.6 %copy-done.3 = bf16[4096,1536]{1,0:T(8,128)(2,1)S(1)} copy-done((bf16[4096,1536]{1,0:T(8,128)(2,1)S(1)}, bf16[4096,1536]{1,0:T(8,128)(2,1)}, u32[]{:S(2)}) %copy-start.3) | copy-done | bytes 12582936
  227.5 3.3 %gate_up.11.rest_2_ = bf16[272,512]{1,0:T(8,128)(2,1)S(1)} custom-call(bf16[272,4096]{1,0:T(8,128)(2,1)S(1)} %tenant_norm.3.x_ref, bf16[4096,1536]{1,0:T(8,128)(2,1)S(1)} %copy-done.1, bf16[4096,1536]{1,0:T(8,128)(2,1)S(1)} %copy-done.3), custom_call_target="tpu_custom_call" | custom-call | flops 2281701376 | bytes 10616832 | tf_op jit(solution)/shard_map/gate_up/pallas_call | solution.py:242
  230.8 3.3 %gate_up.10.rest_1_ = bf16[272,512]{1,0:T(8,128)(2,1)S(1)} custom-call(bf16[272,4096]{1,0:T(8,128)(2,1)S(1)} %tenant_norm.3.x_ref, bf16[4096,1536]{1,0:T(8,128)(2,1)S(1)} %copy-done.1, bf16[4096,1536]{1,0:T(8,128)(2,1)S(1)} %copy-done.3), custom_call_target="tpu_custom_call" | custom-call | flops 2281701376 | bytes 10616832 | tf_op jit(solution)/shard_map/gate_up/pallas_call | solution.py:242
  234.1 3.3 %gate_up.9.rest_0_ = bf16[272,512]{1,0:T(8,128)(2,1)S(1)} custom-call(bf16[272,4096]{1,0:T(8,128)(2,1)S(1)} %tenant_norm.3.x_ref, bf16[4096,1536]{1,0:T(8,128)(2,1)S(1)} %copy-done.1, bf16[4096,1536]{1,0:T(8,128)(2,1)S(1)} %copy-done.3), custom_call_target="tpu_custom_call" | custom-call | flops 2281701376 | bytes 10616832 | tf_op jit(solution)/shard_map/gate_up/pallas_call | solution.py:242
  (295 shorter events, 162.7 us)
Async XLA Ops:
  17.0 13.4 %collective-permute-start.6 = (bf16[64,2048]{1,0:T(8,128)(2,1)S(1)}, bf16[64,2048]{1,0:T(8,128)(2,1)S(1)}, u32[]{:S(2)}, u32[]{:S(2)}) collective-permute-start(bf16[64,2048]{1,0:T(8,128)(2,1)S(1)} %collective-permute-done.5.rest_7_), channel_id=1, source_target_pairs={{2,0},{4,2},{6,4},{7,6},{5,7},{3,5},{1,3},{0,1},{10,8},{12,10},{14... | collective-permute-start | bytes 786440 | tf_op jit(solution)/shard_map/ppermute | solution.py:334
  18.4 13.4 %collective-permute-start.2 = (bf16[64,2048]{1,0:T(8,128)(2,1)S(1)}, bf16[64,2048]{1,0:T(8,128)(2,1)S(1)}, u32[]{:S(2)}, u32[]{:S(2)}) collective-permute-start(bf16[64,2048]{1,0:T(8,128)(2,1)S(1)} %collective-permute-done.1.rest_2_), channel_id=1, source_target_pairs={{0,2},{2,4},{4,6},{6,7},{7,5},{5,3},{3,1},{1,0},{8,10},{10,12},{12... | collective-permute-start | bytes 786440 | tf_op jit(solution)/shard_map/ppermute | solution.py:334
  43.7 43.4 %collective-permute-start.12 = (bf16[32,4096]{1,0:T(8,128)(2,1)S(1)}, bf16[32,4096]{1,0:T(8,128)(2,1)}, u32[]{:S(2)}, u32[]{:S(2)}) collective-permute-start(bf16[32,4096]{1,0:T(8,128)(2,1)S(1)} %prefill_attention.2.rest_0_), channel_id=1, source_target_pairs={{2,0},{4,2},{6,4},{7,6},{5,7},{3,5},{1,3},{0,1},{10,8},{12,10},{14... | collective-permute-start | bytes 786440 | tf_op jit(solution)/shard_map/ppermute | solution.py:334
  45.2 43.5 %collective-permute-start.8 = (bf16[32,4096]{1,0:T(8,128)(2,1)S(1)}, bf16[32,4096]{1,0:T(8,128)(2,1)}, u32[]{:S(2)}, u32[]{:S(2)}) collective-permute-start(bf16[32,4096]{1,0:T(8,128)(2,1)S(1)} %prefill_attention.2.rest_0_), channel_id=1, source_target_pairs={{0,2},{2,4},{4,6},{6,7},{7,5},{5,3},{3,1},{1,0},{8,10},{10,12},{12... | collective-permute-start | bytes 786440 | tf_op jit(solution)/shard_map/ppermute | solution.py:334
  53.7 35.5 %collective-permute-start.53 = (bf16[32,4096]{1,0:T(8,128)(2,1)S(1)}, bf16[32,4096]{1,0:T(8,128)(2,1)S(1)}, u32[]{:S(2)}, u32[]{:S(2)}) collective-permute-start(bf16[32,4096]{1,0:T(8,128)(2,1)S(1)} %prefill_attention.3.rest_2_), channel_id=1, source_target_pairs={{2,0},{4,2},{6,4},{7,6},{5,7},{3,5},{1,3},{0,1},{10,8},{12,10},{14... | collective-permute-start | bytes 786440 | tf_op jit(solution)/shard_map/ppermute | solution.py:334
  55.3 35.4 %collective-permute-start.49 = (bf16[32,4096]{1,0:T(8,128)(2,1)S(1)}, bf16[32,4096]{1,0:T(8,128)(2,1)S(1)}, u32[]{:S(2)}, u32[]{:S(2)}) collective-permute-start(bf16[32,4096]{1,0:T(8,128)(2,1)S(1)} %prefill_attention.3.rest_2_), channel_id=1, source_target_pairs={{0,2},{2,4},{4,6},{6,7},{7,5},{5,3},{3,1},{1,0},{8,10},{10,12},{12... | collective-permute-start | bytes 786440 | tf_op jit(solution)/shard_map/ppermute | solution.py:334
  87.1 15.9 %collective-permute-start.13 = (bf16[32,4096]{1,0:T(8,128)(2,1)}, bf16[32,4096]{1,0:T(8,128)(2,1)}, u32[]{:S(2)}, u32[]{:S(2)}) collective-permute-start(bf16[32,4096]{1,0:T(8,128)(2,1)} %collective-permute-done.12.rest_8_), channel_id=1, source_target_pairs={{2,0},{4,2},{6,4},{7,6},{5,7},{3,5},{1,3},{0,1},{10,8},{12,10},{14... | collective-permute-start | bytes 786440 | tf_op jit(solution)/shard_map/ppermute | solution.py:334
  88.7 15.8 %collective-permute-start.9 = (bf16[32,4096]{1,0:T(8,128)(2,1)}, bf16[32,4096]{1,0:T(8,128)(2,1)}, u32[]{:S(2)}, u32[]{:S(2)}) collective-permute-start(bf16[32,4096]{1,0:T(8,128)(2,1)} %collective-permute-done.8.rest_1_), channel_id=1, source_target_pairs={{0,2},{2,4},{4,6},{6,7},{7,5},{5,3},{3,1},{1,0},{8,10},{10,12},{12... | collective-permute-start | bytes 786440 | tf_op jit(solution)/shard_map/ppermute | solution.py:334
  89.2 29.4 %collective-permute-start.54 = (bf16[32,4096]{1,0:T(8,128)(2,1)S(1)}, bf16[32,4096]{1,0:T(8,128)(2,1)S(1)}, u32[]{:S(2)}, u32[]{:S(2)}) collective-permute-start(bf16[32,4096]{1,0:T(8,128)(2,1)S(1)} %collective-permute-done.53.rest_10_), channel_id=1, source_target_pairs={{2,0},{4,2},{6,4},{7,6},{5,7},{3,5},{1,3},{0,1},{10,8},{12,10},{14... | collective-permute-start | bytes 786440 | tf_op jit(solution)/shard_map/ppermute | solution.py:334
  90.7 28.3 %collective-permute-start.50 = (bf16[32,4096]{1,0:T(8,128)(2,1)S(1)}, bf16[32,4096]{1,0:T(8,128)(2,1)}, u32[]{:S(2)}, u32[]{:S(2)}) collective-permute-start(bf16[32,4096]{1,0:T(8,128)(2,1)S(1)} %collective-permute-done.49.rest_3_), channel_id=1, source_target_pairs={{0,2},{2,4},{4,6},{6,7},{7,5},{5,3},{3,1},{1,0},{8,10},{10,12},{12... | collective-permute-start | bytes 786440 | tf_op jit(solution)/shard_map/ppermute | solution.py:334
  102.9 19.7 %collective-permute-start.14 = (bf16[32,4096]{1,0:T(8,128)(2,1)}, bf16[32,4096]{1,0:T(8,128)(2,1)S(1)}, u32[]{:S(2)}, u32[]{:S(2)}) collective-permute-start(bf16[32,4096]{1,0:T(8,128)(2,1)} %collective-permute-done.13.rest_7_), channel_id=1, source_target_pairs={{2,0},{4,2},{6,4},{7,6},{5,7},{3,5},{1,3},{0,1},{10,8},{12,10},{14... | collective-permute-start | bytes 786440 | tf_op jit(solution)/shard_map/ppermute | solution.py:334
  104.5 18.5 %collective-permute-start.10 = (bf16[32,4096]{1,0:T(8,128)(2,1)}, bf16[32,4096]{1,0:T(8,128)(2,1)S(1)}, u32[]{:S(2)}, u32[]{:S(2)}) collective-permute-start(bf16[32,4096]{1,0:T(8,128)(2,1)} %collective-permute-done.9.rest_2_), channel_id=1, source_target_pairs={{0,2},{2,4},{4,6},{6,7},{7,5},{5,3},{3,1},{1,0},{8,10},{10,12},{12... | collective-permute-start | bytes 786440 | tf_op jit(solution)/shard_map/ppermute | solution.py:334
  127.7 12.4 %collective-permute-start.45 = (bf16[1,4096]{1,0:T(2,128)(2,1)S(1)}, bf16[1,4096]{1,0:T(2,128)(2,1)S(1)}, u32[]{:S(2)}, u32[]{:S(2)}) collective-permute-start(bf16[1,4096]{1,0:T(2,128)(2,1)S(1)} %collective-permute-done.44), channel_id=1, source_target_pairs={{0,2},{2,4},{4,6},{6,7},{7,5},{5,3},{3,1},{1,0},{8,10},{10,12},{12... | collective-permute-start | bytes 24584 | tf_op jit(solution)/shard_map/ppermute | solution.py:344
  138.0 12.7 %collective-permute-start.20 = (bf16[256,512]{1,0:T(8,128)(2,1)S(1)}, bf16[256,512]{1,0:T(8,128)(2,1)S(1)}, u32[]{:S(2)}, u32[]{:S(2)}) collective-permute-start(bf16[256,512]{1,0:T(8,128)(2,1)S(1)} %out_projection.2.rest_0_.rest_6_), channel_id=1, source_target_pairs={{2,0},{4,2},{6,4},{7,6},{5,7},{3,5},{1,3},{0,1},{10,8},{12,10},{14... | collective-permute-start | bytes 786440 | tf_op jit(solution)/shard_map/ppermute | solution.py:334
  138.3 12.7 %collective-permute-start.16 = (bf16[256,512]{1,0:T(8,128)(2,1)S(1)}, bf16[256,512]{1,0:T(8,128)(2,1)S(1)}, u32[]{:S(2)}, u32[]{:S(2)}) collective-permute-start(bf16[256,512]{1,0:T(8,128)(2,1)S(1)} %out_projection.2.rest_0_.rest_6_), channel_id=1, source_target_pairs={{0,2},{2,4},{4,6},{6,7},{7,5},{5,3},{3,1},{1,0},{8,10},{10,12},{12... | collective-permute-start | bytes 786440 | tf_op jit(solution)/shard_map/ppermute | solution.py:334
  150.7 13.2 %collective-permute-start.21 = (bf16[256,512]{1,0:T(8,128)(2,1)S(1)}, bf16[256,512]{1,0:T(8,128)(2,1)S(1)}, u32[]{:S(2)}, u32[]{:S(2)}) collective-permute-start(bf16[256,512]{1,0:T(8,128)(2,1)S(1)} %collective-permute-done.20.rest_8_), channel_id=1, source_target_pairs={{2,0},{4,2},{6,4},{7,6},{5,7},{3,5},{1,3},{0,1},{10,8},{12,10},{14... | collective-permute-start | bytes 786440 | tf_op jit(solution)/shard_map/ppermute | solution.py:334
  151.0 13.3 %collective-permute-start.17 = (bf16[256,512]{1,0:T(8,128)(2,1)S(1)}, bf16[256,512]{1,0:T(8,128)(2,1)}, u32[]{:S(2)}, u32[]{:S(2)}) collective-permute-start(bf16[256,512]{1,0:T(8,128)(2,1)S(1)} %collective-permute-done.16.rest_1_), channel_id=1, source_target_pairs={{0,2},{2,4},{4,6},{6,7},{7,5},{5,3},{3,1},{1,0},{8,10},{10,12},{12... | collective-permute-start | bytes 786440 | tf_op jit(solution)/shard_map/ppermute | solution.py:334
  169.9 14.0 %collective-permute-start.63 = (bf16[272,512]{1,0:T(8,128)(2,1)S(1)}, bf16[272,512]{1,0:T(8,128)(2,1)S(1)}, u32[]{:S(2)}, u32[]{:S(2)}) collective-permute-start(bf16[272,512]{1,0:T(8,128)(2,1)S(1)} %collective-permute-done.62.rest_7_), channel_id=1, source_target_pairs={{2,0},{4,2},{6,4},{7,6},{5,7},{3,5},{1,3},{0,1},{10,8},{12,10},{14... | collective-permute-start | bytes 835592 | tf_op jit(solution)/shard_map/ppermute | solution.py:334
  170.2 15.4 %collective-permute-start.59 = (bf16[272,512]{1,0:T(8,128)(2,1)S(1)}, bf16[272,512]{1,0:T(8,128)(2,1)S(1)}, u32[]{:S(2)}, u32[]{:S(2)}) collective-permute-start(bf16[272,512]{1,0:T(8,128)(2,1)S(1)} %collective-permute-done.58.rest_2_), channel_id=1, source_target_pairs={{0,2},{2,4},{4,6},{6,7},{7,5},{5,3},{3,1},{1,0},{8,10},{10,12},{12... | collective-permute-start | bytes 835592 | tf_op jit(solution)/shard_map/ppermute | solution.py:334
  173.5 13.7 %collective-permute-start.23 = (bf16[128,512]{1,0:T(8,128)(2,1)}, bf16[128,512]{1,0:T(8,128)(2,1)}, u32[]{:S(2)}, u32[]{:S(2)}) collective-permute-start(bf16[128,512]{1,0:T(8,128)(2,1)} %slice.80), channel_id=1, source_target_pairs={{2,0},{4,2},{6,4},{7,6},{5,7},{3,5},{1,3},{0,1},{10,8},{12,10},{14... | collective-permute-start | bytes 393224 | tf_op jit(solution)/shard_map/ppermute | solution.py:334
  184.6 30.9 %collective-permute-start.64 = (bf16[144,512]{1,0:T(8,128)(2,1)}, bf16[144,512]{1,0:T(8,128)(2,1)S(1)}, u32[]{:S(2)}, u32[]{:S(2)}) collective-permute-start(bf16[144,512]{1,0:T(8,128)(2,1)} %slice.86), channel_id=1, source_target_pairs={{2,0},{4,2},{6,4},{7,6},{5,7},{3,5},{1,3},{0,1},{10,8},{12,10},{14... | collective-permute-start | bytes 442376 | tf_op jit(solution)/shard_map/ppermute | solution.py:334
  186.2 29.3 %collective-permute-start.60 = (bf16[128,512]{1,0:T(8,128)(2,1)}, bf16[128,512]{1,0:T(8,128)(2,1)S(1)}, u32[]{:S(2)}, u32[]{:S(2)}) collective-permute-start(bf16[128,512]{1,0:T(8,128)(2,1)} %slice.85), channel_id=1, source_target_pairs={{0,2},{2,4},{4,6},{6,7},{7,5},{5,3},{3,1},{1,0},{8,10},{10,12},{12... | collective-permute-start | bytes 393224 | tf_op jit(solution)/shard_map/ppermute | solution.py:334
  213.4 28.8 %collective-permute-start.24 = (bf16[128,512]{1,0:T(8,128)(2,1)}, bf16[128,512]{1,0:T(8,128)(2,1)}, u32[]{:S(2)}, u32[]{:S(2)}) collective-permute-start(bf16[128,512]{1,0:T(8,128)(2,1)} %get-tuple-element.21), channel_id=1, source_target_pairs={{0,2},{2,4},{4,6},{6,7},{7,5},{5,3},{3,1},{1,0},{8,10},{10,12},{12... | collective-permute-start | bytes 393224 | tf_op jit(solution)/shard_map/ppermute | solution.py:334
  214.1 28.0 %collective-permute-start.25 = (bf16[128,512]{1,0:T(8,128)(2,1)}, bf16[128,512]{1,0:T(8,128)(2,1)}, u32[]{:S(2)}, u32[]{:S(2)}) collective-permute-start(bf16[128,512]{1,0:T(8,128)(2,1)} %get-tuple-element.22), channel_id=1, source_target_pairs={{2,0},{4,2},{6,4},{7,6},{5,7},{3,5},{1,3},{0,1},{10,8},{12,10},{14... | collective-permute-start | bytes 393224 | tf_op jit(solution)/shard_map/ppermute | solution.py:334
  (98 other events, 1020.2 us)

commit v2 on v0

v2 whole, which is shorter than its diff:
```python
import functools
import math

import jax
import jax.numpy as jnp
from jax import lax
from jax.experimental import pallas as pl
from jax.experimental.pallas import tpu as pltpu
from jax.sharding import PartitionSpec as P

D = 4096
H = 32
KVH = 8
HD = 128
GROUP = H // KVH
WIDTH = KVH * HD
EPS = 1e-05
NEG = -1e30
Z_CHIPS = 4

HBM = pl.BlockSpec(memory_space=pltpu.HBM)
VMEM = pl.BlockSpec(memory_space=pltpu.VMEM)
SMEM = pl.BlockSpec(memory_space=pltpu.SMEM)
F32 = jnp.float32
BF16 = jnp.bfloat16


def ring_order(n):
    columns = n // Z_CHIPS
    if n % Z_CHIPS or columns % 2:
        return list(range(n))
    order = [z * columns for z in range(Z_CHIPS)]
    for i, z in enumerate(reversed(range(Z_CHIPS))):
        xs = range(1, columns) if i % 2 == 0 else range(columns - 1, 0, -1)
        order += [z * columns + x for x in xs]
    return order


def params(mib):
    return pltpu.CompilerParams(vmem_limit_bytes=mib * 2**20)


STEP = pl.CostEstimate(flops=500_000_000, bytes_accessed=1_000_000, transcendentals=0)


def copies(pairs, sems):
    out = [pltpu.make_async_copy(src, dst, sems.at[i]) for i, (src, dst) in enumerate(pairs)]
    for c in out:
        c.start()
    return out


def spread(parts, owners, target, rows):
    n, half = len(parts), len(parts) // 2
    pairs = []
    for i, part in enumerate(parts):
        d = i if n % 2 == 0 or i <= half else i - 1
        start, size = owners[d] * rows, rows
        if n % 2 and d == half:
            start, size = start + (i - half) * (rows // 2), rows // 2
        pairs.append((part, target.at[pl.ds(pl.multiple_of(start, 16), size)]))
    return pairs


def attention_kernel(count, first, rows, owners, q_in, seg_ref, *rest):
    parts, (out_ref, kv, q, sems) = rest[:count], rest[-4:]
    total = kv.shape[0]
    local = q_in.shape[0]
    moving = copies(spread(parts, owners, kv, local) + [(q_in.at[pl.ds(first, rows)], q)], sems)
    key_pos = lax.broadcasted_iota(jnp.int32, (rows, total), 1)
    query_pos = lax.broadcasted_iota(jnp.int32, (rows, total), 0) + (owners[0] * local + first)
    span = jnp.broadcast_to(seg_ref[...], (rows, total)).astype(F32)
    own_span = jnp.sum(jnp.where(key_pos == query_pos, span, 0.0), axis=-1, keepdims=True)
    seen = (key_pos <= query_pos) & (span == own_span)
    bias = jnp.where(seen, 0.0, NEG).astype(F32)
    bias = jnp.concatenate([bias] * GROUP, axis=0)
    if len(rest) > count + 4:
        out_ref[H * rows :, :] = rest[count][...]
    for c in moving:
        c.wait()
    for k in range(KVH):
        heads = range(k * GROUP, (k + 1) * GROUP)
        four = jnp.concatenate([q[:, i * HD : (i + 1) * HD] for i in heads], axis=0)
        s = lax.dot_general(
            four, kv[:, k * HD : (k + 1) * HD], (((1,), (1,)), ((), ())), preferred_element_type=F32
        )
        s = s * (1.0 / math.sqrt(HD)) + bias
        w = jnp.exp(s - jnp.max(s, axis=-1, keepdims=True)).astype(BF16)
        t = jnp.sum(w.astype(F32), axis=-1, keepdims=True)
        o = jnp.dot(w, kv[:, WIDTH + k * HD : WIDTH + (k + 1) * HD], preferred_element_type=F32) / t
        out_ref[k * GROUP * rows : (k + 1) * GROUP * rows, :] = o.astype(BF16)


def attention(first, rows, owners, q, seg, parts, dec=()):
    total = seg.shape[1]
    return pl.pallas_call(
        functools.partial(attention_kernel, len(parts), first, rows),
        out_shape=jax.ShapeDtypeStruct((H * (rows + len(dec)), HD), BF16),
        in_specs=[SMEM, HBM, VMEM] + [VMEM] * (len(parts) + len(dec)),
        out_specs=VMEM,
        scratch_shapes=[
            pltpu.VMEM((total, 2 * WIDTH), BF16),
            pltpu.VMEM((rows, D), BF16),
            pltpu.SemaphoreType.DMA((len(parts) + 1,)),
        ],
        compiler_params=params(40),
        cost_estimate=STEP,
        name="prefill_attention",
    )(owners, q, seg, *parts, *dec)


def decode_kernel(n, groups, owners, slots, length, cache_in, *rest):
    parts, (out_ref, stack, cache_ref, sems) = rest[:n], rest[n:]
    positions = cache_ref.shape[1]
    moving = copies(spread(parts, owners, stack, groups * H) + [(cache_in, cache_ref)], sems)
    tok, grp = owners[0], owners[n]
    request = slots[grp * n + tok]
    at = (request % n) * groups + ((request // n) ^ grp)
    head = lax.broadcasted_iota(jnp.int32, (H, positions), 0) // GROUP
    for c in moving:
        c.wait()
    q = stack[pl.ds(pl.multiple_of(at * H, H), H), :]
    s = jnp.zeros((H, positions), F32)
    for k in range(KVH):
        one = lax.dot_general(
            q, cache_ref[0, :, k * HD : (k + 1) * HD], (((1,), (1,)), ((), ())), preferred_element_type=F32
        )
        s = jnp.where(head == k, one, s)
    spot = lax.broadcasted_iota(jnp.int32, (H, positions), 1)
    s = jnp.where(spot < length[0], s * (1.0 / math.sqrt(HD)), NEG)
    w = jnp.exp(s - jnp.max(s, axis=-1, keepdims=True)).astype(BF16).astype(F32)
    t = jnp.sum(w, axis=-1, keepdims=True)
    o = jnp.zeros((H, HD), F32)
    for k in range(KVH):
        mine = jnp.where(head == k, w, 0.0).astype(BF16)
        o = o + jnp.dot(
            mine, cache_ref[0, :, WIDTH + k * HD : WIDTH + (k + 1) * HD], preferred_element_type=F32
        )
    out_ref[...] = (o / t).astype(BF16)


def decode(n, groups, owners, slots, length, parts, cache):
    return pl.pallas_call(
        functools.partial(decode_kernel, n, groups),
        out_shape=jax.ShapeDtypeStruct((H, HD), BF16),
        in_specs=[SMEM, SMEM, SMEM, HBM] + [VMEM] * n,
        out_specs=VMEM,
        scratch_shapes=[
            pltpu.VMEM((n * groups * H, HD), BF16),
            pltpu.VMEM(cache.shape, BF16),
            pltpu.SemaphoreType.DMA((n + 1,)),
        ],
        compiler_params=params(40),
        cost_estimate=STEP,
        name="decode_attention",
    )(owners, slots, length, cache, *parts)


def project_kernel(n, rows, owners, *rest):
    parts, (wo_ref, resid_ref, out_ref, x, dec) = rest[:n], rest[n:]
    for d, part in enumerate(parts):
        at = pl.ds(pl.multiple_of(owners[d] * rows, 16), rows)
        for i in range(H):
            x[at, i * HD : (i + 1) * HD] = part[i * rows : (i + 1) * rows, :]
        if part.shape[0] > H * rows:
            dec[pl.ds(pl.multiple_of(owners[d] * H, H), H), :] = part[H * rows :, :]
    spare = x.shape[0] - n * rows
    if spare:
        at = lax.broadcasted_iota(jnp.int32, (H * spare, n * H), 0)
        of = lax.broadcasted_iota(jnp.int32, (H * spare, n * H), 1)
        pick = jnp.where(of == (at % spare) * H + at // spare, 1.0, 0.0).astype(BF16)
        heads = jnp.dot(pick, dec[...], preferred_element_type=F32).astype(BF16)
        for i in range(H):
            x[n * rows :, i * HD : (i + 1) * HD] = heads[i * spare : (i + 1) * spare]
    total = jnp.dot(x[...], wo_ref[...], preferred_element_type=F32)
    out_ref[...] = (resid_ref[...].astype(F32) + total).astype(BF16)


def project(rows, owners, parts, wo, resid):
    m, cols = resid.shape
    n = len(parts)
    return pl.pallas_call(
        functools.partial(project_kernel, n, rows),
        out_shape=jax.ShapeDtypeStruct((m, cols), BF16),
        in_specs=[SMEM] + [VMEM] * (n + 2),
        out_specs=VMEM,
        scratch_shapes=[pltpu.VMEM((m, D), BF16), pltpu.VMEM((n * H, HD), BF16)],
        compiler_params=params(16),
        cost_estimate=STEP,
        name="out_projection",
    )(owners, *parts, wo, resid)


def gate_kernel(taken, shares, owners, tenants_ref, gain_ref, w_ref, *rest):
    parts, rest = rest[: 2 * len(shares)], rest[2 * len(shares) :]
    if taken:
        held, squares, rest = rest[0], rest[1], rest[2:]
    out, squares_out, scaled, w, sems = rest
    cols = w.shape[1]
    m = out.shape[0]
    places = [pl.ds(pl.multiple_of(owners[s] * cols, cols), cols) for s in shares]
    weights = copies([(w_ref.at[at], w.at[i]) for i, at in enumerate(places)], sems)
    tenants = tenants_ref[...]
    total = squares[...] if taken else jnp.zeros((m, HD), F32)
    for i, at in enumerate(places):
        x = jnp.concatenate([p[...] for p in parts[2 * i : 2 * i + 2]], axis=0).astype(F32)
        for j in range(0, cols, HD):
            total = total + x[:, j : j + HD] * x[:, j : j + HD]
        gain = jnp.broadcast_to(gain_ref[0:1, at], (m, cols))
        for t in range(1, gain_ref.shape[0]):
            gain = jnp.where(tenants == t, gain_ref[t : t + 1, at], gain)
        scaled[:, i * cols : (i + 1) * cols] = (x * gain).astype(BF16)
    squares_out[...] = total
    accumulate(out, held if taken else None, scaled, w, weights)


def up_kernel(taken, shares, owners, w_ref, scaled, *rest):
    if taken:
        held, rest = rest[0], rest[1:]
    out, w, sems = rest
    cols = w.shape[1]
    places = [pl.ds(pl.multiple_of(owners[s] * cols, cols), cols) for s in shares]
    weights = copies([(w_ref.at[at], w.at[i]) for i, at in enumerate(places)], sems)
    accumulate(out, held if taken else None, scaled, w, weights)


def accumulate(out, held, scaled, w, weights):
    cols = w.shape[1]
    for i, copy in enumerate(weights):
        copy.wait()
        one = jnp.dot(scaled[:, i * cols : (i + 1) * cols], w[i], preferred_element_type=F32)
        if i == 0:
            out[...] = one if held is None else held[...] + one
        else:
            out[...] += one


def gate_step(shares, owners, tenants, gain, w_gate, parts, held):
    m, wide = tenants.shape[0], w_gate.shape[1]
    cols = parts[0].shape[1]
    first = 4 + len(parts)
    return pl.pallas_call(
        functools.partial(gate_kernel, len(held) > 0, shares),
        out_shape=[
            jax.ShapeDtypeStruct((m, wide), F32),
            jax.ShapeDtypeStruct((m, HD), F32),
            jax.ShapeDtypeStruct((m, cols * len(shares)), BF16),
        ],
        in_specs=[SMEM, VMEM, VMEM, HBM] + [VMEM] * (len(parts) + len(held)),
        out_specs=[VMEM] * 3,
        scratch_shapes=[
            pltpu.VMEM((len(shares), cols, wide), BF16),
            pltpu.SemaphoreType.DMA((len(shares),)),
        ],
        input_output_aliases={first: 0, first + 1: 1} if held else {},
        compiler_params=params(46),
        cost_estimate=STEP,
        name="gate_sum",
    )(owners, tenants, gain, w_gate, *parts, *held)


def up_step(shares, owners, w_up, scaled, held):
    m, wide = scaled.shape[0], w_up.shape[1]
    cols = scaled.shape[1] // len(shares)
    return pl.pallas_call(
        functools.partial(up_kernel, len(held) > 0, shares),
        out_shape=jax.ShapeDtypeStruct((m, wide), F32),
        in_specs=[SMEM, HBM, VMEM] + [VMEM] * len(held),
        out_specs=VMEM,
        scratch_shapes=[
            pltpu.VMEM((len(shares), cols, wide), BF16),
            pltpu.SemaphoreType.DMA((len(shares),)),
        ],
        input_output_aliases={3: 0} if held else {},
        compiler_params=params(46),
        cost_estimate=STEP,
        name="up_sum",
    )(owners, w_up, scaled, *held)


def hidden_kernel(lo, hi, share, owners, tenants_ref, gain_ref, gate_ref, up_ref, part, gates, lifts, squares, out, w, sems):
    cols = w.shape[1]
    m = hi - lo
    at = pl.ds(pl.multiple_of(owners[share] * cols, cols), cols)
    weights = copies([(gate_ref.at[at], w.at[0]), (up_ref.at[at], w.at[1])], sems)
    tenants = tenants_ref[lo:hi, :]
    x = part[...].astype(F32)
    total = squares[lo:hi, :]
    for j in range(0, cols, HD):
        total = total + x[:, j : j + HD] * x[:, j : j + HD]
    gain = jnp.broadcast_to(gain_ref[0:1, at], (m, cols))
    for t in range(1, gain_ref.shape[0]):
        gain = jnp.where(tenants == t, gain_ref[t : t + 1, at], gain)
    scaled = (x * gain).astype(BF16)
    scale = lax.rsqrt(jnp.sum(total, axis=-1, keepdims=True) / D + EPS)
    weights[0].wait()
    gate = (gates[lo:hi, :] + jnp.dot(scaled, w[0], preferred_element_type=F32)) * scale
    gate = gate / (1.0 + jnp.exp(-gate))
    weights[1].wait()
    lift = (lifts[lo:hi, :] + jnp.dot(scaled, w[1], preferred_element_type=F32)) * scale
    out[...] = (gate * lift).astype(BF16)


def hidden_step(lo, hi, share, owners, tenants, gain, w_gate, w_up, part, held):
    wide = w_gate.shape[1]
    return pl.pallas_call(
        functools.partial(hidden_kernel, lo, hi, share),
        out_shape=jax.ShapeDtypeStruct((hi - lo, wide), BF16),
        in_specs=[SMEM, VMEM, VMEM, HBM, HBM] + [VMEM] * 4,
        out_specs=VMEM,
        scratch_shapes=[
            pltpu.VMEM((2, part.shape[1], wide), BF16),
            pltpu.SemaphoreType.DMA((2,)),
        ],
        compiler_params=params(46),
        cost_estimate=STEP,
        name="hidden",
    )(owners, tenants, gain, w_gate, w_up, part, *held)


def pause_kernel(ids, out):
    for i in range(ids.shape[0]):
        out[i] = ids[i]


def pause(ids):
    return pl.pallas_call(
        pause_kernel,
        out_shape=jax.ShapeDtypeStruct(ids.shape, ids.dtype),
        in_specs=[SMEM],
        out_specs=SMEM,
        cost_estimate=STEP,
        name="step",
    )(ids)


def down_kernel(blocks, flags, own, owners, hidden, w_ref, *rest):
    terms, rest = rest[: sum(flags) + own], rest[sum(flags) + own :]
    outs, (w, sems) = rest[: len(blocks)], rest[len(blocks) :]
    cols = w.shape[-1]
    weights = copies(
        [
            (w_ref.at[:, pl.ds(pl.multiple_of(owners[b] * cols, HD), cols)], w.at[i])
            for i, b in enumerate(blocks)
        ],
        sems,
    )
    taken = 0
    for i in range(len(blocks)):
        weights[i].wait()
        total = jnp.dot(hidden[...], w[i], preferred_element_type=F32)
        for term in terms[taken : taken + flags[i] + own]:
            total = total + term[...].astype(F32)
        taken += flags[i]
        outs[i][...] = total.astype(BF16)


def down(blocks, flags, owners, hidden, w_down, arrived, cols, own=()):
    m, deep = hidden.shape
    count = len(blocks)
    return pl.pallas_call(
        functools.partial(down_kernel, blocks, flags, len(own)),
        out_shape=[jax.ShapeDtypeStruct((m, cols), BF16) for _ in blocks],
        in_specs=[SMEM, VMEM, HBM] + [VMEM] * (len(arrived) + len(own)),
        out_specs=[VMEM] * count,
        scratch_shapes=[pltpu.VMEM((count, deep, cols), BF16), pltpu.SemaphoreType.DMA((count,))],
        compiler_params=params(50),
        cost_estimate=STEP,
        name="down_sum",
    )(owners, hidden, w_down, *arrived, *own)


class Chain:
    def __init__(self, n, order, own, last):
        self.n, self.half, self.last = n, n // 2, last
        self.fw = [(order[i], order[(i + 1) % n]) for i in range(n)]
        self.bw = [(b, a) for a, b in self.fw]
        self.own, self.ahead, self.behind, self.hops = own, [own], [own], 0

    def done(self):
        return self.hops == self.half

    def parts(self):
        return [self.own] + self.ahead[1:] + self.behind[:0:-1]


class Order:
    def __init__(self, ids):
        self.ids, self.last = ids, ()

    def after(self):
        return lax.optimization_barrier((self.ids, *self.last))[0]

    def mark(self, *out):
        self.last = out
        return out[0]

    def tied(self, *arrays):
        out = lax.optimization_barrier((*arrays, *self.last))[: len(arrays)]
        self.last = (out[0],)
        return out

    def hop(self, chain):
        chain.hops += 1
        f, b = chain.ahead[-1], chain.behind[-1]
        if chain.done() and chain.last == "split":
            cut = f.shape[0] // 2
            f, b = f[:cut], b[cut:]
        if chain.done() and chain.last == "fw":
            (f,) = self.tied(f)
            chain.ahead.append(lax.ppermute(f, "tok", chain.fw))
        elif chain.done() and chain.last == "bw":
            (b,) = self.tied(b)
            chain.behind.append(lax.ppermute(b, "tok", chain.bw))
        else:
            f, b = self.tied(f, b)
            chain.ahead.append(lax.ppermute(f, "tok", chain.fw))
            chain.behind.append(lax.ppermute(b, "tok", chain.bw))


class Sum:
    def __init__(self, run, chain, hidden, w_down, cols, own):
        self.run, self.chain, self.hidden, self.w_down = run, chain, hidden, w_down
        self.cols, self.own, self.step, self.arrived = cols, own, 0, ()

    def call(self, blocks, flags, own=()):
        blocks = [-b % self.chain.n for b in blocks]
        out = down(blocks, flags, self.run.after(), self.hidden, self.w_down, self.arrived, self.cols, own)
        self.run.mark(out[0])
        return out

    def hop(self):
        chain = self.chain
        d, forward = chain.half - self.step, chain.last == "fw"
        if self.step == 0:
            out = self.run.tied(*self.call([d], [0]))
            self.arrived = (lax.ppermute(out[0], "tok", chain.fw if forward else chain.bw),)
        else:
            flags = [1, 1] if self.step > 1 else ([1, 0] if forward else [0, 1])
            out = self.run.tied(*self.call([d, -d], flags))
            self.arrived = (lax.ppermute(out[0], "tok", chain.fw), lax.ppermute(out[1], "tok", chain.bw))
        self.step += 1

    def finish(self):
        return self.call([0], [2], (self.own,))[0]


def shards(
    pre_q,
    pre_kv,
    pre_segment,
    dec_q,
    cache,
    cache_len,
    slot_request,
    resid,
    wo,
    tenant,
    norm_gain,
    w_gate,
    w_up,
    w_down,
):
    n, groups = lax.axis_size("tok"), lax.axis_size("grp")
    tok, grp = lax.axis_index("tok"), lax.axis_index("grp")
    local = pre_q.shape[0]
    rows = local // 2
    cols = wo.shape[1]
    half = n // 2
    spare = -(-n // 16) * 16
    order = ring_order(n)
    ids = jnp.arange(n, dtype=jnp.int32)
    place = sum(jnp.where(tok == t, i, 0) for i, t in enumerate(order)).astype(jnp.int32)
    spots = (place - ids) % n
    owners = sum(jnp.where(spots == i, t, 0) for i, t in enumerate(order)).astype(jnp.int32)
    owners = jnp.concatenate([owners, jnp.reshape(grp, (1,)).astype(jnp.int32)])

    def split(a):
        a = a.reshape(n, local + 1, -1)
        first = a[:, :rows].reshape(n * rows, -1)
        second = a[:, rows:local].reshape(n * rows, -1)
        tail = jnp.pad(a[:, local], ((0, spare - n), (0, 0)))
        return first, jnp.concatenate([second, tail], axis=0)

    resids = split(resid)
    tenants = jnp.concatenate(split(tenant[0][:, None]), axis=0)
    run = Order(owners)

    def chain(own, last):
        return Chain(n, order, own, last)

    keys = chain(pre_kv, "split")
    run.hop(keys)
    queries = dec_q.reshape(H, HD)
    for i in range(groups.bit_length() - 1):
        pairs = [(j, j ^ (1 << i)) for j in range(groups)]
        (queries,) = run.tied(queries)
        queries = jnp.concatenate([queries, lax.ppermute(queries, "grp", pairs)], axis=0)
    run.mark(*run.last, *resids, tenants, owners)
    asks = chain(queries, "fw")
    while not keys.done():
        run.hop(keys)
        run.hop(asks)
    run.hop(asks)

    kv = keys.parts()
    a = chain(run.mark(attention(0, rows, run.after(), pre_q, pre_segment, kv)), "fw")
    run.hop(a)
    dec = run.mark(decode(n, groups, run.after(), slot_request, cache_len, asks.parts(), cache))
    b = chain(run.mark(attention(rows, rows, run.after(), pre_q, pre_segment, kv, (dec,))), "bw")
    run.hop(b)
    while not a.done():
        run.mark(pause(run.after()))
        run.hop(a)
        run.mark(pause(run.after()))
        run.hop(b)

    mixed_a = run.mark(project(rows, run.after(), a.parts(), wo, resids[0]))
    g = chain(mixed_a, "fw")
    run.hop(g)
    mixed_b = run.mark(project(rows, run.after(), b.parts(), wo, resids[1]))
    h = chain(mixed_b, "bw")
    run.hop(h)

    m_a, m = mixed_a.shape[0], tenants.shape[0]
    gates, lifts = (), ()
    for i in range(half):
        if i:
            shares, parts = [i, n - i], [g.ahead[i], h.ahead[i], g.behind[i], h.behind[i]]
        else:
            shares, parts = [0], [mixed_a, mixed_b]
        out = gate_step(shares, run.after(), tenants, norm_gain, w_gate, parts, gates)
        gates, scaled = out[:2], out[2]
        run.mark(scaled)
        if i + 1 < half:
            run.hop(g)
        lifts = (run.mark(up_step(shares, run.after(), w_up, scaled, lifts)),)
        if i + 1 < half:
            run.hop(h)

    def hide(lo, hi, part):
        held = (gates[0], lifts[0], gates[1])
        return run.mark(
            hidden_step(lo, hi, half, run.after(), tenants, norm_gain, w_gate, w_up, part, held)
        )

    hid_a = hide(0, m_a, g.ahead[half])
    sum_a = Sum(run, g, hid_a, w_down, cols, mixed_a)
    sum_a.hop()
    hid_b = hide(m_a, m, h.behind[half])
    sum_b = Sum(run, h, hid_b, w_down, cols, mixed_b)
    sum_b.hop()
    for _ in range(1, half):
        sum_a.hop()
        sum_b.hop()
    out_a = sum_a.finish()
    out_b = sum_b.finish()

    top = out_a.reshape(n, rows, cols)
    low = out_b[: n * rows].reshape(n, rows, cols)
    tail = out_b[n * rows : n * rows + n].reshape(n, 1, cols)
    return jnp.concatenate([top, low, tail], axis=1).reshape(n * (local + 1), cols)


def solution(mesh):
    in_specs = (
        P(("grp", "tok"), None),
        P(("grp", "tok"), None),
        P("grp", None),
        P(("grp", "tok"), None),
        P(("grp", "tok"), None, None),
        P(("grp", "tok")),
        P(),
        P("grp", "tok"),
        P(None, "tok"),
        P("grp", None),
        P(),
        P(None, "tok"),
        P(None, "tok"),
        P("tok", None),
    )
    out_specs = P("grp", "tok")
    return jax.shard_map(shards, mesh=mesh, in_specs=in_specs, out_specs=out_specs, check_vma=False)
```

time: 405 us -> 216 us (0.53); the launches traced: 405 us -> 212 us
  waiting for transfers between devices: 240 us -> 46.8 us
  Pallas kernels: 0 us -> 83.1 us
  blocking collectives: 74.2 us -> 0 us
  starting transfers between devices: 0.13 us -> 71.4 us
  matrix products: 49 us -> 0 us
  between operations: 15.8 us -> 1.37 us
  local copies, waits for them, and re-layouts: 18 us -> 6.36 us
  other arithmetic: 7.53 us -> 2.59 us
    all_gather x3 -> x0, waiting for transfers between devices: 151 us -> none  [the longest x1 76.7 us: shards(): lax.all_gather(attended, 'tok', axis=0, tiled=True)]
    reduce_scatter x1 -> x0, waiting for transfers between devices: 88.6 us -> none  [shards(): lax.psum_scatter(terms.astype(jnp.bfloat16), 'tok', scatter_dimension=1,...]
    pallas_call x0 -> x25, Pallas kernels: none -> 83.1 us  [the longest x10 29.2 us: down(): pl.pallas_call(functools.partial(down_kernel, blocks, flags, len(own)), o...]
    all_gather x1 -> x0, blocking collectives: 74.2 us -> none  [shards(): all_queries = lax.all_gather(dec_q, ('grp', 'tok'), axis=0, tiled=True)]
    ppermute x0 -> x59, starting transfers between devices: none -> 71.4 us  [the longest x21 31.1 us: hop(): chain.behind.append(lax.ppermute(b, 'tok', chain.bw))]
    dot_general x7 -> x0, matrix products: 48.6 us -> none  [the longest x1 24.8 us: shards(): terms = jnp.dot(hidden, w_down, preferred_element_type=jnp.float32)]
    ppermute x0 -> x59, waiting for transfers between devices: none -> 46.8 us  [the longest x22 22.7 us: hop(): chain.ahead.append(lax.ppermute(f, 'tok', chain.fw))]
    unnamed x22 -> x17, local copies, waits for them, and re-layouts: 11.9 us -> 0.12 us
  transfers between devices with their start and end apart: 4 -> 59, of which waited for: 3 -> 28; matrix products, arithmetic and copies ran while one was open for 2% -> 4% of each run, Pallas kernels for 0% -> 38%
where the time goes in v2:
time: 216 us; the launch traced here: 212 us
  Pallas kernels  83.1 us (38%)
  starting transfers between devices  71.4 us (33%)
  waiting for transfers between devices  46.8 us (22%)
  local copies, waits for them, and re-layouts  6.36 us (3%)
  other arithmetic  2.59 us (1%)
    ppermute x21, starting transfers between devices, hop(): chain.behind.append(lax.ppermute(b, 'tok', chain.bw))  31.1 us
    pallas_call x10, Pallas kernels, down(): pl.pallas_call(functools.partial(down_kernel, blocks, flags, len(own)), o...  29.2 us
    ppermute x22, starting transfers between devices, hop(): chain.ahead.append(lax.ppermute(f, 'tok', chain.fw))  24.1 us
    ppermute x22, waiting for transfers between devices, hop(): chain.ahead.append(lax.ppermute(f, 'tok', chain.fw))  22.7 us
    pallas_call x4, Pallas kernels, gate_step(): pl.pallas_call(functools.partial(gate_kernel, len(held) > 0, shares), out...  16.5 us
    pallas_call x4, Pallas kernels, up_step(): pl.pallas_call(functools.partial(up_kernel, len(held) > 0, shares), out_s...  16 us
    ppermute x21, waiting for transfers between devices, hop(): chain.behind.append(lax.ppermute(b, 'tok', chain.bw))  13.7 us
    pallas_call x2, Pallas kernels, attention(): pl.pallas_call(functools.partial(attention_kernel, len(parts), first, row...  7.99 us
  transfers between devices with their start and end apart: 59, of which 28 were waited for; matrix products, arithmetic and copies ran while one was open for 4% of the time, Pallas kernels for 38%

profile of v2, /device:TPU:0, one launch (start us, length us, event | category | flops | bytes accessed | tf_op | source)
XLA Modules:
  0.0 211.6 jit_solution(3599536924820042222)
XLA Ops:
  0.0 3.1 %collective-permute-start.2 = (bf16[64,2048]{1,0:T(8,128)(2,1)}, bf16[64,2048]{1,0:T(8,128)(2,1)}, u32[]{:S(2)}, u32[]{:S(2)}) collective-permute-start(bf16[64,2048]{1,0:T(8,128)(2,1)} %rest_0_.3), channel_id=1, source_target_pairs={{0,2},{2,4},{4,6},{6,7},{7,5},{5,3},{3,1},{1,0},{8,10},{10,12},{12... | collective-permute-start | bytes 786440 | tf_op jit(solution)/shard_map/ppermute | solution.py:417
  26.4 3.3 %collective-permute-done.4.rest_1_ = bf16[128,128]{1,0:T(8,128)(2,1)S(1)} collective-permute-done((bf16[128,128]{1,0:T(8,128)(2,1)S(1)}, bf16[128,128]{1,0:T(8,128)(2,1)S(1)}, u32[]{:S(2)}, u32[]{:S(2)}) %collective-permute-start.4) | collective-permute-done | bytes 32800 | tf_op jit(solution)/shard_map/ppermute | solution.py:417
  43.2 4.0 %prefill_attention.2.rest_0_ = bf16[1024,128]{1,0:T(8,128)(2,1)S(1)} custom-call(s32[9]{0:T(128)S(1)} %pad_add_fusion.1.owners, bf16[64,4096]{1,0:T(8,128)(2,1)S(1)} %copy-done.3, s32[1,512]{1,0:T(1,128)S(1)} %copy-done.5, bf16[64,2048]{1,0:T(8,128)(2,1)S(1)} %copy-done.4, bf16[64,2048]{1,0:T(8,128)(2,1)} %collective-permute-done.2.rest_1_, ...), custom_call_target="tpu_custom_call" | custom-call | flops 500000000 | bytes 1000000 | tf_op jit(solution)/shard_map/prefill_attention/pallas_call | solution.py:96
  51.4 4.0 %prefill_attention.3.rest_0_ = bf16[1056,128]{1,0:T(8,128)(2,1)S(1)} custom-call(s32[9]{0:T(128)S(1)} %pad_add_fusion.1.owners, bf16[64,4096]{1,0:T(8,128)(2,1)S(1)} %copy-done.3, s32[1,512]{1,0:T(1,128)S(1)} %copy-done.5, bf16[64,2048]{1,0:T(8,128)(2,1)S(1)} %copy-done.4, bf16[64,2048]{1,0:T(8,128)(2,1)} %collective-permute-done.2.rest_1_, ...), custom_call_target="tpu_custom_call" | custom-call | flops 500000000 | bytes 1000000 | tf_op jit(solution)/shard_map/prefill_attention/pallas_call | solution.py:96
  59.5 5.3 %collective-permute-done.17.rest_1_ = bf16[1056,128]{1,0:T(8,128)(2,1)S(1)} collective-permute-done((bf16[1056,128]{1,0:T(8,128)(2,1)S(1)}, bf16[1056,128]{1,0:T(8,128)(2,1)S(1)}, u32[]{:S(2)}, u32[]{:S(2)}) %collective-permute-start.17) | collective-permute-done | bytes 270368 | tf_op jit(solution)/shard_map/ppermute | solution.py:417
  67.6 2.8 %collective-permute-done.24.rest_2_ = bf16[1024,128]{1,0:T(8,128)(2,1)S(1)} collective-permute-done((bf16[1024,128]{1,0:T(8,128)(2,1)S(1)}, bf16[1024,128]{1,0:T(8,128)(2,1)S(1)}, u32[]{:S(2)}, u32[]{:S(2)}) %collective-permute-start.24) | collective-permute-done | bytes 262176 | tf_op jit(solution)/shard_map/ppermute | solution.py:417
  98.1 3.0 %gate_sum.4 = (f32[528,1536]{1,0:T(8,128)S(1)}, f32[528,128]{1,0:T(8,128)S(1)}, bf16[528,512]{1,0:T(8,128)(2,1)S(1)}) custom-call(s32[9]{0:T(128)S(1)} %pad_add_fusion.1.owners, s32[528,1]{1,0:T(8,128)S(1)} %copy.35.tenants_ref, f32[4,4096]{1,0:T(4,128)S(1)} %copy-done.1, bf16[4096,1536]{1,0:T(8,128)(2,1)} %gate_ref.3, ...), custom_call_target="tpu_custom_call" | custom-call | flops 500000000 | bytes 1000000 | tf_op jit(solution)/shard_map/gate_sum/pallas_call | solution.py:242
  103.4 3.0 %up_sum.4.rest_0_ = f32[528,1536]{1,0:T(8,128)S(1)} custom-call(s32[9]{0:T(128)S(1)} %pad_add_fusion.1.owners, bf16[4096,1536]{1,0:T(8,128)(2,1)} %up_ref.3, bf16[528,512]{1,0:T(8,128)(2,1)S(1)} %get-tuple-element.136.scaled), custom_call_target="tpu_custom_call" | custom-call | flops 500000000 | bytes 1000000 | tf_op jit(solution)/shard_map/up_sum/pallas_call | solution.py:265
  108.5 4.5 %gate_sum.5 = (f32[528,1536]{1,0:T(8,128)S(1)}, f32[528,128]{1,0:T(8,128)S(1)}, bf16[528,1024]{1,0:T(8,128)(2,1)S(1)}) custom-call(s32[9]{0:T(128)S(1)} %pad_add_fusion.1.owners, s32[528,1]{1,0:T(8,128)S(1)} %copy.35.tenants_ref, f32[4,4096]{1,0:T(4,128)S(1)} %copy-done.1, ...), custom_call_target="tpu_custom_call", output_to_operand_aliasing={{0}: (8, {}), {1}: (9, {})} | custom-call | flops 500000000 | bytes 1000000 | tf_op jit(solution)/shard_map/gate_sum/pallas_call | solution.py:242
  113.9 4.3 %up_sum.5.rest_0_ = f32[528,1536]{1,0:T(8,128)S(1)} custom-call(s32[9]{0:T(128)S(1)} %pad_add_fusion.1.owners, bf16[4096,1536]{1,0:T(8,128)(2,1)} %up_ref.3, bf16[528,1024]{1,0:T(8,128)(2,1)S(1)} %get-tuple-element.145.scaled, f32[528,1536]{1,0:T(8,128)S(1)} %up_sum.4.rest_0_), custom_call_target="tpu_custom_call", output_to_operand_aliasing={{}: (3, {})} | custom-call | flops 500000000 | bytes 1000000 | tf_op jit(solution)/shard_map/up_sum/pallas_call | solution.py:265
  121.6 4.5 %gate_sum.6 = (f32[528,1536]{1,0:T(8,128)S(1)}, f32[528,128]{1,0:T(8,128)S(1)}, bf16[528,1024]{1,0:T(8,128)(2,1)S(1)}) custom-call(s32[9]{0:T(128)S(1)} %pad_add_fusion.1.owners, s32[528,1]{1,0:T(8,128)S(1)} %copy.35.tenants_ref, f32[4,4096]{1,0:T(4,128)S(1)} %copy-done.1, ...), custom_call_target="tpu_custom_call", output_to_operand_aliasing={{0}: (8, {}), {1}: (9, {})} | custom-call | flops 500000000 | bytes 1000000 | tf_op jit(solution)/shard_map/gate_sum/pallas_call | solution.py:242
  127.0 4.3 %up_sum.6.rest_0_ = f32[528,1536]{1,0:T(8,128)S(1)} custom-call(s32[9]{0:T(128)S(1)} %pad_add_fusion.1.owners, bf16[4096,1536]{1,0:T(8,128)(2,1)} %up_ref.3, bf16[528,1024]{1,0:T(8,128)(2,1)S(1)} %get-tuple-element.153.scaled, f32[528,1536]{1,0:T(8,128)S(1)} %up_sum.5.rest_0_), custom_call_target="tpu_custom_call", output_to_operand_aliasing={{}: (3, {})} | custom-call | flops 500000000 | bytes 1000000 | tf_op jit(solution)/shard_map/up_sum/pallas_call | solution.py:265
  131.3 11.2 %collective-permute-start.44 = (bf16[272,512]{1,0:T(8,128)(2,1)S(1)}, bf16[272,512]{1,0:T(8,128)(2,1)S(1)}, u32[]{:S(2)}, u32[]{:S(2)}) collective-permute-start(bf16[272,512]{1,0:T(8,128)(2,1)S(1)} %collective-permute-done.39.rest_3_), channel_id=1, source_target_pairs={{2,0},{4,2},{6,4},{7,6},{5,7},{3,5},{1,3},{0,1},{10,8},{12,10},{14... | collective-permute-start | bytes 835592 | tf_op jit(solution)/shard_map/ppermute | solution.py:414
  142.6 4.5 %gate_sum.7 = (f32[528,1536]{1,0:T(8,128)S(1)}, f32[528,128]{1,0:T(8,128)S(1)}, bf16[528,1024]{1,0:T(8,128)(2,1)S(1)}) custom-call(s32[9]{0:T(128)S(1)} %pad_add_fusion.1.owners, s32[528,1]{1,0:T(8,128)S(1)} %copy.35.tenants_ref, f32[4,4096]{1,0:T(4,128)S(1)} %copy-done.1, ...), custom_call_target="tpu_custom_call", output_to_operand_aliasing={{0}: (8, {}), {1}: (9, {})} | custom-call | flops 500000000 | bytes 1000000 | tf_op jit(solution)/shard_map/gate_sum/pallas_call | solution.py:242
  147.1 4.3 %up_sum.7.lifts = f32[528,1536]{1,0:T(8,128)S(1)} custom-call(s32[9]{0:T(128)S(1)} %pad_add_fusion.1.owners, bf16[4096,1536]{1,0:T(8,128)(2,1)} %up_ref.3, bf16[528,1024]{1,0:T(8,128)(2,1)S(1)} %get-tuple-element.161.scaled, f32[528,1536]{1,0:T(8,128)S(1)} %up_sum.6.rest_0_), custom_call_target="tpu_custom_call", output_to_operand_aliasing={{}: (3, {})} | custom-call | flops 500000000 | bytes 1000000 | tf_op jit(solution)/shard_map/up_sum/pallas_call | solution.py:265
  151.4 3.4 %hidden.2 = bf16[256,1536]{1,0:T(8,128)(2,1)S(1)} custom-call(s32[9]{0:T(128)S(1)} %pad_add_fusion.1.owners, s32[528,1]{1,0:T(8,128)S(1)} %copy.35.tenants_ref, f32[4,4096]{1,0:T(4,128)S(1)} %copy-done.1, bf16[4096,1536]{1,0:T(8,128)(2,1)} %gate_ref.3, bf16[4096,1536]{1,0:T(8,128)(2,1)} %up_ref.3, bf16[256,512]{1,0:T(8,128)(2,1)S(1)} %collective-permute-done.43.part, ...), custom_call_target="tpu_custom_call" | custom-call | flops 500000000 | bytes 1000000 | tf_op jit(solution)/shard_map/hidden/pallas_call | solution.py:306
  158.3 3.5 %hidden.3 = bf16[272,1536]{1,0:T(8,128)(2,1)S(1)} custom-call(s32[9]{0:T(128)S(1)} %pad_add_fusion.1.owners, s32[528,1]{1,0:T(8,128)S(1)} %copy.35.tenants_ref, f32[4,4096]{1,0:T(4,128)S(1)} %copy-done.1, bf16[4096,1536]{1,0:T(8,128)(2,1)} %gate_ref.3, bf16[4096,1536]{1,0:T(8,128)(2,1)} %up_ref.3, bf16[272,512]{1,0:T(8,128)(2,1)S(1)} %collective-permute-done.44.part, ...), custom_call_target="tpu_custom_call" | custom-call | flops 500000000 | bytes 1000000 | tf_op jit(solution)/shard_map/hidden/pallas_call | solution.py:306
  165.6 3.1 %down_sum.12 = (bf16[256,512]{1,0:T(8,128)(2,1)S(1)}, bf16[256,512]{1,0:T(8,128)(2,1)S(1)}) custom-call(s32[9]{0:T(128)S(1)} %pad_add_fusion.1.owners, bf16[256,1536]{1,0:T(8,128)(2,1)S(1)} %hidden.2, bf16[1536,4096]{1,0:T(8,128)(2,1)} %w_ref.35, bf16[256,512]{1,0:T(8,128)(2,1)S(1)} %collective-permute-done.45.rest_0_), custom_call_target="tpu_custom_call" | custom-call | flops 500000000 | bytes 1000000 | tf_op jit(solution)/shard_map/down_sum/pallas_call | solution.py:361
  170.8 2.9 %collective-permute-done.46.rest_0_ = bf16[272,512]{1,0:T(8,128)(2,1)S(1)} collective-permute-done((bf16[272,512]{1,0:T(8,128)(2,1)S(1)}, bf16[272,512]{1,0:T(8,128)(2,1)S(1)}, u32[]{:S(2)}, u32[]{:S(2)}) %collective-permute-start.46) | collective-permute-done | bytes 278560 | tf_op jit(solution)/shard_map/ppermute | solution.py:437
  173.7 3.2 %down_sum.13 = (bf16[272,512]{1,0:T(8,128)(2,1)S(1)}, bf16[272,512]{1,0:T(8,128)(2,1)S(1)}) custom-call(s32[9]{0:T(128)S(1)} %pad_add_fusion.1.owners, bf16[272,1536]{1,0:T(8,128)(2,1)S(1)} %hidden.3, bf16[1536,4096]{1,0:T(8,128)(2,1)} %w_ref.35, bf16[272,512]{1,0:T(8,128)(2,1)S(1)} %collective-permute-done.46.rest_0_), custom_call_target="tpu_custom_call" | custom-call | flops 500000000 | bytes 1000000 | tf_op jit(solution)/shard_map/down_sum/pallas_call | solution.py:361
  179.3 3.1 %down_sum.14 = (bf16[256,512]{1,0:T(8,128)(2,1)S(1)}, bf16[256,512]{1,0:T(8,128)(2,1)S(1)}) custom-call(s32[9]{0:T(128)S(1)} %pad_add_fusion.1.owners, bf16[256,1536]{1,0:T(8,128)(2,1)S(1)} %hidden.2, bf16[1536,4096]{1,0:T(8,128)(2,1)} %w_ref.35, bf16[256,512]{1,0:T(8,128)(2,1)S(1)} %collective-permute-done.47.rest_0_, ...), custom_call_target="tpu_custom_call" | custom-call | flops 500000000 | bytes 1000000 | tf_op jit(solution)/shard_map/down_sum/pallas_call | solution.py:361
  185.6 3.2 %down_sum.15 = (bf16[272,512]{1,0:T(8,128)(2,1)S(1)}, bf16[272,512]{1,0:T(8,128)(2,1)S(1)}) custom-call(s32[9]{0:T(128)S(1)} %pad_add_fusion.1.owners, bf16[272,1536]{1,0:T(8,128)(2,1)S(1)} %hidden.3, bf16[1536,4096]{1,0:T(8,128)(2,1)} %w_ref.35, bf16[272,512]{1,0:T(8,128)(2,1)S(1)} %collective-permute-done.49.rest_0_, ...), custom_call_target="tpu_custom_call" | custom-call | flops 500000000 | bytes 1000000 | tf_op jit(solution)/shard_map/down_sum/pallas_call | solution.py:361
  191.7 3.1 %down_sum.16 = (bf16[256,512]{1,0:T(8,128)(2,1)S(1)}, bf16[256,512]{1,0:T(8,128)(2,1)S(1)}) custom-call(s32[9]{0:T(128)S(1)} %pad_add_fusion.1.owners, bf16[256,1536]{1,0:T(8,128)(2,1)S(1)} %hidden.2, bf16[1536,4096]{1,0:T(8,128)(2,1)} %w_ref.35, bf16[256,512]{1,0:T(8,128)(2,1)S(1)} %collective-permute-done.51.rest_0_, ...), custom_call_target="tpu_custom_call" | custom-call | flops 500000000 | bytes 1000000 | tf_op jit(solution)/shard_map/down_sum/pallas_call | solution.py:361
  196.9 3.2 %down_sum.17 = (bf16[272,512]{1,0:T(8,128)(2,1)S(1)}, bf16[272,512]{1,0:T(8,128)(2,1)S(1)}) custom-call(s32[9]{0:T(128)S(1)} %pad_add_fusion.1.owners, bf16[272,1536]{1,0:T(8,128)(2,1)S(1)} %hidden.3, bf16[1536,4096]{1,0:T(8,128)(2,1)} %w_ref.35, bf16[272,512]{1,0:T(8,128)(2,1)S(1)} %collective-permute-done.53.rest_0_, ...), custom_call_target="tpu_custom_call" | custom-call | flops 500000000 | bytes 1000000 | tf_op jit(solution)/shard_map/down_sum/pallas_call | solution.py:361
  (160 shorter events, 115.3 us)
Async XLA Ops:
  0.0 11.1 %collective-permute-start.2 = (bf16[64,2048]{1,0:T(8,128)(2,1)}, bf16[64,2048]{1,0:T(8,128)(2,1)}, u32[]{:S(2)}, u32[]{:S(2)}) collective-permute-start(bf16[64,2048]{1,0:T(8,128)(2,1)} %rest_0_.3), channel_id=1, source_target_pairs={{0,2},{2,4},{4,6},{6,7},{7,5},{5,3},{3,1},{1,0},{8,10},{10,12},{12... | collective-permute-start | bytes 786440 | tf_op jit(solution)/shard_map/ppermute | solution.py:417
  31.1 12.1 %collective-permute-start.13 = (bf16[32,2048]{1,0:T(8,128)(2,1)S(1)}, bf16[32,2048]{1,0:T(8,128)(2,1)S(1)}, u32[]{:S(2)}, u32[]{:S(2)}) collective-permute-start(bf16[32,2048]{1,0:T(8,128)(2,1)S(1)} %slice.43), channel_id=1, source_target_pairs={{0,2},{2,4},{4,6},{6,7},{7,5},{5,3},{3,1},{1,0},{8,10},{10,12},{12... | collective-permute-start | bytes 393224 | tf_op jit(solution)/shard_map/ppermute | solution.py:417
  32.6 10.6 %collective-permute-start.14 = (bf16[32,2048]{1,0:T(8,128)(2,1)S(1)}, bf16[32,2048]{1,0:T(8,128)(2,1)S(1)}, u32[]{:S(2)}, u32[]{:S(2)}) collective-permute-start(bf16[32,2048]{1,0:T(8,128)(2,1)S(1)} %slice.44), channel_id=1, source_target_pairs={{2,0},{4,2},{6,4},{7,6},{5,7},{3,5},{1,3},{0,1},{10,8},{12,10},{14... | collective-permute-start | bytes 393224 | tf_op jit(solution)/shard_map/ppermute | solution.py:418
  47.2 10.2 %collective-permute-start.22 = (bf16[1024,128]{1,0:T(8,128)(2,1)S(1)}, bf16[1024,128]{1,0:T(8,128)(2,1)S(1)}, u32[]{:S(2)}, u32[]{:S(2)}) collective-permute-start(bf16[1024,128]{1,0:T(8,128)(2,1)S(1)} %prefill_attention.2.rest_0_), channel_id=1, source_target_pairs={{0,2},{2,4},{4,6},{6,7},{7,5},{5,3},{3,1},{1,0},{8,10},{10,12},{12... | collective-permute-start | bytes 786440 | tf_op jit(solution)/shard_map/ppermute | solution.py:417
  57.4 13.0 %collective-permute-start.24 = (bf16[1024,128]{1,0:T(8,128)(2,1)S(1)}, bf16[1024,128]{1,0:T(8,128)(2,1)S(1)}, u32[]{:S(2)}, u32[]{:S(2)}) collective-permute-start(bf16[1024,128]{1,0:T(8,128)(2,1)S(1)} %collective-permute-done.22.rest_1_), channel_id=1, source_target_pairs={{0,2},{2,4},{4,6},{6,7},{7,5},{5,3},{3,1},{1,0},{8,10},{10,12},{12... | collective-permute-start | bytes 786440 | tf_op jit(solution)/shard_map/ppermute | solution.py:417
  58.2 12.2 %collective-permute-start.25 = (bf16[1024,128]{1,0:T(8,128)(2,1)S(1)}, bf16[1024,128]{1,0:T(8,128)(2,1)S(1)}, u32[]{:S(2)}, u32[]{:S(2)}) collective-permute-start(bf16[1024,128]{1,0:T(8,128)(2,1)S(1)} %collective-permute-done.23.rest_7_), channel_id=1, source_target_pairs={{2,0},{4,2},{6,4},{7,6},{5,7},{3,5},{1,3},{0,1},{10,8},{12,10},{14... | collective-permute-start | bytes 786440 | tf_op jit(solution)/shard_map/ppermute | solution.py:418
  77.0 10.3 %collective-permute-start.28 = (bf16[1024,128]{1,0:T(8,128)(2,1)S(1)}, bf16[1024,128]{1,0:T(8,128)(2,1)S(1)}, u32[]{:S(2)}, u32[]{:S(2)}) collective-permute-start(bf16[1024,128]{1,0:T(8,128)(2,1)S(1)} %collective-permute-done.25.rest_6_), channel_id=1, source_target_pairs={{2,0},{4,2},{6,4},{7,6},{5,7},{3,5},{1,3},{0,1},{10,8},{12,10},{14... | collective-permute-start | bytes 786440 | tf_op jit(solution)/shard_map/ppermute | solution.py:418
  80.3 13.2 %collective-permute-start.29 = (bf16[1056,128]{1,0:T(8,128)(2,1)S(1)}, bf16[1056,128]{1,0:T(8,128)(2,1)S(1)}, u32[]{:S(2)}, u32[]{:S(2)}) collective-permute-start(bf16[1056,128]{1,0:T(8,128)(2,1)S(1)} %collective-permute-done.19.rest_2_), channel_id=1, source_target_pairs={{0,2},{2,4},{4,6},{6,7},{7,5},{5,3},{3,1},{1,0},{8,10},{10,12},{12... | collective-permute-start | bytes 811016 | tf_op jit(solution)/shard_map/ppermute | solution.py:417
  83.4 10.1 %collective-permute-start.30 = (bf16[1056,128]{1,0:T(8,128)(2,1)S(1)}, bf16[1056,128]{1,0:T(8,128)(2,1)S(1)}, u32[]{:S(2)}, u32[]{:S(2)}) collective-permute-start(bf16[1056,128]{1,0:T(8,128)(2,1)S(1)} %collective-permute-done.21.rest_5_), channel_id=1, source_target_pairs={{2,0},{4,2},{6,4},{7,6},{5,7},{3,5},{1,3},{0,1},{10,8},{12,10},{14... | collective-permute-start | bytes 811016 | tf_op jit(solution)/shard_map/ppermute | solution.py:414
  89.9 11.2 %collective-permute-start.33 = (bf16[256,512]{1,0:T(8,128)(2,1)S(1)}, bf16[256,512]{1,0:T(8,128)(2,1)S(1)}, u32[]{:S(2)}, u32[]{:S(2)}) collective-permute-start(bf16[256,512]{1,0:T(8,128)(2,1)S(1)} %out_projection.2.rest_0_.rest_2_), channel_id=1, source_target_pairs={{0,2},{2,4},{4,6},{6,7},{7,5},{5,3},{3,1},{1,0},{8,10},{10,12},{12... | collective-permute-start | bytes 786440 | tf_op jit(solution)/shard_map/ppermute | solution.py:417
  90.7 10.3 %collective-permute-start.34 = (bf16[256,512]{1,0:T(8,128)(2,1)S(1)}, bf16[256,512]{1,0:T(8,128)(2,1)S(1)}, u32[]{:S(2)}, u32[]{:S(2)}) collective-permute-start(bf16[256,512]{1,0:T(8,128)(2,1)S(1)} %out_projection.2.rest_0_.rest_2_), channel_id=1, source_target_pairs={{2,0},{4,2},{6,4},{7,6},{5,7},{3,5},{1,3},{0,1},{10,8},{12,10},{14... | collective-permute-start | bytes 786440 | tf_op jit(solution)/shard_map/ppermute | solution.py:418
  95.8 10.6 %collective-permute-start.31 = (bf16[272,512]{1,0:T(8,128)(2,1)S(1)}, bf16[272,512]{1,0:T(8,128)(2,1)S(1)}, u32[]{:S(2)}, u32[]{:S(2)}) collective-permute-start(bf16[272,512]{1,0:T(8,128)(2,1)S(1)} %out_projection.3.rest_1_.rest_2_), channel_id=1, source_target_pairs={{0,2},{2,4},{4,6},{6,7},{7,5},{5,3},{3,1},{1,0},{8,10},{10,12},{12... | collective-permute-start | bytes 835592 | tf_op jit(solution)/shard_map/ppermute | solution.py:417
  96.7 9.7 %collective-permute-start.32 = (bf16[272,512]{1,0:T(8,128)(2,1)S(1)}, bf16[272,512]{1,0:T(8,128)(2,1)S(1)}, u32[]{:S(2)}, u32[]{:S(2)}) collective-permute-start(bf16[272,512]{1,0:T(8,128)(2,1)S(1)} %out_projection.3.rest_1_.rest_2_), channel_id=1, source_target_pairs={{2,0},{4,2},{6,4},{7,6},{5,7},{3,5},{1,3},{0,1},{10,8},{12,10},{14... | collective-permute-start | bytes 835592 | tf_op jit(solution)/shard_map/ppermute | solution.py:418
  101.1 11.9 %collective-permute-start.37 = (bf16[256,512]{1,0:T(8,128)(2,1)S(1)}, bf16[256,512]{1,0:T(8,128)(2,1)S(1)}, u32[]{:S(2)}, u32[]{:S(2)}) collective-permute-start(bf16[256,512]{1,0:T(8,128)(2,1)S(1)} %collective-permute-done.33.rest_0_), channel_id=1, source_target_pairs={{0,2},{2,4},{4,6},{6,7},{7,5},{5,3},{3,1},{1,0},{8,10},{10,12},{12... | collective-permute-start | bytes 786440 | tf_op jit(solution)/shard_map/ppermute | solution.py:417
  102.2 10.8 %collective-permute-start.38 = (bf16[256,512]{1,0:T(8,128)(2,1)S(1)}, bf16[256,512]{1,0:T(8,128)(2,1)S(1)}, u32[]{:S(2)}, u32[]{:S(2)}) collective-permute-start(bf16[256,512]{1,0:T(8,128)(2,1)S(1)} %collective-permute-done.34.rest_2_), channel_id=1, source_target_pairs={{2,0},{4,2},{6,4},{7,6},{5,7},{3,5},{1,3},{0,1},{10,8},{12,10},{14... | collective-permute-start | bytes 786440 | tf_op jit(solution)/shard_map/ppermute | solution.py:418
  106.4 11.8 %collective-permute-start.35 = (bf16[272,512]{1,0:T(8,128)(2,1)S(1)}, bf16[272,512]{1,0:T(8,128)(2,1)S(1)}, u32[]{:S(2)}, u32[]{:S(2)}) collective-permute-start(bf16[272,512]{1,0:T(8,128)(2,1)S(1)} %collective-permute-done.31.rest_1_), channel_id=1, source_target_pairs={{0,2},{2,4},{4,6},{6,7},{7,5},{5,3},{3,1},{1,0},{8,10},{10,12},{12... | collective-permute-start | bytes 835592 | tf_op jit(solution)/shard_map/ppermute | solution.py:417
  107.3 11.0 %collective-permute-start.36 = (bf16[272,512]{1,0:T(8,128)(2,1)S(1)}, bf16[272,512]{1,0:T(8,128)(2,1)S(1)}, u32[]{:S(2)}, u32[]{:S(2)}) collective-permute-start(bf16[272,512]{1,0:T(8,128)(2,1)S(1)} %collective-permute-done.32.rest_3_), channel_id=1, source_target_pairs={{2,0},{4,2},{6,4},{7,6},{5,7},{3,5},{1,3},{0,1},{10,8},{12,10},{14... | collective-permute-start | bytes 835592 | tf_op jit(solution)/shard_map/ppermute | solution.py:418
  113.0 13.1 %collective-permute-start.40 = (bf16[256,512]{1,0:T(8,128)(2,1)S(1)}, bf16[256,512]{1,0:T(8,128)(2,1)S(1)}, u32[]{:S(2)}, u32[]{:S(2)}) collective-permute-start(bf16[256,512]{1,0:T(8,128)(2,1)S(1)} %collective-permute-done.37.rest_0_), channel_id=1, source_target_pairs={{0,2},{2,4},{4,6},{6,7},{7,5},{5,3},{3,1},{1,0},{8,10},{10,12},{12... | collective-permute-start | bytes 786440 | tf_op jit(solution)/shard_map/ppermute | solution.py:417
  118.3 13.0 %collective-permute-start.39 = (bf16[272,512]{1,0:T(8,128)(2,1)S(1)}, bf16[272,512]{1,0:T(8,128)(2,1)S(1)}, u32[]{:S(2)}, u32[]{:S(2)}) collective-permute-start(bf16[272,512]{1,0:T(8,128)(2,1)S(1)} %collective-permute-done.36.rest_3_), channel_id=1, source_target_pairs={{2,0},{4,2},{6,4},{7,6},{5,7},{3,5},{1,3},{0,1},{10,8},{12,10},{14... | collective-permute-start | bytes 835592 | tf_op jit(solution)/shard_map/ppermute | solution.py:418
  119.5 23.0 %collective-permute-start.41 = (bf16[272,512]{1,0:T(8,128)(2,1)S(1)}, bf16[272,512]{1,0:T(8,128)(2,1)S(1)}, u32[]{:S(2)}, u32[]{:S(2)}) collective-permute-start(bf16[272,512]{1,0:T(8,128)(2,1)S(1)} %collective-permute-done.35.rest_1_), channel_id=1, source_target_pairs={{0,2},{2,4},{4,6},{6,7},{7,5},{5,3},{3,1},{1,0},{8,10},{10,12},{12... | collective-permute-start | bytes 835592 | tf_op jit(solution)/shard_map/ppermute | solution.py:417
  120.3 22.2 %collective-permute-start.42 = (bf16[256,512]{1,0:T(8,128)(2,1)S(1)}, bf16[256,512]{1,0:T(8,128)(2,1)S(1)}, u32[]{:S(2)}, u32[]{:S(2)}) collective-permute-start(bf16[256,512]{1,0:T(8,128)(2,1)S(1)} %collective-permute-done.38.rest_2_), channel_id=1, source_target_pairs={{2,0},{4,2},{6,4},{7,6},{5,7},{3,5},{1,3},{0,1},{10,8},{12,10},{14... | collective-permute-start | bytes 786440 | tf_op jit(solution)/shard_map/ppermute | solution.py:418
  126.1 25.3 %collective-permute-start.43 = (bf16[256,512]{1,0:T(8,128)(2,1)S(1)}, bf16[256,512]{1,0:T(8,128)(2,1)S(1)}, u32[]{:S(2)}, u32[]{:S(2)}) collective-permute-start(bf16[256,512]{1,0:T(8,128)(2,1)S(1)} %collective-permute-done.40.rest_0_), channel_id=1, source_target_pairs={{0,2},{2,4},{4,6},{6,7},{7,5},{5,3},{3,1},{1,0},{8,10},{10,12},{12... | collective-permute-start | bytes 786440 | tf_op jit(solution)/shard_map/ppermute | solution.py:411
  131.3 27.0 %collective-permute-start.44 = (bf16[272,512]{1,0:T(8,128)(2,1)S(1)}, bf16[272,512]{1,0:T(8,128)(2,1)S(1)}, u32[]{:S(2)}, u32[]{:S(2)}) collective-permute-start(bf16[272,512]{1,0:T(8,128)(2,1)S(1)} %collective-permute-done.39.rest_3_), channel_id=1, source_target_pairs={{2,0},{4,2},{6,4},{7,6},{5,7},{3,5},{1,3},{0,1},{10,8},{12,10},{14... | collective-permute-start | bytes 835592 | tf_op jit(solution)/shard_map/ppermute | solution.py:414
  168.7 10.2 %collective-permute-start.47 = (bf16[256,512]{1,0:T(8,128)(2,1)S(1)}, bf16[256,512]{1,0:T(8,128)(2,1)S(1)}, u32[]{:S(2)}, u32[]{:S(2)}) collective-permute-start(bf16[256,512]{1,0:T(8,128)(2,1)S(1)} %get-tuple-element.170), channel_id=1, source_target_pairs={{0,2},{2,4},{4,6},{6,7},{7,5},{5,3},{3,1},{1,0},{8,10},{10,12},{12... | collective-permute-start | bytes 786440 | tf_op jit(solution)/shard_map/ppermute | solution.py:441
  (42 other events, 540.2 us)

commit v3 on v2

v3 whole, which is shorter than its diff:
```python
import functools
import math

import jax
import jax.numpy as jnp
from jax import lax
from jax.experimental import pallas as pl
from jax.experimental.pallas import tpu as pltpu
from jax.sharding import PartitionSpec as P

D = 4096
H = 32
KVH = 8
HD = 128
GROUP = H // KVH
WIDTH = KVH * HD
EPS = 1e-05
NEG = -1e30
Z_CHIPS = 4

HBM = pl.BlockSpec(memory_space=pltpu.HBM)
VMEM = pl.BlockSpec(memory_space=pltpu.VMEM)
SMEM = pl.BlockSpec(memory_space=pltpu.SMEM)
F32 = jnp.float32
BF16 = jnp.bfloat16


def ring_order(n):
    columns = n // Z_CHIPS
    if n % Z_CHIPS or columns % 2:
        return list(range(n))
    order = [z * columns for z in range(Z_CHIPS)]
    for i, z in enumerate(reversed(range(Z_CHIPS))):
        xs = range(1, columns) if i % 2 == 0 else range(columns - 1, 0, -1)
        order += [z * columns + x for x in xs]
    return order


def params(mib):
    return pltpu.CompilerParams(vmem_limit_bytes=mib * 2**20)


STEP = pl.CostEstimate(flops=500_000_000, bytes_accessed=1_000_000, transcendentals=0)


def copies(pairs, sems):
    out = [pltpu.make_async_copy(src, dst, sems.at[i]) for i, (src, dst) in enumerate(pairs)]
    for c in out:
        c.start()
    return out


def pack_kernel(kv_ref, ask_ref, out_ref):
    rows, width = kv_ref.shape
    for i in range(width // HD):
        out_ref[i * rows : (i + 1) * rows, :] = kv_ref[:, i * HD : (i + 1) * HD]
    ask = ask_ref[...].astype(F32)
    heads = jnp.concatenate([ask[:, i * HD : (i + 1) * HD] for i in range(H)], axis=0)
    out_ref[rows * (width // HD) :, :] = heads.astype(BF16)


def pack(kv, ask):
    rows, count = kv.shape[0], kv.shape[1] // HD
    return pl.pallas_call(
        pack_kernel,
        out_shape=jax.ShapeDtypeStruct((count * rows + H, HD), BF16),
        in_specs=[VMEM, VMEM],
        out_specs=VMEM,
        cost_estimate=STEP,
        name="pack_keys",
    )(kv, ask)


def pieces(parts, rows):
    half = len(parts) // 2
    out = []
    for i, part in enumerate(parts):
        if i == half:
            out.append((half, part, 0, range(KVH)))
        elif i == half + 1:
            out.append((half, part, -KVH * rows, range(KVH, 2 * KVH)))
        else:
            out.append((i if i < half else i - 1, part, 0, range(2 * KVH)))
    return out


def attention_kernel(count, first, rows, owners, q_in, seg_ref, *rest):
    parts, (out_ref, kv, q, sems) = rest[:count], rest[-4:]
    total = kv.shape[1]
    local = q_in.shape[0]
    moving = copies([(q_in.at[pl.ds(first, rows)], q)], sems)
    for d, part, offset, heads in pieces(parts, local):
        at = pl.ds(pl.multiple_of(owners[d] * local, 16), local)
        for i in heads:
            kv[i, at, :] = part[offset + i * local : offset + (i + 1) * local, :]
    key_pos = lax.broadcasted_iota(jnp.int32, (rows, total), 1)
    query_pos = lax.broadcasted_iota(jnp.int32, (rows, total), 0) + (owners[0] * local + first)
    span = jnp.broadcast_to(seg_ref[...], (rows, total)).astype(F32)
    own_span = jnp.sum(jnp.where(key_pos == query_pos, span, 0.0), axis=-1, keepdims=True)
    seen = (key_pos <= query_pos) & (span == own_span)
    bias = jnp.where(seen, 0.0, NEG).astype(F32)
    bias = jnp.concatenate([bias] * GROUP, axis=0)
    if len(rest) > count + 4:
        out_ref[H * rows :, :] = rest[count][...]
    moving[0].wait()
    for k in range(KVH):
        heads = range(k * GROUP, (k + 1) * GROUP)
        four = jnp.concatenate([q[:, i * HD : (i + 1) * HD] for i in heads], axis=0)
        s = lax.dot_general(four, kv[k], (((1,), (1,)), ((), ())), preferred_element_type=F32)
        s = s * (1.0 / math.sqrt(HD)) + bias
        w = jnp.exp(s - jnp.max(s, axis=-1, keepdims=True)).astype(BF16)
        t = jnp.sum(w.astype(F32), axis=-1, keepdims=True)
        o = jnp.dot(w, kv[KVH + k], preferred_element_type=F32) / t
        out_ref[k * GROUP * rows : (k + 1) * GROUP * rows, :] = o.astype(BF16)


def attention(first, rows, owners, q, seg, parts, dec=()):
    total = seg.shape[1]
    return pl.pallas_call(
        functools.partial(attention_kernel, len(parts), first, rows),
        out_shape=jax.ShapeDtypeStruct((H * (rows + len(dec)), HD), BF16),
        in_specs=[SMEM, HBM, VMEM] + [VMEM] * (len(parts) + len(dec)),
        out_specs=VMEM,
        scratch_shapes=[
            pltpu.VMEM((2 * KVH, total, HD), BF16),
            pltpu.VMEM((rows, D), BF16),
            pltpu.SemaphoreType.DMA((1,)),
        ],
        compiler_params=params(40),
        cost_estimate=STEP,
        name="prefill_attention",
    )(owners, q, seg, *parts, *dec)


def pick_kernel(n, groups, owners, slots, *rest):
    parts, outs = rest[: n + 1], rest[n + 1 :]
    tok, grp = owners[0], owners[n]
    for j in range(groups):
        request = slots[(grp ^ j) * n + tok]
        for i, part in enumerate(parts):
            if i != n // 2:
                d = i if i < n // 2 else i - 1

                @pl.when(owners[d] == request % n)
                def _(part=part, out=outs[j]):
                    out[...] = part[part.shape[0] - H :, :]


def pick(n, groups, owners, slots, parts):
    return pl.pallas_call(
        functools.partial(pick_kernel, n, groups),
        out_shape=[jax.ShapeDtypeStruct((H, HD), BF16) for _ in range(groups)],
        in_specs=[SMEM, SMEM] + [VMEM] * (n + 1),
        out_specs=[VMEM] * groups,
        compiler_params=params(40),
        cost_estimate=STEP,
        name="pick_queries",
    )(owners, slots, *parts)


def decode_kernel(n, groups, owners, slots, length, cache_in, *rest):
    choices, (out_ref, cache_ref, sems) = rest[:groups], rest[groups:]
    positions = cache_ref.shape[1]
    moving = copies([(cache_in, cache_ref)], sems)
    tok, grp = owners[0], owners[n]
    source = (slots[grp * n + tok] // n) ^ grp
    q = choices[0][...]
    for j in range(1, groups):
        q = jnp.where(source == j, choices[j][...], q)
    head = lax.broadcasted_iota(jnp.int32, (H, positions), 0) // GROUP
    moving[0].wait()
    s = jnp.zeros((H, positions), F32)
    for k in range(KVH):
        one = lax.dot_general(
            q, cache_ref[0, :, k * HD : (k + 1) * HD], (((1,), (1,)), ((), ())), preferred_element_type=F32
        )
        s = jnp.where(head == k, one, s)
    spot = lax.broadcasted_iota(jnp.int32, (H, positions), 1)
    s = jnp.where(spot < length[0], s * (1.0 / math.sqrt(HD)), NEG)
    w = jnp.exp(s - jnp.max(s, axis=-1, keepdims=True)).astype(BF16).astype(F32)
    t = jnp.sum(w, axis=-1, keepdims=True)
    o = jnp.zeros((H, HD), F32)
    for k in range(KVH):
        mine = jnp.where(head == k, w, 0.0).astype(BF16)
        o = o + jnp.dot(
            mine, cache_ref[0, :, WIDTH + k * HD : WIDTH + (k + 1) * HD], preferred_element_type=F32
        )
    out_ref[...] = (o / t).astype(BF16)


def decode(n, owners, slots, length, choices, cache):
    groups = len(choices)
    return pl.pallas_call(
        functools.partial(decode_kernel, n, groups),
        out_shape=jax.ShapeDtypeStruct((H, HD), BF16),
        in_specs=[SMEM, SMEM, SMEM, HBM] + [VMEM] * groups,
        out_specs=VMEM,
        scratch_shapes=[pltpu.VMEM(cache.shape, BF16), pltpu.SemaphoreType.DMA((1,))],
        compiler_params=params(40),
        cost_estimate=STEP,
        name="decode_attention",
    )(owners, slots, length, cache, *choices)


class Fetch:
    def __init__(self, shares=(), blocks=()):
        self.shares, self.blocks = tuple(shares), tuple(blocks)

    def shapes(self, cols, wide):
        out = [jax.ShapeDtypeStruct((len(self.shares) * cols, wide), BF16)] * 2 if self.shares else []
        return out + [jax.ShapeDtypeStruct((wide, cols), BF16) for _ in self.blocks]

    def count(self):
        return 2 * len(self.shares) + len(self.blocks)

    def ins(self):
        return 3 if self.blocks else 2 if self.shares else 0

    def start(self, owners, weights, outs, sems):
        pairs = []
        if self.shares:
            gate, up = weights[:2]
            cols = outs[0].shape[0] // len(self.shares)
            for i, share in enumerate(self.shares):
                at = pl.ds(pl.multiple_of(owners[share] * cols, cols), cols)
                to = pl.ds(i * cols, cols)
                pairs += [(gate.at[at], outs[0].at[to]), (up.at[at], outs[1].at[to])]
            outs = outs[2:]
        for block, out in zip(self.blocks, outs):
            cols = out.shape[1]
            pairs.append((weights[2].at[:, pl.ds(pl.multiple_of(owners[block] * cols, HD), cols)], out))
        return copies(pairs, sems)


def project_kernel(n, rows, fetch, owners, *rest):
    weights, rest = rest[: fetch.ins()], rest[fetch.ins() :]
    parts, (wo_ref, resid_ref, out_ref) = rest[:n], rest[n : n + 3]
    x, dec, sems = rest[-3:]
    moving = fetch.start(owners, weights, rest[n + 3 : -3], sems)
    for d, part in enumerate(parts):
        at = pl.ds(pl.multiple_of(owners[d] * rows, 16), rows)
        for i in range(H):
            x[at, i * HD : (i + 1) * HD] = part[i * rows : (i + 1) * rows, :]
        if part.shape[0] > H * rows:
            dec[pl.ds(pl.multiple_of(owners[d] * H, H), H), :] = part[H * rows :, :]
    spare = x.shape[0] - n * rows
    if spare:
        at = lax.broadcasted_iota(jnp.int32, (H * spare, n * H), 0)
        of = lax.broadcasted_iota(jnp.int32, (H * spare, n * H), 1)
        chosen = jnp.where(of == (at % spare) * H + at // spare, 1.0, 0.0).astype(BF16)
        heads = jnp.dot(chosen, dec[...], preferred_element_type=F32).astype(BF16)
        for i in range(H):
            x[n * rows :, i * HD : (i + 1) * HD] = heads[i * spare : (i + 1) * spare]
    total = jnp.dot(x[...], wo_ref[...], preferred_element_type=F32)
    out_ref[...] = (resid_ref[...].astype(F32) + total).astype(BF16)
    for c in moving:
        c.wait()


def project(rows, owners, parts, wo, resid, fetch, weights):
    m, cols = resid.shape
    n = len(parts)
    fetched = fetch.shapes(cols, weights[0].shape[1])
    return pl.pallas_call(
        functools.partial(project_kernel, n, rows, fetch),
        out_shape=[jax.ShapeDtypeStruct((m, cols), BF16)] + fetched,
        in_specs=[SMEM] + [HBM] * fetch.ins() + [VMEM] * (n + 2),
        out_specs=[VMEM] * (1 + len(fetched)),
        scratch_shapes=[
            pltpu.VMEM((m, D), BF16),
            pltpu.VMEM((n * H, HD), BF16),
            pltpu.SemaphoreType.DMA((max(fetch.count(), 1),)),
        ],
        compiler_params=params(42),
        cost_estimate=STEP,
        name="out_projection",
    )(owners, *weights[: fetch.ins()], *parts, wo, resid)


def scale_in(x, squares, tenants, gain_ref, at):
    for j in range(0, x.shape[1], HD):
        squares = squares + x[:, j : j + HD] * x[:, j : j + HD]
    gain = jnp.broadcast_to(gain_ref[0:1, at], x.shape)
    for t in range(1, gain_ref.shape[0]):
        gain = jnp.where(tenants == t, gain_ref[t : t + 1, at], gain)
    return squares, (x * gain).astype(BF16)


def feed_kernel(shares, taken, fetch, owners, tenants_ref, gain_ref, *rest):
    weights, rest = rest[: fetch.ins()], rest[fetch.ins() :]
    w_refs, rest = rest[:2], rest[2:]
    parts, rest = rest[: 2 * len(shares)], rest[2 * len(shares) :]
    held, rest = (rest[:3], rest[3:]) if taken else (None, rest)
    (gates, lifts, squares), fetched, (scaled, sems) = rest[:3], rest[3:-2], rest[-2:]
    moving = fetch.start(owners, weights, fetched, sems)
    m = gates.shape[0]
    cols = parts[0].shape[1]
    tenants = tenants_ref[...]
    total = held[2][...] if taken else jnp.zeros((m, HD), F32)
    for i, share in enumerate(shares):
        x = jnp.concatenate([p[...] for p in parts[2 * i : 2 * i + 2]], axis=0).astype(F32)
        at = pl.ds(pl.multiple_of(owners[share] * cols, HD), cols)
        total, x = scale_in(x, total, tenants, gain_ref, at)
        scaled[:, i * cols : (i + 1) * cols] = x
    squares[...] = total
    for i, out in enumerate((gates, lifts)):
        one = jnp.dot(scaled[...], w_refs[i][...], preferred_element_type=F32)
        out[...] = held[i][...] + one if taken else one
    for c in moving:
        c.wait()


def feed(shares, owners, tenants, gain, weights, w, parts, held, fetch, grant):
    m, (deep, wide) = tenants.shape[0], w[0].shape
    cols = parts[0].shape[1]
    first = 5 + fetch.ins() + len(parts)
    fetched = fetch.shapes(cols, wide)
    sums = [jax.ShapeDtypeStruct((m, wide), F32)] * 2 + [jax.ShapeDtypeStruct((m, HD), F32)]
    return pl.pallas_call(
        functools.partial(feed_kernel, shares, len(held) > 0, fetch),
        out_shape=sums + fetched,
        in_specs=[SMEM, VMEM, VMEM] + [HBM] * fetch.ins() + [VMEM] * (2 + len(parts) + len(held)),
        out_specs=[VMEM] * (3 + len(fetched)),
        scratch_shapes=[
            pltpu.VMEM((m, deep), BF16),
            pltpu.SemaphoreType.DMA((fetch.count(),)),
        ],
        input_output_aliases={first + i: i for i in range(len(held))},
        compiler_params=params(grant),
        cost_estimate=STEP,
        name="gate_up_sum",
    )(owners, tenants, gain, *weights[: fetch.ins()], *w, *parts, *held)


def hidden_kernel(lo, hi, share, owners, tenants_ref, gain_ref, w_gate, w_up, part, gates, lifts, squares, out):
    cols = part.shape[1]
    at = pl.ds(pl.multiple_of(owners[share] * cols, HD), cols)
    total, x = scale_in(part[...].astype(F32), squares[lo:hi, :], tenants_ref[lo:hi, :], gain_ref, at)
    scale = lax.rsqrt(jnp.sum(total, axis=-1, keepdims=True) / D + EPS)
    gate = (gates[lo:hi, :] + jnp.dot(x, w_gate[...], preferred_element_type=F32)) * scale
    gate = gate / (1.0 + jnp.exp(-gate))
    lift = (lifts[lo:hi, :] + jnp.dot(x, w_up[...], preferred_element_type=F32)) * scale
    out[...] = (gate * lift).astype(BF16)


def hide(lo, hi, share, owners, tenants, gain, w, part, held):
    return pl.pallas_call(
        functools.partial(hidden_kernel, lo, hi, share),
        out_shape=jax.ShapeDtypeStruct((hi - lo, w[0].shape[1]), BF16),
        in_specs=[SMEM] + [VMEM] * 8,
        out_specs=VMEM,
        compiler_params=params(16),
        cost_estimate=STEP,
        name="hidden",
    )(owners, tenants, gain, *w, part, *held)


def down_kernel(flags, own, owners, hidden, *rest):
    count = len(flags)
    weights, rest = rest[:count], rest[count:]
    terms, outs = rest[: sum(flags) + own], rest[sum(flags) + own :]
    taken = 0
    for i in range(count):
        total = jnp.dot(hidden[...], weights[i][...], preferred_element_type=F32)
        for term in terms[taken : taken + flags[i] + own]:
            total = total + term[...].astype(F32)
        taken += flags[i]
        outs[i][...] = total.astype(BF16)


def down(flags, owners, hidden, weights, arrived, own=()):
    m, cols = hidden.shape[0], weights[0].shape[1]
    return pl.pallas_call(
        functools.partial(down_kernel, flags, len(own)),
        out_shape=[jax.ShapeDtypeStruct((m, cols), BF16) for _ in flags],
        in_specs=[SMEM] + [VMEM] * (1 + len(flags) + len(arrived) + len(own)),
        out_specs=[VMEM] * len(flags),
        compiler_params=params(16),
        cost_estimate=STEP,
        name="down_sum",
    )(owners, hidden, *weights, *arrived, *own)


class Chain:
    def __init__(self, n, order, own, last, cut=0):
        self.n, self.half, self.last, self.cut = n, n // 2, last, cut
        self.fw = [(order[i], order[(i + 1) % n]) for i in range(n)]
        self.bw = [(b, a) for a, b in self.fw]
        self.own, self.ahead, self.behind, self.hops = own, [own], [own], 0

    def done(self):
        return self.hops == self.half

    def parts(self):
        return [self.own] + self.ahead[1:] + self.behind[:0:-1]


class Order:
    def __init__(self, ids):
        self.ids, self.last = ids, ()

    def after(self):
        return lax.optimization_barrier((self.ids, *self.last))[0]

    def mark(self, *out):
        self.last = out
        return out[0]

    def tied(self, *arrays):
        out = lax.optimization_barrier((*arrays, *self.last))[: len(arrays)]
        self.last = (out[0],)
        return out

    def hop(self, chain):
        chain.hops += 1
        f, b = chain.ahead[-1], chain.behind[-1]
        if chain.done() and chain.last == "split":
            f, b = f[: chain.cut], b[chain.cut :]
        if chain.done() and chain.last == "fw":
            (f,) = self.tied(f)
            chain.ahead.append(lax.ppermute(f, "tok", chain.fw))
        elif chain.done() and chain.last == "bw":
            (b,) = self.tied(b)
            chain.behind.append(lax.ppermute(b, "tok", chain.bw))
        else:
            f, b = self.tied(f, b)
            chain.ahead.append(lax.ppermute(f, "tok", chain.fw))
            chain.behind.append(lax.ppermute(b, "tok", chain.bw))


class Sum:
    def __init__(self, run, chain, hidden, blocks, own):
        self.run, self.chain, self.hidden, self.blocks = run, chain, hidden, blocks
        self.own, self.step, self.arrived = own, 0, ()

    def call(self, blocks, flags, own=()):
        weights = [self.blocks[-b % self.chain.n] for b in blocks]
        out = down(flags, self.run.after(), self.hidden, weights, self.arrived, own)
        self.run.mark(out[0])
        return out

    def hop(self):
        chain = self.chain
        d, forward = chain.half - self.step, chain.last == "fw"
        if self.step == 0:
            out = self.run.tied(*self.call([d], [0]))
            self.arrived = (lax.ppermute(out[0], "tok", chain.fw if forward else chain.bw),)
        else:
            flags = [1, 1] if self.step > 1 else ([1, 0] if forward else [0, 1])
            out = self.run.tied(*self.call([d, -d], flags))
            self.arrived = (lax.ppermute(out[0], "tok", chain.fw), lax.ppermute(out[1], "tok", chain.bw))
        self.step += 1

    def finish(self):
        return self.call([0], [2], (self.own,))[0]


def shards(
    pre_q,
    pre_kv,
    pre_segment,
    dec_q,
    cache,
    cache_len,
    slot_request,
    resid,
    wo,
    tenant,
    norm_gain,
    w_gate,
    w_up,
    w_down,
):
    n, groups = lax.axis_size("tok"), lax.axis_size("grp")
    tok, grp = lax.axis_index("tok"), lax.axis_index("grp")
    local = pre_q.shape[0]
    rows = local // 2
    cols = wo.shape[1]
    half = n // 2
    spare = -(-n // 16) * 16
    order = ring_order(n)
    ids = jnp.arange(n, dtype=jnp.int32)
    place = sum(jnp.where(tok == t, i, 0) for i, t in enumerate(order)).astype(jnp.int32)
    spots = (place - ids) % n
    owners = sum(jnp.where(spots == i, t, 0) for i, t in enumerate(order)).astype(jnp.int32)
    owners = jnp.concatenate([owners, jnp.reshape(grp, (1,)).astype(jnp.int32)])

    def split(a):
        a = a.reshape(n, local + 1, -1)
        first = a[:, :rows].reshape(n * rows, -1)
        second = a[:, rows:local].reshape(n * rows, -1)
        tail = jnp.pad(a[:, local], ((0, spare - n), (0, 0)))
        return first, jnp.concatenate([second, tail], axis=0)

    resids = split(resid)
    tenants = jnp.concatenate(split(tenant[0][:, None]), axis=0)
    run = Order(owners)

    def chain(own, last):
        return Chain(n, order, own, last)

    keys = Chain(n, order, pack(pre_kv, dec_q), "split", KVH * local)
    run.hop(keys)
    run.mark(*run.last, *resids, tenants, owners)
    while not keys.done():
        run.hop(keys)
    kv = keys.parts()
    a = chain(run.mark(attention(0, rows, run.after(), pre_q, pre_segment, kv)), "fw")
    run.hop(a)
    choices = list(pick(n, groups, run.after(), slot_request, kv))
    run.mark(choices[0])
    for j in range(1, groups):
        (choices[j],) = run.tied(choices[j])
        choices[j] = lax.ppermute(choices[j], "grp", [(i, i ^ j) for i in range(groups)])
    run.hop(a)
    dec = run.mark(decode(n, run.after(), slot_request, cache_len, choices, cache))
    b = chain(run.mark(attention(rows, rows, run.after(), pre_q, pre_segment, kv, (dec,))), "bw")
    run.hop(b)
    while not a.done():
        run.hop(a)
        run.hop(b)

    weights = (w_gate, w_up, w_down)
    mixed_a = project(rows, run.after(), a.parts(), wo, resids[0], Fetch(), weights)[0]
    run.mark(mixed_a)
    g = chain(mixed_a, "fw")
    run.hop(g)
    while not b.done():
        run.hop(b)
        if not b.done():
            run.hop(g)
    mixed_b, *w = project(rows, run.after(), b.parts(), wo, resids[1], Fetch([0]), weights)
    run.mark(mixed_b)
    h = chain(mixed_b, "bw")
    run.hop(h)

    m_a, m = mixed_a.shape[0], tenants.shape[0]
    held, blocks = (), {}
    for i in range(half):
        shares = [i, n - i] if i else [0]
        if i:
            parts = [g.ahead[i], h.ahead[i], g.behind[i], h.behind[i]]
        else:
            parts = [mixed_a, mixed_b]
        later = [half] if i + 1 == half else [i + 1, n - i - 1]
        early = []
        if i == 1:
            early = [half]
        elif i > 1:
            early = [half + 1 - i, n - half - 1 + i]
        if i + 1 == half:
            early += [d for d in range(n) if d not in early and d not in blocks]
        grant = 30 if i == 0 else 20 if i + 1 == half else 24
        out = feed(
            shares, run.after(), tenants, norm_gain, weights, w, parts, held, Fetch(later, early), grant
        )
        held, w = out[:3], out[3:5]
        blocks.update(zip(early, out[5:]))
        run.mark(out[2])
        if not g.done():
            run.hop(g)
        if not h.done():
            run.hop(h)

    def finish(lo, hi, part):
        return run.mark(hide(lo, hi, half, run.after(), tenants, norm_gain, w, part, held))

    hid_a = finish(0, m_a, g.ahead[half])
    sum_a = Sum(run, g, hid_a, blocks, mixed_a)
    sum_a.hop()
    hid_b = finish(m_a, m, h.behind[half])
    sum_b = Sum(run, h, hid_b, blocks, mixed_b)
    sum_b.hop()
    for _ in range(1, half):
        sum_a.hop()
        sum_b.hop()
    out_a = sum_a.finish()
    out_b = sum_b.finish()

    top = out_a.reshape(n, rows, cols)
    low = out_b[: n * rows].reshape(n, rows, cols)
    tail = out_b[n * rows : n * rows + n].reshape(n, 1, cols)
    return jnp.concatenate([top, low, tail], axis=1).reshape(n * (local + 1), cols)


def solution(mesh):
    in_specs = (
        P(("grp", "tok"), None),
        P(("grp", "tok"), None),
        P("grp", None),
        P(("grp", "tok"), None),
        P(("grp", "tok"), None, None),
        P(("grp", "tok")),
        P(),
        P("grp", "tok"),
        P(None, "tok"),
        P("grp", None),
        P(),
        P(None, "tok"),
        P(None, "tok"),
        P("tok", None),
    )
    out_specs = P("grp", "tok")
    return jax.shard_map(shards, mesh=mesh, in_specs=in_specs, out_specs=out_specs, check_vma=False)
```

time: 216 us -> 189 us (0.88); the launches traced: 212 us -> 189 us
  Pallas kernels: 83.1 us -> 60.9 us
  starting transfers between devices: 71.4 us -> 53.7 us
  waiting for transfers between devices: 46.8 us -> 63.6 us
    ppermute x21 -> x18, starting transfers between devices: 31.1 us -> 5.63 us  [hop(): chain.behind.append(lax.ppermute(b, 'tok', chain.bw))]
    pallas_call x22 -> x20, Pallas kernels: 73.1 us -> 53.4 us  [the longest x4 28 us: feed(): pl.pallas_call(functools.partial(feed_kernel, shares, len(held) > 0, fetc...]
    ppermute x21 -> x18, waiting for transfers between devices: 13.7 us -> 24.1 us  [hop(): chain.behind.append(lax.ppermute(b, 'tok', chain.bw))]
    ppermute x22 -> x18, starting transfers between devices: 24.1 us -> 30.9 us  [hop(): chain.ahead.append(lax.ppermute(f, 'tok', chain.fw))]
    ppermute x6, waiting for transfers between devices: 2.01 us -> 7.07 us  [hop(): lax.ppermute(out[1], 'tok', chain.bw)]
    unnamed x17 -> x24, local copies, waits for them, and re-layouts: 0.12 us -> 2.7 us
    ppermute x6, starting transfers between devices: 6.4 us -> 8.81 us  [hop(): lax.ppermute(out[1], 'tok', chain.bw)]
    ppermute x2 -> x3, waiting for transfers between devices: 2.22 us -> 0.01 us  [shards(): lax.ppermute(choices[j], 'grp', [(i, i ^ j) for i in range(groups)])]
  transfers between devices with their start and end apart: 59 -> 53, of which waited for: 28 -> 30; matrix products, arithmetic and copies ran while one was open for 4% -> 3% of each run, Pallas kernels for 38% -> 29%
where the time goes in v3:
time: 189 us
  waiting for transfers between devices  63.6 us (34%)
  Pallas kernels  60.9 us (32%)
  starting transfers between devices  53.7 us (28%)
  local copies, waits for them, and re-layouts  7.42 us (4%)
    ppermute x18, starting transfers between devices, hop(): chain.ahead.append(lax.ppermute(f, 'tok', chain.fw))  30.9 us
    pallas_call x4, Pallas kernels, feed(): pl.pallas_call(functools.partial(feed_kernel, shares, len(held) > 0, fetc...  28 us
    ppermute x18, waiting for transfers between devices, hop(): chain.ahead.append(lax.ppermute(f, 'tok', chain.fw))  24.1 us
    ppermute x18, waiting for transfers between devices, hop(): chain.behind.append(lax.ppermute(b, 'tok', chain.bw))  24.1 us
    pallas_call x10, Pallas kernels, down(): pl.pallas_call(functools.partial(down_kernel, flags, len(own)), out_shape...  13.8 us
    ppermute x6, starting transfers between devices, hop(): lax.ppermute(out[1], 'tok', chain.bw)  8.81 us
    ppermute x6, waiting for transfers between devices, hop(): lax.ppermute(out[1], 'tok', chain.bw)  7.07 us
    pallas_call x2, Pallas kernels, attention(): pl.pallas_call(functools.partial(attention_kernel, len(parts), first, row...  5.92 us
  transfers between devices with their start and end apart: 53, of which 30 were waited for; matrix products, arithmetic and copies ran while one was open for 3% of the time, Pallas kernels for 29%

profile of v3, /device:TPU:0, one launch (start us, length us, event | category | flops | bytes accessed | tf_op | source)
XLA Modules:
  0.0 188.5 jit_solution(1630651543526071665)
XLA Ops:
  1.8 3.0 %collective-permute-start = (bf16[1056,128]{1,0:T(8,128)(2,1)}, bf16[1056,128]{1,0:T(8,128)(2,1)S(1)}, u32[]{:S(2)}, u32[]{:S(2)}) collective-permute-start(bf16[1056,128]{1,0:T(8,128)(2,1)} %pack_keys.1.rest_0_), channel_id=1, source_target_pairs={{0,2},{2,4},{4,6},{6,7},{7,5},{5,3},{3,1},{1,0},{8,10},{10,12},{12... | collective-permute-start | bytes 811016 | tf_op jit(solution)/shard_map/ppermute | solution.py:427
  15.0 5.0 %collective-permute-done.2.rest_2_ = bf16[1056,128]{1,0:T(8,128)(2,1)S(1)} collective-permute-done((bf16[1056,128]{1,0:T(8,128)(2,1)S(1)}, bf16[1056,128]{1,0:T(8,128)(2,1)S(1)}, u32[]{:S(2)}, u32[]{:S(2)}) %collective-permute-start.2) | collective-permute-done | bytes 270368 | tf_op jit(solution)/shard_map/ppermute | solution.py:427
  23.3 4.4 %collective-permute-done.4.rest_3_ = bf16[1056,128]{1,0:T(8,128)(2,1)S(1)} collective-permute-done((bf16[1056,128]{1,0:T(8,128)(2,1)S(1)}, bf16[1056,128]{1,0:T(8,128)(2,1)S(1)}, u32[]{:S(2)}, u32[]{:S(2)}) %collective-permute-start.4) | collective-permute-done | bytes 270368 | tf_op jit(solution)/shard_map/ppermute | solution.py:427
  27.8 2.5 %collective-permute-done.5.rest_6_ = bf16[1056,128]{1,0:T(8,128)(2,1)S(1)} collective-permute-done((bf16[1056,128]{1,0:T(8,128)(2,1)S(1)}, bf16[1056,128]{1,0:T(8,128)(2,1)S(1)}, u32[]{:S(2)}, u32[]{:S(2)}) %collective-permute-start.5) | collective-permute-done | bytes 270368 | tf_op jit(solution)/shard_map/ppermute | solution.py:428
  32.4 3.4 %collective-permute-done.6.rest_4_ = bf16[512,128]{1,0:T(8,128)(2,1)S(1)} collective-permute-done((bf16[512,128]{1,0:T(8,128)(2,1)S(1)}, bf16[512,128]{1,0:T(8,128)(2,1)S(1)}, u32[]{:S(2)}, u32[]{:S(2)}) %collective-permute-start.6) | collective-permute-done | bytes 131104 | tf_op jit(solution)/shard_map/ppermute | solution.py:427
  35.8 3.0 %prefill_attention.2.rest_0_ = bf16[1024,128]{1,0:T(8,128)(2,1)S(1)} custom-call(s32[9]{0:T(128)S(1)} %pad_add_fusion.1.owners, bf16[64,4096]{1,0:T(8,128)(2,1)S(1)} %copy-done.4, s32[1,512]{1,0:T(1,128)S(1)} %copy-done.8, bf16[1056,128]{1,0:T(8,128)(2,1)S(1)} %copy-done.1, bf16[1056,128]{1,0:T(8,128)(2,1)S(1)} %collective-permute-done.rest_1_, ...), custom_call_target="tpu_custom_call" | custom-call | flops 500000000 | bytes 1000000 | tf_op jit(solution)/shard_map/prefill_attention/pallas_call | solution.py:119
  50.4 3.0 %prefill_attention.3.rest_2_ = bf16[1056,128]{1,0:T(8,128)(2,1)S(1)} custom-call(s32[9]{0:T(128)S(1)} %pad_add_fusion.1.owners, bf16[64,4096]{1,0:T(8,128)(2,1)S(1)} %copy-done.4, s32[1,512]{1,0:T(1,128)S(1)} %copy-done.8, bf16[1056,128]{1,0:T(8,128)(2,1)S(1)} %copy-done.1, bf16[1056,128]{1,0:T(8,128)(2,1)S(1)} %collective-permute-done.rest_1_, ...), custom_call_target="tpu_custom_call" | custom-call | flops 500000000 | bytes 1000000 | tf_op jit(solution)/shard_map/prefill_attention/pallas_call | solution.py:119
  55.5 3.0 %collective-permute-done.16.rest_6_ = bf16[1024,128]{1,0:T(8,128)(2,1)S(1)} collective-permute-done((bf16[1024,128]{1,0:T(8,128)(2,1)S(1)}, bf16[1024,128]{1,0:T(8,128)(2,1)S(1)}, u32[]{:S(2)}, u32[]{:S(2)}) %collective-permute-start.16) | collective-permute-done | bytes 262176 | tf_op jit(solution)/shard_map/ppermute | solution.py:428
  58.8 3.3 %collective-permute-done.13.rest_3_ = bf16[1056,128]{1,0:T(8,128)(2,1)S(1)} collective-permute-done((bf16[1056,128]{1,0:T(8,128)(2,1)S(1)}, bf16[1056,128]{1,0:T(8,128)(2,1)S(1)}, u32[]{:S(2)}, u32[]{:S(2)}) %collective-permute-start.13) | collective-permute-done | bytes 270368 | tf_op jit(solution)/shard_map/ppermute | solution.py:427
  69.1 3.7 %collective-permute-done.17.rest_4_ = bf16[1056,128]{1,0:T(8,128)(2,1)S(1)} collective-permute-done((bf16[1056,128]{1,0:T(8,128)(2,1)S(1)}, bf16[1056,128]{1,0:T(8,128)(2,1)S(1)}, u32[]{:S(2)}, u32[]{:S(2)}) %collective-permute-start.17) | collective-permute-done | bytes 270368 | tf_op jit(solution)/shard_map/ppermute | solution.py:427
  75.2 3.6 %collective-permute-done.22.rest_5_ = bf16[1024,128]{1,0:T(8,128)(2,1)S(1)} collective-permute-done((bf16[1024,128]{1,0:T(8,128)(2,1)S(1)}, bf16[1024,128]{1,0:T(8,128)(2,1)S(1)}, u32[]{:S(2)}, u32[]{:S(2)}) %collective-permute-start.22) | collective-permute-done | bytes 262176 | tf_op jit(solution)/shard_map/ppermute | solution.py:428
  78.8 2.2 %out_projection.2.rest_4_.rest_3_ = bf16[256,512]{1,0:T(8,128)(2,1)S(1)} custom-call(s32[9]{0:T(128)S(1)} %pad_add_fusion.1.owners, bf16[1024,128]{1,0:T(8,128)(2,1)S(1)} %prefill_attention.2.rest_0_, bf16[1024,128]{1,0:T(8,128)(2,1)S(1)} %collective-permute-done.8.rest_1_, bf16[1024,128]{1,0:T(8,128)(2,1)S(1)} %collective-permute-done.15.rest_2_, ...), custom_call_target="tpu_custom_call" | custom-call | flops 500000000 | bytes 1000000 | tf_op jit(solution)/shard_map/out_projection/pallas_call | solution.py:264
  84.2 7.0 %collective-permute-done.24.rest_6_ = bf16[1056,128]{1,0:T(8,128)(2,1)S(1)} collective-permute-done((bf16[1056,128]{1,0:T(8,128)(2,1)S(1)}, bf16[1056,128]{1,0:T(8,128)(2,1)S(1)}, u32[]{:S(2)}, u32[]{:S(2)}) %collective-permute-start.24) | collective-permute-done | bytes 270368 | tf_op jit(solution)/shard_map/ppermute | solution.py:424
  91.2 2.9 %out_projection.3 = (bf16[272,512]{1,0:T(8,128)(2,1)S(1)}, bf16[512,1536]{1,0:T(8,128)(2,1)S(1)}, bf16[512,1536]{1,0:T(8,128)(2,1)S(1)}) custom-call(s32[9]{0:T(128)S(1)} %pad_add_fusion.1.owners, bf16[4096,1536]{1,0:T(8,128)(2,1)} %rest_0_.9, bf16[4096,1536]{1,0:T(8,128)(2,1)} %rest_1_.9, bf16[1056,128]{1,0:T(8,128)(2,1)S(1)} %prefill_attention.3.rest_2_, ...), custom_call_target="tpu_custom_call" | custom-call | flops 500000000 | bytes 1000000 | tf_op jit(solution)/shard_map/out_projection/pallas_call | solution.py:264
  98.9 5.1 %gate_up_sum.4 = (f32[528,1536]{1,0:T(8,128)S(1)}, f32[528,1536]{1,0:T(8,128)S(1)}, f32[528,128]{1,0:T(8,128)S(1)}, bf16[1024,1536]{1,0:T(8,128)(2,1)S(1)}, bf16[1024,1536]{1,0:T(8,128)(2,1)S(1)}) custom-call(s32[9]{0:T(128)S(1)} %pad_add_fusion.1.owners, s32[528,1]{1,0:T(8,128)S(1)} %copy.35.tenants_ref, f32[4,4096]{1,0:T(4,128)S(1)} %copy-done.2, ...), custom_call_target="tpu_custom_call" | custom-call | flops 500000000 | bytes 1000000 | tf_op jit(solution)/shard_map/gate_up_sum/pallas_call | solution.py:319
  108.1 7.7 %gate_up_sum.5 = (f32[528,1536]{1,0:T(8,128)S(1)}, f32[528,1536]{1,0:T(8,128)S(1)}, f32[528,128]{1,0:T(8,128)S(1)}, bf16[1024,1536]{1,0:T(8,128)(2,1)S(1)}, bf16...) custom-call(s32[9]{0:T(128)S(1)} %pad_add_fusion.1.owners, ...), custom_call_target="tpu_custom_call", output_to_operand_aliasing={{0}: (12, {}), {1}: (13, {}), {2}: (14, {})} | custom-call | flops 500000000 | bytes 1000000 | tf_op jit(solution)/shard_map/gate_up_sum/pallas_call | solution.py:319
  120.1 6.5 %gate_up_sum.6 = (f32[528,1536]{1,0:T(8,128)S(1)}, f32[528,1536]{1,0:T(8,128)S(1)}, f32[528,128]{1,0:T(8,128)S(1)}, bf16[1024,1536]{1,0:T(8,128)(2,1)S(1)}, bf16...) custom-call(s32[9]{0:T(128)S(1)} %pad_add_fusion.1.owners, ...), custom_call_target="tpu_custom_call", output_to_operand_aliasing={{0}: (12, {}), {1}: (13, {}), {2}: (14, {})} | custom-call | flops 500000000 | bytes 1000000 | tf_op jit(solution)/shard_map/gate_up_sum/pallas_call | solution.py:319
  130.2 8.7 %gate_up_sum.7 = (f32[528,1536]{1,0:T(8,128)S(1)}, f32[528,1536]{1,0:T(8,128)S(1)}, f32[528,128]{1,0:T(8,128)S(1)}, bf16[512,1536]{1,0:T(8,128)(2,1)S(1)}, bf16[...) custom-call(s32[9]{0:T(128)S(1)} %pad_add_fusion.1.owners, ...), custom_call_target="tpu_custom_call", output_to_operand_aliasing={{0}: (12, {}), {1}: (13, {}), {2}: (14, {})} | custom-call | flops 500000000 | bytes 1000000 | tf_op jit(solution)/shard_map/gate_up_sum/pallas_call | solution.py:319
  147.4 2.3 %collective-permute-done.39.rest_2_ = bf16[256,512]{1,0:T(8,128)(2,1)S(1)} collective-permute-done((bf16[256,512]{1,0:T(8,128)(2,1)S(1)}, bf16[256,512]{1,0:T(8,128)(2,1)S(1)}, u32[]{:S(2)}, u32[]{:S(2)}) %collective-permute-start.39) | collective-permute-done | bytes 262176 | tf_op jit(solution)/shard_map/ppermute | solution.py:447
  151.2 2.5 %collective-permute-start.41 = (bf16[256,512]{1,0:T(8,128)(2,1)S(1)}, bf16[256,512]{1,0:T(8,128)(2,1)S(1)}, u32[]{:S(2)}, u32[]{:S(2)}) collective-permute-start(bf16[256,512]{1,0:T(8,128)(2,1)S(1)} %get-tuple-element.197), channel_id=1, source_target_pairs={{0,2},{2,4},{4,6},{6,7},{7,5},{5,3},{3,1},{1,0},{8,10},{10,12},{12... | collective-permute-start | bytes 786440 | tf_op jit(solution)/shard_map/ppermute | solution.py:451
  153.7 2.3 %collective-permute-done.40.rest_2_ = bf16[272,512]{1,0:T(8,128)(2,1)S(1)} collective-permute-done((bf16[272,512]{1,0:T(8,128)(2,1)S(1)}, bf16[272,512]{1,0:T(8,128)(2,1)S(1)}, u32[]{:S(2)}, u32[]{:S(2)}) %collective-permute-start.40) | collective-permute-done | bytes 278560 | tf_op jit(solution)/shard_map/ppermute | solution.py:447
  160.4 2.4 %collective-permute-done.42.rest_3_ = bf16[256,512]{1,0:T(8,128)(2,1)S(1)} collective-permute-done((bf16[256,512]{1,0:T(8,128)(2,1)S(1)}, bf16[256,512]{1,0:T(8,128)(2,1)S(1)}, u32[]{:S(2)}, u32[]{:S(2)}) %collective-permute-start.42) | collective-permute-done | bytes 262176 | tf_op jit(solution)/shard_map/ppermute | solution.py:451
  166.4 2.4 %collective-permute-done.44.rest_3_ = bf16[272,512]{1,0:T(8,128)(2,1)S(1)} collective-permute-done((bf16[272,512]{1,0:T(8,128)(2,1)S(1)}, bf16[272,512]{1,0:T(8,128)(2,1)S(1)}, u32[]{:S(2)}, u32[]{:S(2)}) %collective-permute-start.44) | collective-permute-done | bytes 278560 | tf_op jit(solution)/shard_map/ppermute | solution.py:451
  183.6 2.4 %collective-permute-done.51.rest_1_ = bf16[272,512]{1,0:T(8,128)(2,1)S(1)} collective-permute-done((bf16[272,512]{1,0:T(8,128)(2,1)S(1)}, bf16[272,512]{1,0:T(8,128)(2,1)S(1)}, u32[]{:S(2)}, u32[]{:S(2)}) %collective-permute-start.51) | collective-permute-done | bytes 278560 | tf_op jit(solution)/shard_map/ppermute | solution.py:451
  (150 shorter events, 95.1 us)
Async XLA Ops:
  1.8 9.7 %collective-permute-start = (bf16[1056,128]{1,0:T(8,128)(2,1)}, bf16[1056,128]{1,0:T(8,128)(2,1)S(1)}, u32[]{:S(2)}, u32[]{:S(2)}) collective-permute-start(bf16[1056,128]{1,0:T(8,128)(2,1)} %pack_keys.1.rest_0_), channel_id=1, source_target_pairs={{0,2},{2,4},{4,6},{6,7},{7,5},{5,3},{3,1},{1,0},{8,10},{10,12},{12... | collective-permute-start | bytes 811016 | tf_op jit(solution)/shard_map/ppermute | solution.py:427
  62.5 10.2 %collective-permute-start.17 = (bf16[1056,128]{1,0:T(8,128)(2,1)S(1)}, bf16[1056,128]{1,0:T(8,128)(2,1)S(1)}, u32[]{:S(2)}, u32[]{:S(2)}) collective-permute-start(bf16[1056,128]{1,0:T(8,128)(2,1)S(1)} %collective-permute-done.13.rest_3_), channel_id=1, source_target_pairs={{0,2},{2,4},{4,6},{6,7},{7,5},{5,3},{3,1},{1,0},{8,10},{10,12},{12... | collective-permute-start | bytes 811016 | tf_op jit(solution)/shard_map/ppermute | solution.py:427
  63.8 9.4 %collective-permute-start.18 = (bf16[1056,128]{1,0:T(8,128)(2,1)S(1)}, bf16[1056,128]{1,0:T(8,128)(2,1)S(1)}, u32[]{:S(2)}, u32[]{:S(2)}) collective-permute-start(bf16[1056,128]{1,0:T(8,128)(2,1)S(1)} %collective-permute-done.14.rest_9_), channel_id=1, source_target_pairs={{2,0},{4,2},{6,4},{7,6},{5,7},{3,5},{1,3},{0,1},{10,8},{12,10},{14... | collective-permute-start | bytes 811016 | tf_op jit(solution)/shard_map/ppermute | solution.py:428
  64.5 14.3 %collective-permute-start.22 = (bf16[1024,128]{1,0:T(8,128)(2,1)S(1)}, bf16[1024,128]{1,0:T(8,128)(2,1)S(1)}, u32[]{:S(2)}, u32[]{:S(2)}) collective-permute-start(bf16[1024,128]{1,0:T(8,128)(2,1)S(1)} %collective-permute-done.16.rest_6_), channel_id=1, source_target_pairs={{2,0},{4,2},{6,4},{7,6},{5,7},{3,5},{1,3},{0,1},{10,8},{12,10},{14... | collective-permute-start | bytes 786440 | tf_op jit(solution)/shard_map/ppermute | solution.py:428
  67.0 11.8 %collective-permute-start.21 = (bf16[1024,128]{1,0:T(8,128)(2,1)S(1)}, bf16[1024,128]{1,0:T(8,128)(2,1)S(1)}, u32[]{:S(2)}, u32[]{:S(2)}) collective-permute-start(bf16[1024,128]{1,0:T(8,128)(2,1)S(1)} %collective-permute-done.19.rest_3_), channel_id=1, source_target_pairs={{0,2},{2,4},{4,6},{6,7},{7,5},{5,3},{3,1},{1,0},{8,10},{10,12},{12... | collective-permute-start | bytes 786440 | tf_op jit(solution)/shard_map/ppermute | solution.py:421
  74.0 10.1 %collective-permute-start.23 = (bf16[1056,128]{1,0:T(8,128)(2,1)S(1)}, bf16[1056,128]{1,0:T(8,128)(2,1)S(1)}, u32[]{:S(2)}, u32[]{:S(2)}) collective-permute-start(bf16[1056,128]{1,0:T(8,128)(2,1)S(1)} %collective-permute-done.17.rest_4_), channel_id=1, source_target_pairs={{0,2},{2,4},{4,6},{6,7},{7,5},{5,3},{3,1},{1,0},{8,10},{10,12},{12... | collective-permute-start | bytes 811016 | tf_op jit(solution)/shard_map/ppermute | solution.py:427
  82.1 21.9 %collective-permute-start.27 = (bf16[256,512]{1,0:T(8,128)(2,1)S(1)}, bf16[256,512]{1,0:T(8,128)(2,1)S(1)}, u32[]{:S(2)}, u32[]{:S(2)}) collective-permute-start(bf16[256,512]{1,0:T(8,128)(2,1)S(1)} %out_projection.2.rest_4_.rest_3_), channel_id=1, source_target_pairs={{0,2},{2,4},{4,6},{6,7},{7,5},{5,3},{3,1},{1,0},{8,10},{10,12},{12... | collective-permute-start | bytes 786440 | tf_op jit(solution)/shard_map/ppermute | solution.py:427
  84.2 19.8 %collective-permute-start.28 = (bf16[256,512]{1,0:T(8,128)(2,1)S(1)}, bf16[256,512]{1,0:T(8,128)(2,1)S(1)}, u32[]{:S(2)}, u32[]{:S(2)}) collective-permute-start(bf16[256,512]{1,0:T(8,128)(2,1)S(1)} %out_projection.2.rest_4_.rest_3_), channel_id=1, source_target_pairs={{2,0},{4,2},{6,4},{7,6},{5,7},{3,5},{1,3},{0,1},{10,8},{12,10},{14... | collective-permute-start | bytes 786440 | tf_op jit(solution)/shard_map/ppermute | solution.py:428
  95.3 10.8 %collective-permute-start.25 = (bf16[272,512]{1,0:T(8,128)(2,1)S(1)}, bf16[272,512]{1,0:T(8,128)(2,1)S(1)}, u32[]{:S(2)}, u32[]{:S(2)}) collective-permute-start(bf16[272,512]{1,0:T(8,128)(2,1)S(1)} %get-tuple-element.151.rest_5_.rest_3_), channel_id=1, source_target_pairs={{0,2},{2,4},{4,6},{6,7},{7,5},{5,3},{3,1},{1,0},{8,10},{10,12},{12... | collective-permute-start | bytes 835592 | tf_op jit(solution)/shard_map/ppermute | solution.py:427
  104.0 11.8 %collective-permute-start.31 = (bf16[256,512]{1,0:T(8,128)(2,1)S(1)}, bf16[256,512]{1,0:T(8,128)(2,1)S(1)}, u32[]{:S(2)}, u32[]{:S(2)}) collective-permute-start(bf16[256,512]{1,0:T(8,128)(2,1)S(1)} %collective-permute-done.27.rest_5_), channel_id=1, source_target_pairs={{0,2},{2,4},{4,6},{6,7},{7,5},{5,3},{3,1},{1,0},{8,10},{10,12},{12... | collective-permute-start | bytes 786440 | tf_op jit(solution)/shard_map/ppermute | solution.py:427
  105.8 10.1 %collective-permute-start.32 = (bf16[256,512]{1,0:T(8,128)(2,1)S(1)}, bf16[256,512]{1,0:T(8,128)(2,1)S(1)}, u32[]{:S(2)}, u32[]{:S(2)}) collective-permute-start(bf16[256,512]{1,0:T(8,128)(2,1)S(1)} %collective-permute-done.28.rest_7_), channel_id=1, source_target_pairs={{2,0},{4,2},{6,4},{7,6},{5,7},{3,5},{1,3},{0,1},{10,8},{12,10},{14... | collective-permute-start | bytes 786440 | tf_op jit(solution)/shard_map/ppermute | solution.py:428
  106.1 11.6 %collective-permute-start.29 = (bf16[272,512]{1,0:T(8,128)(2,1)S(1)}, bf16[272,512]{1,0:T(8,128)(2,1)S(1)}, u32[]{:S(2)}, u32[]{:S(2)}) collective-permute-start(bf16[272,512]{1,0:T(8,128)(2,1)S(1)} %collective-permute-done.25.rest_6_), channel_id=1, source_target_pairs={{0,2},{2,4},{4,6},{6,7},{7,5},{5,3},{3,1},{1,0},{8,10},{10,12},{12... | collective-permute-start | bytes 835592 | tf_op jit(solution)/shard_map/ppermute | solution.py:427
  107.8 10.0 %collective-permute-start.30 = (bf16[272,512]{1,0:T(8,128)(2,1)S(1)}, bf16[272,512]{1,0:T(8,128)(2,1)S(1)}, u32[]{:S(2)}, u32[]{:S(2)}) collective-permute-start(bf16[272,512]{1,0:T(8,128)(2,1)S(1)} %collective-permute-done.26.rest_8_), channel_id=1, source_target_pairs={{2,0},{4,2},{6,4},{7,6},{5,7},{3,5},{1,3},{0,1},{10,8},{12,10},{14... | collective-permute-start | bytes 835592 | tf_op jit(solution)/shard_map/ppermute | solution.py:428
  115.9 10.7 %collective-permute-start.34 = (bf16[256,512]{1,0:T(8,128)(2,1)S(1)}, bf16[256,512]{1,0:T(8,128)(2,1)S(1)}, u32[]{:S(2)}, u32[]{:S(2)}) collective-permute-start(bf16[256,512]{1,0:T(8,128)(2,1)S(1)} %collective-permute-done.31.rest_5_), channel_id=1, source_target_pairs={{0,2},{2,4},{4,6},{6,7},{7,5},{5,3},{3,1},{1,0},{8,10},{10,12},{12... | collective-permute-start | bytes 786440 | tf_op jit(solution)/shard_map/ppermute | solution.py:427
  117.8 10.6 %collective-permute-start.33 = (bf16[272,512]{1,0:T(8,128)(2,1)S(1)}, bf16[272,512]{1,0:T(8,128)(2,1)S(1)}, u32[]{:S(2)}, u32[]{:S(2)}) collective-permute-start(bf16[272,512]{1,0:T(8,128)(2,1)S(1)} %collective-permute-done.30.rest_8_), channel_id=1, source_target_pairs={{2,0},{4,2},{6,4},{7,6},{5,7},{3,5},{1,3},{0,1},{10,8},{12,10},{14... | collective-permute-start | bytes 835592 | tf_op jit(solution)/shard_map/ppermute | solution.py:428
  118.1 12.1 %collective-permute-start.35 = (bf16[272,512]{1,0:T(8,128)(2,1)S(1)}, bf16[272,512]{1,0:T(8,128)(2,1)S(1)}, u32[]{:S(2)}, u32[]{:S(2)}) collective-permute-start(bf16[272,512]{1,0:T(8,128)(2,1)S(1)} %collective-permute-done.29.rest_6_), channel_id=1, source_target_pairs={{0,2},{2,4},{4,6},{6,7},{7,5},{5,3},{3,1},{1,0},{8,10},{10,12},{12... | collective-permute-start | bytes 835592 | tf_op jit(solution)/shard_map/ppermute | solution.py:427
  119.9 10.3 %collective-permute-start.36 = (bf16[256,512]{1,0:T(8,128)(2,1)S(1)}, bf16[256,512]{1,0:T(8,128)(2,1)S(1)}, u32[]{:S(2)}, u32[]{:S(2)}) collective-permute-start(bf16[256,512]{1,0:T(8,128)(2,1)S(1)} %collective-permute-done.32.rest_7_), channel_id=1, source_target_pairs={{2,0},{4,2},{6,4},{7,6},{5,7},{3,5},{1,3},{0,1},{10,8},{12,10},{14... | collective-permute-start | bytes 786440 | tf_op jit(solution)/shard_map/ppermute | solution.py:428
  126.6 12.3 %collective-permute-start.37 = (bf16[256,512]{1,0:T(8,128)(2,1)S(1)}, bf16[256,512]{1,0:T(8,128)(2,1)S(1)}, u32[]{:S(2)}, u32[]{:S(2)}) collective-permute-start(bf16[256,512]{1,0:T(8,128)(2,1)S(1)} %collective-permute-done.34.rest_5_), channel_id=1, source_target_pairs={{0,2},{2,4},{4,6},{6,7},{7,5},{5,3},{3,1},{1,0},{8,10},{10,12},{12... | collective-permute-start | bytes 786440 | tf_op jit(solution)/shard_map/ppermute | solution.py:421
  128.4 14.9 %collective-permute-start.38 = (bf16[272,512]{1,0:T(8,128)(2,1)S(1)}, bf16[272,512]{1,0:T(8,128)(2,1)S(1)}, u32[]{:S(2)}, u32[]{:S(2)}) collective-permute-start(bf16[272,512]{1,0:T(8,128)(2,1)S(1)} %collective-permute-done.33.rest_8_), channel_id=1, source_target_pairs={{2,0},{4,2},{6,4},{7,6},{5,7},{3,5},{1,3},{0,1},{10,8},{12,10},{14... | collective-permute-start | bytes 835592 | tf_op jit(solution)/shard_map/ppermute | solution.py:424
  146.5 9.6 %collective-permute-start.40 = (bf16[272,512]{1,0:T(8,128)(2,1)S(1)}, bf16[272,512]{1,0:T(8,128)(2,1)S(1)}, u32[]{:S(2)}, u32[]{:S(2)}) collective-permute-start(bf16[272,512]{1,0:T(8,128)(2,1)S(1)} %down_sum.11), channel_id=1, source_target_pairs={{2,0},{4,2},{6,4},{7,6},{5,7},{3,5},{1,3},{0,1},{10,8},{12,10},{14... | collective-permute-start | bytes 835592 | tf_op jit(solution)/shard_map/ppermute | solution.py:447
  151.2 9.2 %collective-permute-start.41 = (bf16[256,512]{1,0:T(8,128)(2,1)S(1)}, bf16[256,512]{1,0:T(8,128)(2,1)S(1)}, u32[]{:S(2)}, u32[]{:S(2)}) collective-permute-start(bf16[256,512]{1,0:T(8,128)(2,1)S(1)} %get-tuple-element.197), channel_id=1, source_target_pairs={{0,2},{2,4},{4,6},{6,7},{7,5},{5,3},{3,1},{1,0},{8,10},{10,12},{12... | collective-permute-start | bytes 786440 | tf_op jit(solution)/shard_map/ppermute | solution.py:451
  153.7 9.1 %collective-permute-start.42 = (bf16[256,512]{1,0:T(8,128)(2,1)S(1)}, bf16[256,512]{1,0:T(8,128)(2,1)S(1)}, u32[]{:S(2)}, u32[]{:S(2)}) collective-permute-start(bf16[256,512]{1,0:T(8,128)(2,1)S(1)} %get-tuple-element.203), channel_id=1, source_target_pairs={{2,0},{4,2},{6,4},{7,6},{5,7},{3,5},{1,3},{0,1},{10,8},{12,10},{14... | collective-permute-start | bytes 786440 | tf_op jit(solution)/shard_map/ppermute | solution.py:451
  157.9 10.9 %collective-permute-start.44 = (bf16[272,512]{1,0:T(8,128)(2,1)S(1)}, bf16[272,512]{1,0:T(8,128)(2,1)S(1)}, u32[]{:S(2)}, u32[]{:S(2)}) collective-permute-start(bf16[272,512]{1,0:T(8,128)(2,1)S(1)} %get-tuple-element.206), channel_id=1, source_target_pairs={{2,0},{4,2},{6,4},{7,6},{5,7},{3,5},{1,3},{0,1},{10,8},{12,10},{14... | collective-permute-start | bytes 835592 | tf_op jit(solution)/shard_map/ppermute | solution.py:451
  164.6 9.5 %collective-permute-start.46 = (bf16[256,512]{1,0:T(8,128)(2,1)S(1)}, bf16[256,512]{1,0:T(8,128)(2,1)S(1)}, u32[]{:S(2)}, u32[]{:S(2)}) collective-permute-start(bf16[256,512]{1,0:T(8,128)(2,1)S(1)} %get-tuple-element.211), channel_id=1, source_target_pairs={{2,0},{4,2},{6,4},{7,6},{5,7},{3,5},{1,3},{0,1},{10,8},{12,10},{14... | collective-permute-start | bytes 786440 | tf_op jit(solution)/shard_map/ppermute | solution.py:451
  (40 other events, 493.4 us)

commit v4 on v3

--- a/solution.py
+++ b/solution.py
@@ -50,38 +50,33 @@
     return out
 
 
-def pack_kernel(kv_ref, ask_ref, out_ref):
-    rows, width = kv_ref.shape
-    for i in range(width // HD):
-        out_ref[i * rows : (i + 1) * rows, :] = kv_ref[:, i * HD : (i + 1) * HD]
+def in_hbm(x):
+    return pltpu.with_memory_space_constraint(x, pltpu.HBM)
+
+
+def pack_kernel(kv_ref, ask_ref, keys_ref, values_ref):
+    rows = kv_ref.shape[0]
+    for i in range(KVH):
+        keys_ref[i * rows : (i + 1) * rows, :] = kv_ref[:, i * HD : (i + 1) * HD]
+        values_ref[i * rows : (i + 1) * rows, :] = kv_ref[:, WIDTH + i * HD : WIDTH + (i + 1) * HD]
     ask = ask_ref[...].astype(F32)
     heads = jnp.concatenate([ask[:, i * HD : (i + 1) * HD] for i in range(H)], axis=0)
-    out_ref[rows * (width // HD) :, :] = heads.astype(BF16)
+    keys_ref[KVH * rows :, :] = heads.astype(BF16)
 
 
 def pack(kv, ask):
-    rows, count = kv.shape[0], kv.shape[1] // HD
+    rows = kv.shape[0]
     return pl.pallas_call(
         pack_kernel,
-        out_shape=jax.ShapeDtypeStruct((count * rows + H, HD), BF16),
+        out_shape=[
+            jax.ShapeDtypeStruct((KVH * rows + H, HD), BF16),
+            jax.ShapeDtypeStruct((KVH * rows, HD), BF16),
+        ],
         in_specs=[VMEM, VMEM],
-        out_specs=VMEM,
+        out_specs=[VMEM, VMEM],
         cost_estimate=STEP,
         name="pack_keys",
     )(kv, ask)
-
-
-def pieces(parts, rows):
-    half = len(parts) // 2
-    out = []
-    for i, part in enumerate(parts):
-        if i == half:
-            out.append((half, part, 0, range(KVH)))
-        elif i == half + 1:
-            out.append((half, part, -KVH * rows, range(KVH, 2 * KVH)))
-        else:
-            out.append((i if i < half else i - 1, part, 0, range(2 * KVH)))
-    return out
 
 
 def attention_kernel(count, first, rows, owners, q_in, seg_ref, *rest):
@@ -89,10 +84,10 @@
     total = kv.shape[1]
     local = q_in.shape[0]
     moving = copies([(q_in.at[pl.ds(first, rows)], q)], sems)
-    for d, part, offset, heads in pieces(parts, local):
-        at = pl.ds(pl.multiple_of(owners[d] * local, 16), local)
-        for i in heads:
-            kv[i, at, :] = part[offset + i * local : offset + (i + 1) * local, :]
+    for j, part in enumerate(parts):
+        at = pl.ds(pl.multiple_of(owners[j % (count // 2)] * local, 16), local)
+        for i in range(KVH):
+            kv[j // (count // 2) * KVH + i, at, :] = part[i * local : (i + 1) * local, :]
     key_pos = lax.broadcasted_iota(jnp.int32, (rows, total), 1)
     query_pos = lax.broadcasted_iota(jnp.int32, (rows, total), 0) + (owners[0] * local + first)
     span = jnp.broadcast_to(seg_ref[...], (rows, total)).astype(F32)
@@ -126,33 +121,31 @@
             pltpu.VMEM((rows, D), BF16),
             pltpu.SemaphoreType.DMA((1,)),
         ],
-        compiler_params=params(40),
+        compiler_params=params(16),
         cost_estimate=STEP,
         name="prefill_attention",
     )(owners, q, seg, *parts, *dec)
 
 
 def pick_kernel(n, groups, owners, slots, *rest):
-    parts, outs = rest[: n + 1], rest[n + 1 :]
+    parts, outs = rest[:n], rest[n:]
     tok, grp = owners[0], owners[n]
     for j in range(groups):
         request = slots[(grp ^ j) * n + tok]
-        for i, part in enumerate(parts):
-            if i != n // 2:
-                d = i if i < n // 2 else i - 1
-
-                @pl.when(owners[d] == request % n)
-                def _(part=part, out=outs[j]):
-                    out[...] = part[part.shape[0] - H :, :]
+        for d, part in enumerate(parts):
+
+            @pl.when(owners[d] == request % n)
+            def _(part=part, out=outs[j]):
+                out[...] = part[part.shape[0] - H :, :]
 
 
 def pick(n, groups, owners, slots, parts):
     return pl.pallas_call(
         functools.partial(pick_kernel, n, groups),
         out_shape=[jax.ShapeDtypeStruct((H, HD), BF16) for _ in range(groups)],
-        in_specs=[SMEM, SMEM] + [VMEM] * (n + 1),
+        in_specs=[SMEM, SMEM] + [VMEM] * n,
         out_specs=[VMEM] * groups,
-        compiler_params=params(40),
+        compiler_params=params(16),
         cost_estimate=STEP,
         name="pick_queries",
     )(owners, slots, *parts)
@@ -196,7 +189,7 @@
         in_specs=[SMEM, SMEM, SMEM, HBM] + [VMEM] * groups,
         out_specs=VMEM,
         scratch_shapes=[pltpu.VMEM(cache.shape, BF16), pltpu.SemaphoreType.DMA((1,))],
-        compiler_params=params(40),
+        compiler_params=params(16),
         cost_estimate=STEP,
         name="decode_attention",
     )(owners, slots, length, cache, *choices)
@@ -207,10 +200,13 @@
         self.shares, self.blocks = tuple(shares), tuple(blocks)
 
     def shapes(self, cols, wide):
-        out = [jax.ShapeDtypeStruct((len(self.shares) * cols, wide), BF16)] * 2 if self.shares else []
-        return out + [jax.ShapeDtypeStruct((wide, cols), BF16) for _ in self.blocks]
+        out = [pltpu.VMEM((cols, wide), BF16)] * (2 * len(self.shares))
+        return out + [pltpu.VMEM((wide, cols), BF16) for _ in self.blocks]
 
     def count(self):
+        return 2 * len(self.shares) + len(self.blocks)
+
+    def outs(self):
         return 2 * len(self.shares) + len(self.blocks)
 
     def ins(self):
@@ -220,23 +216,41 @@
         pairs = []
         if self.shares:
             gate, up = weights[:2]
-            cols = outs[0].shape[0] // len(self.shares)
-            for i, share in enumerate(self.shares):
+            cols = outs[0].shape[0]
+            for share in self.shares:
                 at = pl.ds(pl.multiple_of(owners[share] * cols, cols), cols)
-                to = pl.ds(i * cols, cols)
-                pairs += [(gate.at[at], outs[0].at[to]), (up.at[at], outs[1].at[to])]
-            outs = outs[2:]
+                pairs += [(gate.at[at], outs[0]), (up.at[at], outs[1])]
+                outs = outs[2:]
         for block, out in zip(self.blocks, outs):
             cols = out.shape[1]
             pairs.append((weights[2].at[:, pl.ds(pl.multiple_of(owners[block] * cols, HD), cols)], out))
         return copies(pairs, sems)
 
 
-def project_kernel(n, rows, fetch, owners, *rest):
-    weights, rest = rest[: fetch.ins()], rest[fetch.ins() :]
-    parts, (wo_ref, resid_ref, out_ref) = rest[:n], rest[n : n + 3]
-    x, dec, sems = rest[-3:]
-    moving = fetch.start(owners, weights, rest[n + 3 : -3], sems)
+def fetch_kernel(fetch, owners, *rest):
+    for c in fetch.start(owners, rest[: fetch.ins()], rest[fetch.ins() : -1], rest[-1]):
+        c.wait()
+
+
+def fetch_early(fetch, owners, weights, cols, wide):
+    shapes = fetch.shapes(cols, wide)
+    return pl.pallas_call(
+        functools.partial(fetch_kernel, fetch),
+        out_shape=shapes,
+        in_specs=[SMEM] + [HBM] * fetch.ins(),
+        out_specs=[VMEM] * len(shapes),
+        scratch_shapes=[pltpu.SemaphoreType.DMA((fetch.count(),))],
+        compiler_params=params(16),
+        cost_estimate=STEP,
+        name="fetch_weights",
+    )(owners, *[in_hbm(x) for x in weights[: fetch.ins()]])
+
+
+def project_kernel(n, rows, first, owners, *rest):
+    parts, (wo_ref, resid_ref, out_ref, x, dec, resid) = rest[:n], rest[n:]
+    resid[...] = resid_ref[...].astype(F32)
+    local = resid.shape[0] // n
+    wide = [resid[b * local + first : b * local + first + rows, :] for b in range(n)]
     for d, part in enumerate(parts):
         at = pl.ds(pl.multiple_of(owners[d] * rows, 16), rows)
         for i in range(H):
@@ -251,30 +265,30 @@
         heads = jnp.dot(chosen, dec[...], preferred_element_type=F32).astype(BF16)
         for i in range(H):
             x[n * rows :, i * HD : (i + 1) * HD] = heads[i * spare : (i + 1) * spare]
+        wide += [resid[(b + 1) * local - 1 : (b + 1) * local, :] for b in range(n)]
+        if spare > n:
+            wide.append(jnp.zeros((spare - n, resid.shape[1]), F32))
     total = jnp.dot(x[...], wo_ref[...], preferred_element_type=F32)
-    out_ref[...] = (resid_ref[...].astype(F32) + total).astype(BF16)
-    for c in moving:
-        c.wait()
-
-
-def project(rows, owners, parts, wo, resid, fetch, weights):
-    m, cols = resid.shape
+    out_ref[...] = (jnp.concatenate(wide, axis=0) + total).astype(BF16)
+
+
+def project(rows, spare, first, owners, parts, wo, resid):
     n = len(parts)
-    fetched = fetch.shapes(cols, weights[0].shape[1])
-    return pl.pallas_call(
-        functools.partial(project_kernel, n, rows, fetch),
-        out_shape=[jax.ShapeDtypeStruct((m, cols), BF16)] + fetched,
-        in_specs=[SMEM] + [HBM] * fetch.ins() + [VMEM] * (n + 2),
-        out_specs=[VMEM] * (1 + len(fetched)),
+    m, cols = n * rows + spare, wo.shape[1]
+    return pl.pallas_call(
+        functools.partial(project_kernel, n, rows, first),
+        out_shape=jax.ShapeDtypeStruct((m, cols), BF16),
+        in_specs=[SMEM] + [VMEM] * (n + 2),
+        out_specs=VMEM,
         scratch_shapes=[
             pltpu.VMEM((m, D), BF16),
             pltpu.VMEM((n * H, HD), BF16),
-            pltpu.SemaphoreType.DMA((max(fetch.count(), 1),)),
+            pltpu.VMEM(resid.shape, F32),
         ],
-        compiler_params=params(42),
+        compiler_params=params(16),
         cost_estimate=STEP,
         name="out_projection",
-    )(owners, *weights[: fetch.ins()], *parts, wo, resid)
+    )(owners, *parts, wo, resid)
 
 
 def scale_in(x, squares, tenants, gain_ref, at):
@@ -286,50 +300,52 @@
     return squares, (x * gain).astype(BF16)
 
 
-def feed_kernel(shares, taken, fetch, owners, tenants_ref, gain_ref, *rest):
+def feed_kernel(lo, hi, shares, taken, fetch, owners, tenants_ref, gain_ref, *rest):
     weights, rest = rest[: fetch.ins()], rest[fetch.ins() :]
-    w_refs, rest = rest[:2], rest[2:]
-    parts, rest = rest[: 2 * len(shares)], rest[2 * len(shares) :]
+    w_refs, rest = rest[: 2 * len(shares)], rest[2 * len(shares) :]
+    chunks = (len(rest) - 5 - fetch.outs() - 3 * taken) // len(shares)
+    parts, rest = rest[: chunks * len(shares)], rest[chunks * len(shares) :]
     held, rest = (rest[:3], rest[3:]) if taken else (None, rest)
     (gates, lifts, squares), fetched, (scaled, sems) = rest[:3], rest[3:-2], rest[-2:]
     moving = fetch.start(owners, weights, fetched, sems)
-    m = gates.shape[0]
     cols = parts[0].shape[1]
-    tenants = tenants_ref[...]
-    total = held[2][...] if taken else jnp.zeros((m, HD), F32)
+    tenants = tenants_ref[lo:hi, :]
+    total = held[2][lo:hi, :] if taken else jnp.zeros((hi - lo, HD), F32)
     for i, share in enumerate(shares):
-        x = jnp.concatenate([p[...] for p in parts[2 * i : 2 * i + 2]], axis=0).astype(F32)
+        x = jnp.concatenate([p[...] for p in parts[chunks * i : chunks * (i + 1)]], axis=0).astype(F32)
         at = pl.ds(pl.multiple_of(owners[share] * cols, HD), cols)
         total, x = scale_in(x, total, tenants, gain_ref, at)
         scaled[:, i * cols : (i + 1) * cols] = x
-    squares[...] = total
+    squares[lo:hi, :] = total
     for i, out in enumerate((gates, lifts)):
-        one = jnp.dot(scaled[...], w_refs[i][...], preferred_element_type=F32)
-        out[...] = held[i][...] + one if taken else one
+        one = jnp.dot(scaled[:, :cols], w_refs[i][...], preferred_element_type=F32)
+        if len(shares) > 1:
+            one = one + jnp.dot(scaled[:, cols:], w_refs[2 + i][...], preferred_element_type=F32)
+        out[lo:hi, :] = held[i][lo:hi, :] + one if taken else one
     for c in moving:
         c.wait()
 
 
-def feed(shares, owners, tenants, gain, weights, w, parts, held, fetch, grant):
-    m, (deep, wide) = tenants.shape[0], w[0].shape
+def feed(lo, hi, shares, owners, tenants, gain, weights, w, parts, held, fetch, grant):
+    m, wide = tenants.shape[0], w[0].shape[1]
     cols = parts[0].shape[1]
-    first = 5 + fetch.ins() + len(parts)
+    first = 3 + fetch.ins() + len(w) + len(parts)
     fetched = fetch.shapes(cols, wide)
     sums = [jax.ShapeDtypeStruct((m, wide), F32)] * 2 + [jax.ShapeDtypeStruct((m, HD), F32)]
     return pl.pallas_call(
-        functools.partial(feed_kernel, shares, len(held) > 0, fetch),
+        functools.partial(feed_kernel, lo, hi, shares, len(held) > 0, fetch),
         out_shape=sums + fetched,
-        in_specs=[SMEM, VMEM, VMEM] + [HBM] * fetch.ins() + [VMEM] * (2 + len(parts) + len(held)),
+        in_specs=[SMEM, VMEM, VMEM] + [HBM] * fetch.ins() + [VMEM] * (len(w) + len(parts) + len(held)),
         out_specs=[VMEM] * (3 + len(fetched)),
         scratch_shapes=[
-            pltpu.VMEM((m, deep), BF16),
-            pltpu.SemaphoreType.DMA((fetch.count(),)),
+            pltpu.VMEM((hi - lo, cols * len(shares)), BF16),
+            pltpu.SemaphoreType.DMA((max(fetch.count(), 1),)),
         ],
         input_output_aliases={first + i: i for i in range(len(held))},
-        compiler_params=params(grant),
+        compiler_params=params(16),
         cost_estimate=STEP,
         name="gate_up_sum",
-    )(owners, tenants, gain, *weights[: fetch.ins()], *w, *parts, *held)
+    )(owners, tenants, gain, *[in_hbm(x) for x in weights[: fetch.ins()]], *w, *parts, *held)
 
 
 def hidden_kernel(lo, hi, share, owners, tenants_ref, gain_ref, w_gate, w_up, part, gates, lifts, squares, out):
@@ -382,8 +398,8 @@
 
 
 class Chain:
-    def __init__(self, n, order, own, last, cut=0):
-        self.n, self.half, self.last, self.cut = n, n // 2, last, cut
+    def __init__(self, n, order, own, last):
+        self.n, self.half, self.last = n, n // 2, last
         self.fw = [(order[i], order[(i + 1) % n]) for i in range(n)]
         self.bw = [(b, a) for a, b in self.fw]
         self.own, self.ahead, self.behind, self.hops = own, [own], [own], 0
@@ -395,9 +411,41 @@
         return [self.own] + self.ahead[1:] + self.behind[:0:-1]
 
 
+def settle_kernel(*refs):
+    for i in range(len(refs) // 2):
+        refs[len(refs) // 2 + i][...] = refs[i][...]
+
+
+def settle(*arrays):
+    return pl.pallas_call(
+        settle_kernel,
+        out_shape=[jax.ShapeDtypeStruct(x.shape, x.dtype) for x in arrays],
+        in_specs=[VMEM] * len(arrays),
+        out_specs=[VMEM] * len(arrays),
+        cost_estimate=STEP,
+        name="settle",
+    )(*arrays)
+
+
+def tick_kernel(token, out):
+    out[...] = token[...]
+
+
+def tick(token):
+    return pl.pallas_call(
+        tick_kernel,
+        out_shape=jax.ShapeDtypeStruct(token.shape, token.dtype),
+        in_specs=[VMEM],
+        out_specs=VMEM,
+        cost_estimate=STEP,
+        name="tick",
+    )(token)
+
+
 class Order:
     def __init__(self, ids):
         self.ids, self.last = ids, ()
+        self.token = jnp.zeros((8, HD), F32)
 
     def after(self):
         return lax.optimization_barrier((self.ids, *self.last))[0]
@@ -406,24 +454,23 @@
         self.last = out
         return out[0]
 
+    def tick(self):
+        self.token = tick(lax.optimization_barrier((self.token, *self.last))[0])
+
     def tied(self, *arrays):
-        out = lax.optimization_barrier((*arrays, *self.last))[: len(arrays)]
-        self.last = (out[0],)
-        return out
+        out = lax.optimization_barrier((*arrays, self.token, *self.last))
+        self.last, self.token = (out[0],), out[len(arrays)]
+        return out[: len(arrays)]
 
     def hop(self, chain):
         chain.hops += 1
         f, b = chain.ahead[-1], chain.behind[-1]
-        if chain.done() and chain.last == "split":
-            f, b = f[: chain.cut], b[chain.cut :]
+        f, b = self.tied(f, b)
         if chain.done() and chain.last == "fw":
-            (f,) = self.tied(f)
             chain.ahead.append(lax.ppermute(f, "tok", chain.fw))
-        elif chain.done() and chain.last == "bw":
-            (b,) = self.tied(b)
+        elif chain.done():
             chain.behind.append(lax.ppermute(b, "tok", chain.bw))
         else:
-            f, b = self.tied(f, b)
             chain.ahead.append(lax.ppermute(f, "tok", chain.fw))
             chain.behind.append(lax.ppermute(b, "tok", chain.bw))
 
@@ -492,82 +539,101 @@
         tail = jnp.pad(a[:, local], ((0, spare - n), (0, 0)))
         return first, jnp.concatenate([second, tail], axis=0)
 
-    resids = split(resid)
     tenants = jnp.concatenate(split(tenant[0][:, None]), axis=0)
     run = Order(owners)
 
     def chain(own, last):
         return Chain(n, order, own, last)
 
-    keys = Chain(n, order, pack(pre_kv, dec_q), "split", KVH * local)
+    own_keys, own_values = pack(pre_kv, dec_q)
+    keys, values = chain(own_keys, "fw"), chain(own_values, "bw")
     run.hop(keys)
-    run.mark(*run.last, *resids, tenants, owners)
+    run.tick()
+    run.hop(values)
     while not keys.done():
+        run.tick()
         run.hop(keys)
-    kv = keys.parts()
-    a = chain(run.mark(attention(0, rows, run.after(), pre_q, pre_segment, kv)), "fw")
-    run.hop(a)
-    choices = list(pick(n, groups, run.after(), slot_request, kv))
+        run.tick()
+        run.hop(values)
+    choices = list(pick(n, groups, run.after(), slot_request, keys.parts()))
     run.mark(choices[0])
     for j in range(1, groups):
         (choices[j],) = run.tied(choices[j])
         choices[j] = lax.ppermute(choices[j], "grp", [(i, i ^ j) for i in range(groups)])
+    kv = keys.parts() + values.parts()
+    a = chain(run.mark(attention(0, rows, run.after(), pre_q, pre_segment, kv)), "fw")
     run.hop(a)
     dec = run.mark(decode(n, run.after(), slot_request, cache_len, choices, cache))
     b = chain(run.mark(attention(rows, rows, run.after(), pre_q, pre_segment, kv, (dec,))), "bw")
     run.hop(b)
+    run.hop(a)
+    tenants, gain = settle(tenants, norm_gain)
+    run.mark(*run.last, tenants)
+    run.hop(b)
+    weights = (w_gate, w_up, w_down)
+    wide = w_gate.shape[1]
+    far = [d for d in range(half - 1, half + 2)]
+    fetches = [Fetch([0]), Fetch([1]), Fetch([n - 1]), Fetch((), far)]
+    blocks, early = {}, {}
+
+    def fetch_some():
+        if fetches:
+            fetch = fetches.pop(0)
+            out = fetch_early(fetch, run.after(), weights, cols, wide)
+            run.mark(out[0])
+            blocks.update(zip(fetch.blocks, out))
+            early.update({share: out for share in fetch.shares})
+
     while not a.done():
         run.hop(a)
+        fetch_some()
         run.hop(b)
-
-    weights = (w_gate, w_up, w_down)
-    mixed_a = project(rows, run.after(), a.parts(), wo, resids[0], Fetch(), weights)[0]
-    run.mark(mixed_a)
+        fetch_some()
+    while fetches:
+        fetch_some()
+    mixed_a = run.mark(project(rows, 0, 0, run.after(), a.parts(), wo, resid))
     g = chain(mixed_a, "fw")
     run.hop(g)
-    while not b.done():
-        run.hop(b)
-        if not b.done():
-            run.hop(g)
-    mixed_b, *w = project(rows, run.after(), b.parts(), wo, resids[1], Fetch([0]), weights)
-    run.mark(mixed_b)
+    mixed_b = run.mark(project(rows, spare, rows, run.after(), b.parts(), wo, resid))
     h = chain(mixed_b, "bw")
     run.hop(h)
 
     m_a, m = mixed_a.shape[0], tenants.shape[0]
-    held, blocks = (), {}
-    for i in range(half):
-        shares = [i, n - i] if i else [0]
-        if i:
-            parts = [g.ahead[i], h.ahead[i], g.behind[i], h.behind[i]]
+    held = ()
+
+    def add(lo, hi, shares, parts, fetch, grant):
+        w = [x for share in shares for x in early[share]]
+        out = feed(lo, hi, shares, run.after(), tenants, gain, weights, w, parts, held, fetch, grant)
+        run.mark(out[2])
+        for i, share in enumerate(fetch.shares):
+            early[share] = out[3 + 2 * i : 5 + 2 * i]
+        blocks.update(zip(fetch.blocks, out[3 + 2 * len(fetch.shares) :]))
+        return out[:3]
+
+    def arrived(i):
+        return [g.ahead[i], h.ahead[i], g.behind[i], h.behind[i]]
+
+    held = add(0, m, [0], [mixed_a, mixed_b], Fetch([2, n - 2] if half > 2 else [half]), 24)
+    run.hop(g)
+    run.hop(h)
+    for i in range(1, half - 1):
+        if i == 1:
+            fetch = Fetch((), [half - 2, half + 2])
         else:
-            parts = [mixed_a, mixed_b]
-        later = [half] if i + 1 == half else [i + 1, n - i - 1]
-        early = []
-        if i == 1:
-            early = [half]
-        elif i > 1:
-            early = [half + 1 - i, n - half - 1 + i]
-        if i + 1 == half:
-            early += [d for d in range(n) if d not in early and d not in blocks]
-        grant = 30 if i == 0 else 20 if i + 1 == half else 24
-        out = feed(
-            shares, run.after(), tenants, norm_gain, weights, w, parts, held, Fetch(later, early), grant
-        )
-        held, w = out[:3], out[3:5]
-        blocks.update(zip(early, out[5:]))
-        run.mark(out[2])
-        if not g.done():
-            run.hop(g)
-        if not h.done():
-            run.hop(h)
+            fetch = Fetch([i + 1, n - i - 1])
+        held = add(0, m, [i, n - i], arrived(i), fetch, 24)
+        run.hop(g)
+        run.hop(h)
+    i = half - 1
+    held = add(0, m_a, [i, n - i], arrived(i)[::2], Fetch([half], [d for d in range(1, n) if d not in blocks]), 16)
 
     def finish(lo, hi, part):
-        return run.mark(hide(lo, hi, half, run.after(), tenants, norm_gain, w, part, held))
+        return run.mark(hide(lo, hi, half, run.after(), tenants, gain, early[half], part, held))
 
     hid_a = finish(0, m_a, g.ahead[half])
     sum_a = Sum(run, g, hid_a, blocks, mixed_a)
     sum_a.hop()
+    held = add(m_a, m, [i, n - i], arrived(i)[1::2], Fetch((), [0]), 16)
     hid_b = finish(m_a, m, h.behind[half])
     sum_b = Sum(run, h, hid_b, blocks, mixed_b)
     sum_b.hop()

time: 189 us -> 182 us (0.963)
  waiting for transfers between devices: 63.6 us -> 44.8 us
  Pallas kernels: 60.9 us -> 71.4 us
  starting transfers between devices: 53.7 us -> 60.5 us
  local copies, waits for them, and re-layouts: 7.42 us -> 3.28 us
    ppermute x18 -> x21, waiting for transfers between devices: 24.1 us -> 11 us  [hop(): chain.ahead.append(lax.ppermute(f, 'tok', chain.fw))]
    pallas_call x7 -> x13, Pallas kernels: 34.9 us -> 45.4 us  [the longest x5 26.9 us: feed(): pl.pallas_call(functools.partial(feed_kernel, lo, hi, shares, len(held) >...]
    ppermute x18 -> x21, waiting for transfers between devices: 24.1 us -> 16 us  [hop(): chain.behind.append(lax.ppermute(b, 'tok', chain.bw))]
    ppermute x6, starting transfers between devices: 8.81 us -> 2.24 us  [hop(): lax.ppermute(out[1], 'tok', chain.bw)]
    ppermute x6, starting transfers between devices: 4.11 us -> 10.4 us  [hop(): lax.ppermute(out[0], 'tok', chain.fw)]
    ppermute x18 -> x21, starting transfers between devices: 5.63 us -> 10.9 us  [hop(): chain.behind.append(lax.ppermute(b, 'tok', chain.bw))]
    ppermute x6, waiting for transfers between devices: 7.07 us -> 10.4 us  [hop(): lax.ppermute(out[1], 'tok', chain.bw)]
    ppermute x18 -> x21, starting transfers between devices: 30.9 us -> 32.7 us  [hop(): chain.ahead.append(lax.ppermute(f, 'tok', chain.fw))]
  transfers between devices with their start and end apart: 53 -> 59, of which waited for: 30 -> 31; matrix products, arithmetic and copies ran while one was open for 3% -> 1% of each run, Pallas kernels for 29% -> 38%
where the time goes in v4:
time: 182 us; the launch traced here: 181 us
  Pallas kernels  71.4 us (39%)
  starting transfers between devices  60.5 us (33%)
  waiting for transfers between devices  44.8 us (25%)
  local copies, waits for them, and re-layouts  3.28 us (2%)
    ppermute x21, starting transfers between devices, hop(): chain.ahead.append(lax.ppermute(f, 'tok', chain.fw))  32.7 us
    pallas_call x5, Pallas kernels, feed(): pl.pallas_call(functools.partial(feed_kernel, lo, hi, shares, len(held) >...  26.9 us
    ppermute x21, waiting for transfers between devices, hop(): chain.behind.append(lax.ppermute(b, 'tok', chain.bw))  16 us
    pallas_call x10, Pallas kernels, down(): pl.pallas_call(functools.partial(down_kernel, flags, len(own)), out_shape...  13.8 us
    ppermute x21, waiting for transfers between devices, hop(): chain.ahead.append(lax.ppermute(f, 'tok', chain.fw))  11 us
    ppermute x21, starting transfers between devices, hop(): chain.behind.append(lax.ppermute(b, 'tok', chain.bw))  10.9 us
    pallas_call x4, Pallas kernels, fetch_early(): pl.pallas_call(functools.partial(fetch_kernel, fetch), out_shape=shapes,...  10.5 us
    ppermute x6, waiting for transfers between devices, hop(): lax.ppermute(out[1], 'tok', chain.bw)  10.4 us
  transfers between devices with their start and end apart: 59, of which 31 were waited for; matrix products, arithmetic and copies ran while one was open for 1% of the time, Pallas kernels for 38%

profile of v4, /device:TPU:0, one launch (start us, length us, event | category | flops | bytes accessed | tf_op | source)
XLA Modules:
  0.0 181.3 jit_solution(8959729433476472905)
XLA Ops:
  1.8 3.0 %collective-permute-start = (bf16[544,128]{1,0:T(8,128)(2,1)}, bf16[544,128]{1,0:T(8,128)(2,1)S(1)}, u32[]{:S(2)}, u32[]{:S(2)}) collective-permute-start(bf16[544,128]{1,0:T(8,128)(2,1)} %get-tuple-element.166.rest_0_), channel_id=1, source_target_pairs={{0,2},{2,4},{4,6},{6,7},{7,5},{5,3},{3,1},{1,0},{8,10},{10,12},{12... | collective-permute-start | bytes 417800 | tf_op jit(solution)/shard_map/ppermute | solution.py:474
  4.8 2.0 %collective-permute-start.4 = (bf16[512,128]{1,0:T(8,128)(2,1)}, bf16[512,128]{1,0:T(8,128)(2,1)S(1)}, u32[]{:S(2)}, u32[]{:S(2)}) collective-permute-start(bf16[512,128]{1,0:T(8,128)(2,1)} %get-tuple-element.175.rest_8_), channel_id=1, source_target_pairs={{0,2},{2,4},{4,6},{6,7},{7,5},{5,3},{3,1},{1,0},{8,10},{10,12},{12... | collective-permute-start | bytes 393224 | tf_op jit(solution)/shard_map/ppermute | solution.py:474
  6.8 2.6 %collective-permute-done.rest_1_ = bf16[544,128]{1,0:T(8,128)(2,1)S(1)} collective-permute-done((bf16[544,128]{1,0:T(8,128)(2,1)}, bf16[544,128]{1,0:T(8,128)(2,1)S(1)}, u32[]{:S(2)}, u32[]{:S(2)}) %collective-permute-start) | collective-permute-done | bytes 139296 | tf_op jit(solution)/shard_map/ppermute | solution.py:474
  9.4 2.1 %collective-permute-done.1.rest_7_ = bf16[544,128]{1,0:T(8,128)(2,1)S(1)} collective-permute-done((bf16[544,128]{1,0:T(8,128)(2,1)}, bf16[544,128]{1,0:T(8,128)(2,1)S(1)}, u32[]{:S(2)}, u32[]{:S(2)}) %collective-permute-start.1) | collective-permute-done | bytes 139296 | tf_op jit(solution)/shard_map/ppermute | solution.py:475
  33.9 3.0 %prefill_attention.2.rest_0_ = bf16[1024,128]{1,0:T(8,128)(2,1)S(1)} custom-call(s32[9]{0:T(128)S(1)} %pad_add_fusion.1.owners, bf16[64,4096]{1,0:T(8,128)(2,1)S(1)} %copy-done.5, s32[1,512]{1,0:T(1,128)S(1)} %copy-done.9, bf16[544,128]{1,0:T(8,128)(2,1)S(1)} %copy-done.6, bf16[544,128]{1,0:T(8,128)(2,1)S(1)} %collective-permute-done.rest_1_, ...), custom_call_target="tpu_custom_call" | custom-call | flops 500000000 | bytes 1000000 | tf_op jit(solution)/shard_map/prefill_attention/pallas_call | solution.py:114
  40.6 3.0 %prefill_attention.3.rest_0_ = bf16[1056,128]{1,0:T(8,128)(2,1)S(1)} custom-call(s32[9]{0:T(128)S(1)} %pad_add_fusion.1.owners, bf16[64,4096]{1,0:T(8,128)(2,1)S(1)} %copy-done.5, s32[1,512]{1,0:T(1,128)S(1)} %copy-done.9, bf16[544,128]{1,0:T(8,128)(2,1)S(1)} %copy-done.7, bf16[544,128]{1,0:T(8,128)(2,1)S(1)} %collective-permute-done.rest_1_, ...), custom_call_target="tpu_custom_call" | custom-call | flops 500000000 | bytes 1000000 | tf_op jit(solution)/shard_map/prefill_attention/pallas_call | solution.py:114
  56.6 2.0 %collective-permute-done.19.rest_2_ = bf16[1024,128]{1,0:T(8,128)(2,1)S(1)} collective-permute-done((bf16[1024,128]{1,0:T(8,128)(2,1)S(1)}, bf16[1024,128]{1,0:T(8,128)(2,1)S(1)}, u32[]{:S(2)}, u32[]{:S(2)}) %collective-permute-start.19) | collective-permute-done | bytes 262176 | tf_op jit(solution)/shard_map/ppermute | solution.py:474
  62.2 2.4 %fetch_weights.5 = (bf16[512,1536]{1,0:T(8,128)(2,1)S(1)}, bf16[512,1536]{1,0:T(8,128)(2,1)S(1)}) custom-call(s32[9]{0:T(128)S(1)} %pad_add_fusion.1.owners, bf16[4096,1536]{1,0:T(8,128)(2,1)} %rest_0_.17, bf16[4096,1536]{1,0:T(8,128)(2,1)} %rest_1_.17), custom_call_target="tpu_custom_call" | custom-call | flops 500000000 | bytes 1000000 | tf_op jit(solution)/shard_map/fetch_weights/pallas_call | solution.py:237
  68.0 2.4 %fetch_weights.6 = (bf16[512,1536]{1,0:T(8,128)(2,1)S(1)}, bf16[512,1536]{1,0:T(8,128)(2,1)S(1)}) custom-call(s32[9]{0:T(128)S(1)} %pad_add_fusion.1.owners, bf16[4096,1536]{1,0:T(8,128)(2,1)} %rest_0_.17, bf16[4096,1536]{1,0:T(8,128)(2,1)} %rest_1_.17), custom_call_target="tpu_custom_call" | custom-call | flops 500000000 | bytes 1000000 | tf_op jit(solution)/shard_map/fetch_weights/pallas_call | solution.py:237
  72.9 2.4 %fetch_weights.7 = (bf16[512,1536]{1,0:T(8,128)(2,1)S(1)}, bf16[512,1536]{1,0:T(8,128)(2,1)S(1)}) custom-call(s32[9]{0:T(128)S(1)} %pad_add_fusion.1.owners, bf16[4096,1536]{1,0:T(8,128)(2,1)} %rest_0_.17, bf16[4096,1536]{1,0:T(8,128)(2,1)} %rest_1_.17), custom_call_target="tpu_custom_call" | custom-call | flops 500000000 | bytes 1000000 | tf_op jit(solution)/shard_map/fetch_weights/pallas_call | solution.py:237
  76.4 3.2 %fetch_weights.4 = (bf16[1536,512]{1,0:T(8,128)(2,1)S(1)}, bf16[1536,512]{1,0:T(8,128)(2,1)S(1)}, bf16[1536,512]{1,0:T(8,128)(2,1)S(1)}) custom-call(s32[9]{0:T(128)S(1)} %pad_add_fusion.1.owners, bf16[4096,1536]{1,0:T(8,128)(2,1)} %rest_0_.17, bf16[4096,1536]{1,0:T(8,128)(2,1)} %rest_1_.17, bf16[1536,4096]{1,0:T(8,128)(2,1)} %rest_2_.7), custom_call_target="tpu_custom_call" | custom-call | flops 500000000 | bytes 1000000 | tf_op jit(solution)/shard_map/fetch_weights/pallas_call | solution.py:237
  80.2 2.2 %out_projection.2.rest_4_.rest_3_ = bf16[256,512]{1,0:T(8,128)(2,1)S(1)} custom-call(s32[9]{0:T(128)S(1)} %pad_add_fusion.1.owners, bf16[1024,128]{1,0:T(8,128)(2,1)S(1)} %prefill_attention.2.rest_0_, bf16[1024,128]{1,0:T(8,128)(2,1)S(1)} %collective-permute-done.14.rest_1_, bf16[1024,128]{1,0:T(8,128)(2,1)S(1)} %collective-permute-done.19.rest_2_, ...), custom_call_target="tpu_custom_call" | custom-call | flops 500000000 | bytes 1000000 | tf_op jit(solution)/shard_map/out_projection/pallas_call | solution.py:278
  84.5 2.3 %out_projection.3.rest_5_.rest_3_ = bf16[272,512]{1,0:T(8,128)(2,1)S(1)} custom-call(s32[9]{0:T(128)S(1)} %pad_add_fusion.1.owners, bf16[1056,128]{1,0:T(8,128)(2,1)S(1)} %prefill_attention.3.rest_0_, bf16[1056,128]{1,0:T(8,128)(2,1)S(1)} %collective-permute-done.21.rest_1_, bf16[1056,128]{1,0:T(8,128)(2,1)S(1)} %collective-permute-done.25.rest_2_, ...), custom_call_target="tpu_custom_call" | custom-call | flops 500000000 | bytes 1000000 | tf_op jit(solution)/shard_map/out_projection/pallas_call | solution.py:278
  88.9 4.7 %gate_up_sum.5 = (f32[528,1536]{1,0:T(8,128)S(1)}, f32[528,1536]{1,0:T(8,128)S(1)}, f32[528,128]{1,0:T(8,128)S(1)}, bf16[512,1536]{1,0:T(8,128)(2,1)S(1)}, bf16[...) custom-call(s32[9]{0:T(128)S(1)} %pad_add_fusion.1.owners, ...), custom_call_target="tpu_custom_call" | custom-call | flops 500000000 | bytes 1000000 | tf_op jit(solution)/shard_map/gate_up_sum/pallas_call | solution.py:335
  100.2 6.5 %gate_up_sum.6 = (f32[528,1536]{1,0:T(8,128)S(1)}, f32[528,1536]{1,0:T(8,128)S(1)}, f32[528,128]{1,0:T(8,128)S(1)}, bf16[1536,512]{1,0:T(8,128)(2,1)S(1)}, bf16[1536,512]{1,0:T(8,128)(2,1)S(1)}) custom-call(s32[9]{0:T(128)S(1)} %pad_add_fusion.1.owners, s32[528,1]{1,0:T(8,128)S(1)} %copy-done.1, ...), custom_call_target="tpu_custom_call", output_to_operand_aliasing={{0}: (14, {}), {1}: (15, {}), {2}: (16, {})} | custom-call | flops 500000000 | bytes 1000000 | tf_op jit(solution)/shard_map/gate_up_sum/pallas_call | solution.py:335
  111.9 7.4 %gate_up_sum.7 = (f32[528,1536]{1,0:T(8,128)S(1)}, f32[528,1536]{1,0:T(8,128)S(1)}, f32[528,128]{1,0:T(8,128)S(1)}, bf16[512,1536]{1,0:T(8,128)(2,1)S(1)}, bf16[...) custom-call(s32[9]{0:T(128)S(1)} %pad_add_fusion.1.owners, ...), custom_call_target="tpu_custom_call", output_to_operand_aliasing={{0}: (13, {}), {1}: (14, {}), {2}: (15, {})} | custom-call | flops 500000000 | bytes 1000000 | tf_op jit(solution)/shard_map/gate_up_sum/pallas_call | solution.py:335
  121.4 5.3 %gate_up_sum.8 = (f32[528,1536]{1,0:T(8,128)S(1)}, f32[528,1536]{1,0:T(8,128)S(1)}, f32[528,128]{1,0:T(8,128)S(1)}, bf16[512,1536]{1,0:T(8,128)(2,1)S(1)}, bf16[...) custom-call(s32[9]{0:T(128)S(1)} %pad_add_fusion.1.owners, ...), custom_call_target="tpu_custom_call", output_to_operand_aliasing={{0}: (12, {}), {1}: (13, {}), {2}: (14, {})} | custom-call | flops 500000000 | bytes 1000000 | tf_op jit(solution)/shard_map/gate_up_sum/pallas_call | solution.py:335
  131.5 2.9 %gate_up_sum.9 = (f32[528,1536]{1,0:T(8,128)S(1)}, f32[528,1536]{1,0:T(8,128)S(1)}, f32[528,128]{1,0:T(8,128)S(1)}, bf16[1536,512]{1,0:T(8,128)(2,1)S(1)}) custom-call(s32[9]{0:T(128)S(1)} %pad_add_fusion.1.owners, s32[528,1]{1,0:T(8,128)S(1)} %copy-done.1, f32[4,4096]{1,0:T(4,128)S(1)} %copy-done.2, ...), custom_call_target="tpu_custom_call", output_to_operand_aliasing={{0}: (12, {}), {1}: (13, {}), {2}: (14, {})} | custom-call | flops 500000000 | bytes 1000000 | tf_op jit(solution)/shard_map/gate_up_sum/pallas_call | solution.py:335
  134.4 2.0 %hidden.3 = bf16[272,1536]{1,0:T(8,128)(2,1)S(1)} custom-call(s32[9]{0:T(128)S(1)} %pad_add_fusion.1.owners, s32[528,1]{1,0:T(8,128)S(1)} %copy-done.1, f32[4,4096]{1,0:T(4,128)S(1)} %copy-done.2, bf16[512,1536]{1,0:T(8,128)(2,1)S(1)} %get-tuple-element.274.w_gate, bf16[512,1536]{1,0:T(8,128)(2,1)S(1)} %get-tuple-element.275.w_up, ...), custom_call_target="tpu_custom_call" | custom-call | flops 500000000 | bytes 1000000 | tf_op jit(solution)/shard_map/hidden/pallas_call | solution.py:363
  141.8 3.3 %collective-permute-done.46.rest_2_ = bf16[272,512]{1,0:T(8,128)(2,1)S(1)} collective-permute-done((bf16[272,512]{1,0:T(8,128)(2,1)S(1)}, bf16[272,512]{1,0:T(8,128)(2,1)S(1)}, u32[]{:S(2)}, u32[]{:S(2)}) %collective-permute-start.46) | collective-permute-done | bytes 278560 | tf_op jit(solution)/shard_map/ppermute | solution.py:494
  154.3 2.5 %collective-permute-done.50.rest_3_ = bf16[272,512]{1,0:T(8,128)(2,1)S(1)} collective-permute-done((bf16[272,512]{1,0:T(8,128)(2,1)S(1)}, bf16[272,512]{1,0:T(8,128)(2,1)S(1)}, u32[]{:S(2)}, u32[]{:S(2)}) %collective-permute-start.50) | collective-permute-done | bytes 278560 | tf_op jit(solution)/shard_map/ppermute | solution.py:498
  158.4 2.2 %collective-permute-start.53 = (bf16[272,512]{1,0:T(8,128)(2,1)S(1)}, bf16[272,512]{1,0:T(8,128)(2,1)S(1)}, u32[]{:S(2)}, u32[]{:S(2)}) collective-permute-start(bf16[272,512]{1,0:T(8,128)(2,1)S(1)} %get-tuple-element.301), channel_id=1, source_target_pairs={{0,2},{2,4},{4,6},{6,7},{7,5},{5,3},{3,1},{1,0},{8,10},{10,12},{12... | collective-permute-start | bytes 835592 | tf_op jit(solution)/shard_map/ppermute | solution.py:498
  166.7 2.8 %collective-permute-done.54.rest_3_ = bf16[272,512]{1,0:T(8,128)(2,1)S(1)} collective-permute-done((bf16[272,512]{1,0:T(8,128)(2,1)S(1)}, bf16[272,512]{1,0:T(8,128)(2,1)S(1)}, u32[]{:S(2)}, u32[]{:S(2)}) %collective-permute-start.54) | collective-permute-done | bytes 278560 | tf_op jit(solution)/shard_map/ppermute | solution.py:498
  174.6 3.1 %collective-permute-done.57.rest_1_ = bf16[272,512]{1,0:T(8,128)(2,1)S(1)} collective-permute-done((bf16[272,512]{1,0:T(8,128)(2,1)S(1)}, bf16[272,512]{1,0:T(8,128)(2,1)S(1)}, u32[]{:S(2)}, u32[]{:S(2)}) %collective-permute-start.57) | collective-permute-done | bytes 278560 | tf_op jit(solution)/shard_map/ppermute | solution.py:498
  (163 shorter events, 104.6 us)
Async XLA Ops:
  43.6 9.4 %collective-permute-start.21 = (bf16[1056,128]{1,0:T(8,128)(2,1)S(1)}, bf16[1056,128]{1,0:T(8,128)(2,1)S(1)}, u32[]{:S(2)}, u32[]{:S(2)}) collective-permute-start(bf16[1056,128]{1,0:T(8,128)(2,1)S(1)} %prefill_attention.3.rest_0_), channel_id=1, source_target_pairs={{0,2},{2,4},{4,6},{6,7},{7,5},{5,3},{3,1},{1,0},{8,10},{10,12},{12... | collective-permute-start | bytes 811016 | tf_op jit(solution)/shard_map/ppermute | solution.py:474
  45.1 9.4 %collective-permute-start.22 = (bf16[1056,128]{1,0:T(8,128)(2,1)S(1)}, bf16[1056,128]{1,0:T(8,128)(2,1)S(1)}, u32[]{:S(2)}, u32[]{:S(2)}) collective-permute-start(bf16[1056,128]{1,0:T(8,128)(2,1)S(1)} %prefill_attention.3.rest_0_), channel_id=1, source_target_pairs={{2,0},{4,2},{6,4},{7,6},{5,7},{3,5},{1,3},{0,1},{10,8},{12,10},{14... | collective-permute-start | bytes 811016 | tf_op jit(solution)/shard_map/ppermute | solution.py:475
  46.8 11.9 %collective-permute-start.19 = (bf16[1024,128]{1,0:T(8,128)(2,1)S(1)}, bf16[1024,128]{1,0:T(8,128)(2,1)S(1)}, u32[]{:S(2)}, u32[]{:S(2)}) collective-permute-start(bf16[1024,128]{1,0:T(8,128)(2,1)S(1)} %collective-permute-done.14.rest_1_), channel_id=1, source_target_pairs={{0,2},{2,4},{4,6},{6,7},{7,5},{5,3},{3,1},{1,0},{8,10},{10,12},{12... | collective-permute-start | bytes 786440 | tf_op jit(solution)/shard_map/ppermute | solution.py:474
  48.0 12.2 %collective-permute-start.20 = (bf16[1024,128]{1,0:T(8,128)(2,1)S(1)}, bf16[1024,128]{1,0:T(8,128)(2,1)S(1)}, u32[]{:S(2)}, u32[]{:S(2)}) collective-permute-start(bf16[1024,128]{1,0:T(8,128)(2,1)S(1)} %collective-permute-done.15.rest_7_), channel_id=1, source_target_pairs={{2,0},{4,2},{6,4},{7,6},{5,7},{3,5},{1,3},{0,1},{10,8},{12,10},{14... | collective-permute-start | bytes 786440 | tf_op jit(solution)/shard_map/ppermute | solution.py:475
  54.6 10.1 %collective-permute-start.25 = (bf16[1056,128]{1,0:T(8,128)(2,1)S(1)}, bf16[1056,128]{1,0:T(8,128)(2,1)S(1)}, u32[]{:S(2)}, u32[]{:S(2)}) collective-permute-start(bf16[1056,128]{1,0:T(8,128)(2,1)S(1)} %collective-permute-done.21.rest_1_), channel_id=1, source_target_pairs={{0,2},{2,4},{4,6},{6,7},{7,5},{5,3},{3,1},{1,0},{8,10},{10,12},{12... | collective-permute-start | bytes 811016 | tf_op jit(solution)/shard_map/ppermute | solution.py:474
  55.8 10.1 %collective-permute-start.26 = (bf16[1056,128]{1,0:T(8,128)(2,1)S(1)}, bf16[1056,128]{1,0:T(8,128)(2,1)S(1)}, u32[]{:S(2)}, u32[]{:S(2)}) collective-permute-start(bf16[1056,128]{1,0:T(8,128)(2,1)S(1)} %collective-permute-done.22.rest_7_), channel_id=1, source_target_pairs={{2,0},{4,2},{6,4},{7,6},{5,7},{3,5},{1,3},{0,1},{10,8},{12,10},{14... | collective-permute-start | bytes 811016 | tf_op jit(solution)/shard_map/ppermute | solution.py:475
  60.2 10.3 %collective-permute-start.23 = (bf16[1024,128]{1,0:T(8,128)(2,1)S(1)}, bf16[1024,128]{1,0:T(8,128)(2,1)S(1)}, u32[]{:S(2)}, u32[]{:S(2)}) collective-permute-start(bf16[1024,128]{1,0:T(8,128)(2,1)S(1)} %collective-permute-done.19.rest_2_), channel_id=1, source_target_pairs={{0,2},{2,4},{4,6},{6,7},{7,5},{5,3},{3,1},{1,0},{8,10},{10,12},{12... | collective-permute-start | bytes 786440 | tf_op jit(solution)/shard_map/ppermute | solution.py:474
  61.5 10.1 %collective-permute-start.24 = (bf16[1024,128]{1,0:T(8,128)(2,1)S(1)}, bf16[1024,128]{1,0:T(8,128)(2,1)S(1)}, u32[]{:S(2)}, u32[]{:S(2)}) collective-permute-start(bf16[1024,128]{1,0:T(8,128)(2,1)S(1)} %collective-permute-done.20.rest_6_), channel_id=1, source_target_pairs={{2,0},{4,2},{6,4},{7,6},{5,7},{3,5},{1,3},{0,1},{10,8},{12,10},{14... | collective-permute-start | bytes 786440 | tf_op jit(solution)/shard_map/ppermute | solution.py:475
  66.0 9.8 %collective-permute-start.28 = (bf16[1056,128]{1,0:T(8,128)(2,1)S(1)}, bf16[1056,128]{1,0:T(8,128)(2,1)S(1)}, u32[]{:S(2)}, u32[]{:S(2)}) collective-permute-start(bf16[1056,128]{1,0:T(8,128)(2,1)S(1)} %collective-permute-done.25.rest_2_), channel_id=1, source_target_pairs={{0,2},{2,4},{4,6},{6,7},{7,5},{5,3},{3,1},{1,0},{8,10},{10,12},{12... | collective-permute-start | bytes 811016 | tf_op jit(solution)/shard_map/ppermute | solution.py:474
  82.4 11.3 %collective-permute-start.33 = (bf16[256,512]{1,0:T(8,128)(2,1)S(1)}, bf16[256,512]{1,0:T(8,128)(2,1)S(1)}, u32[]{:S(2)}, u32[]{:S(2)}) collective-permute-start(bf16[256,512]{1,0:T(8,128)(2,1)S(1)} %out_projection.2.rest_4_.rest_3_), channel_id=1, source_target_pairs={{0,2},{2,4},{4,6},{6,7},{7,5},{5,3},{3,1},{1,0},{8,10},{10,12},{12... | collective-permute-start | bytes 786440 | tf_op jit(solution)/shard_map/ppermute | solution.py:474
  84.0 9.7 %collective-permute-start.34 = (bf16[256,512]{1,0:T(8,128)(2,1)S(1)}, bf16[256,512]{1,0:T(8,128)(2,1)S(1)}, u32[]{:S(2)}, u32[]{:S(2)}) collective-permute-start(bf16[256,512]{1,0:T(8,128)(2,1)S(1)} %out_projection.2.rest_4_.rest_3_), channel_id=1, source_target_pairs={{2,0},{4,2},{6,4},{7,6},{5,7},{3,5},{1,3},{0,1},{10,8},{12,10},{14... | collective-permute-start | bytes 786440 | tf_op jit(solution)/shard_map/ppermute | solution.py:475
  86.9 10.1 %collective-permute-start.31 = (bf16[272,512]{1,0:T(8,128)(2,1)S(1)}, bf16[272,512]{1,0:T(8,128)(2,1)S(1)}, u32[]{:S(2)}, u32[]{:S(2)}) collective-permute-start(bf16[272,512]{1,0:T(8,128)(2,1)S(1)} %out_projection.3.rest_5_.rest_3_), channel_id=1, source_target_pairs={{0,2},{2,4},{4,6},{6,7},{7,5},{5,3},{3,1},{1,0},{8,10},{10,12},{12... | collective-permute-start | bytes 835592 | tf_op jit(solution)/shard_map/ppermute | solution.py:474
  88.4 9.7 %collective-permute-start.32 = (bf16[272,512]{1,0:T(8,128)(2,1)S(1)}, bf16[272,512]{1,0:T(8,128)(2,1)S(1)}, u32[]{:S(2)}, u32[]{:S(2)}) collective-permute-start(bf16[272,512]{1,0:T(8,128)(2,1)S(1)} %out_projection.3.rest_5_.rest_3_), channel_id=1, source_target_pairs={{2,0},{4,2},{6,4},{7,6},{5,7},{3,5},{1,3},{0,1},{10,8},{12,10},{14... | collective-permute-start | bytes 835592 | tf_op jit(solution)/shard_map/ppermute | solution.py:475
  93.7 12.9 %collective-permute-start.37 = (bf16[256,512]{1,0:T(8,128)(2,1)S(1)}, bf16[256,512]{1,0:T(8,128)(2,1)S(1)}, u32[]{:S(2)}, u32[]{:S(2)}) collective-permute-start(bf16[256,512]{1,0:T(8,128)(2,1)S(1)} %collective-permute-done.33.rest_7_), channel_id=1, source_target_pairs={{0,2},{2,4},{4,6},{6,7},{7,5},{5,3},{3,1},{1,0},{8,10},{10,12},{12... | collective-permute-start | bytes 786440 | tf_op jit(solution)/shard_map/ppermute | solution.py:474
  95.3 11.4 %collective-permute-start.38 = (bf16[256,512]{1,0:T(8,128)(2,1)S(1)}, bf16[256,512]{1,0:T(8,128)(2,1)S(1)}, u32[]{:S(2)}, u32[]{:S(2)}) collective-permute-start(bf16[256,512]{1,0:T(8,128)(2,1)S(1)} %collective-permute-done.34.rest_9_), channel_id=1, source_target_pairs={{2,0},{4,2},{6,4},{7,6},{5,7},{3,5},{1,3},{0,1},{10,8},{12,10},{14... | collective-permute-start | bytes 786440 | tf_op jit(solution)/shard_map/ppermute | solution.py:475
  98.1 10.6 %collective-permute-start.35 = (bf16[272,512]{1,0:T(8,128)(2,1)S(1)}, bf16[272,512]{1,0:T(8,128)(2,1)S(1)}, u32[]{:S(2)}, u32[]{:S(2)}) collective-permute-start(bf16[272,512]{1,0:T(8,128)(2,1)S(1)} %collective-permute-done.31.rest_8_), channel_id=1, source_target_pairs={{0,2},{2,4},{4,6},{6,7},{7,5},{5,3},{3,1},{1,0},{8,10},{10,12},{12... | collective-permute-start | bytes 835592 | tf_op jit(solution)/shard_map/ppermute | solution.py:474
  99.4 10.4 %collective-permute-start.36 = (bf16[272,512]{1,0:T(8,128)(2,1)S(1)}, bf16[272,512]{1,0:T(8,128)(2,1)S(1)}, u32[]{:S(2)}, u32[]{:S(2)}) collective-permute-start(bf16[272,512]{1,0:T(8,128)(2,1)S(1)} %collective-permute-done.32.rest_10_), channel_id=1, source_target_pairs={{2,0},{4,2},{6,4},{7,6},{5,7},{3,5},{1,3},{0,1},{10,8},{12,10},{14... | collective-permute-start | bytes 835592 | tf_op jit(solution)/shard_map/ppermute | solution.py:475
  106.7 12.6 %collective-permute-start.39 = (bf16[256,512]{1,0:T(8,128)(2,1)S(1)}, bf16[256,512]{1,0:T(8,128)(2,1)S(1)}, u32[]{:S(2)}, u32[]{:S(2)}) collective-permute-start(bf16[256,512]{1,0:T(8,128)(2,1)S(1)} %collective-permute-done.37.rest_6_), channel_id=1, source_target_pairs={{0,2},{2,4},{4,6},{6,7},{7,5},{5,3},{3,1},{1,0},{8,10},{10,12},{12... | collective-permute-start | bytes 786440 | tf_op jit(solution)/shard_map/ppermute | solution.py:474
  108.0 11.3 %collective-permute-start.40 = (bf16[256,512]{1,0:T(8,128)(2,1)S(1)}, bf16[256,512]{1,0:T(8,128)(2,1)S(1)}, u32[]{:S(2)}, u32[]{:S(2)}) collective-permute-start(bf16[256,512]{1,0:T(8,128)(2,1)S(1)} %collective-permute-done.38.rest_8_), channel_id=1, source_target_pairs={{2,0},{4,2},{6,4},{7,6},{5,7},{3,5},{1,3},{0,1},{10,8},{12,10},{14... | collective-permute-start | bytes 786440 | tf_op jit(solution)/shard_map/ppermute | solution.py:475
  109.8 11.0 %collective-permute-start.42 = (bf16[272,512]{1,0:T(8,128)(2,1)S(1)}, bf16[272,512]{1,0:T(8,128)(2,1)S(1)}, u32[]{:S(2)}, u32[]{:S(2)}) collective-permute-start(bf16[272,512]{1,0:T(8,128)(2,1)S(1)} %collective-permute-done.35.rest_7_), channel_id=1, source_target_pairs={{0,2},{2,4},{4,6},{6,7},{7,5},{5,3},{3,1},{1,0},{8,10},{10,12},{12... | collective-permute-start | bytes 835592 | tf_op jit(solution)/shard_map/ppermute | solution.py:474
  111.3 9.5 %collective-permute-start.43 = (bf16[272,512]{1,0:T(8,128)(2,1)S(1)}, bf16[272,512]{1,0:T(8,128)(2,1)S(1)}, u32[]{:S(2)}, u32[]{:S(2)}) collective-permute-start(bf16[272,512]{1,0:T(8,128)(2,1)S(1)} %collective-permute-done.36.rest_9_), channel_id=1, source_target_pairs={{2,0},{4,2},{6,4},{7,6},{5,7},{3,5},{1,3},{0,1},{10,8},{12,10},{14... | collective-permute-start | bytes 835592 | tf_op jit(solution)/shard_map/ppermute | solution.py:475
  120.8 13.6 %collective-permute-start.44 = (bf16[272,512]{1,0:T(8,128)(2,1)S(1)}, bf16[272,512]{1,0:T(8,128)(2,1)S(1)}, u32[]{:S(2)}, u32[]{:S(2)}) collective-permute-start(bf16[272,512]{1,0:T(8,128)(2,1)S(1)} %collective-permute-done.43.rest_8_), channel_id=1, source_target_pairs={{2,0},{4,2},{6,4},{7,6},{5,7},{3,5},{1,3},{0,1},{10,8},{12,10},{14... | collective-permute-start | bytes 835592 | tf_op jit(solution)/shard_map/ppermute | solution.py:472
  141.2 9.5 %collective-permute-start.48 = (bf16[256,512]{1,0:T(8,128)(2,1)S(1)}, bf16[256,512]{1,0:T(8,128)(2,1)S(1)}, u32[]{:S(2)}, u32[]{:S(2)}) collective-permute-start(bf16[256,512]{1,0:T(8,128)(2,1)S(1)} %get-tuple-element.297), channel_id=1, source_target_pairs={{2,0},{4,2},{6,4},{7,6},{5,7},{3,5},{1,3},{0,1},{10,8},{12,10},{14... | collective-permute-start | bytes 786440 | tf_op jit(solution)/shard_map/ppermute | solution.py:498
  152.2 9.3 %collective-permute-start.51 = (bf16[256,512]{1,0:T(8,128)(2,1)S(1)}, bf16[256,512]{1,0:T(8,128)(2,1)S(1)}, u32[]{:S(2)}, u32[]{:S(2)}) collective-permute-start(bf16[256,512]{1,0:T(8,128)(2,1)S(1)} %get-tuple-element.298), channel_id=1, source_target_pairs={{0,2},{2,4},{4,6},{6,7},{7,5},{5,3},{3,1},{1,0},{8,10},{10,12},{12... | collective-permute-start | bytes 786440 | tf_op jit(solution)/shard_map/ppermute | solution.py:498
  (47 other events, 415.0 us)

commit v5 on v4

--- a/solution.py
+++ b/solution.py
@@ -69,8 +69,8 @@
     return pl.pallas_call(
         pack_kernel,
         out_shape=[
-            jax.ShapeDtypeStruct((KVH * rows + H, HD), BF16),
-            jax.ShapeDtypeStruct((KVH * rows, HD), BF16),
+            pltpu.VMEM((KVH * rows + H, HD), BF16),
+            pltpu.VMEM((KVH * rows, HD), BF16),
         ],
         in_specs=[VMEM, VMEM],
         out_specs=[VMEM, VMEM],
@@ -196,39 +196,47 @@
 
 
 class Fetch:
-    def __init__(self, shares=(), blocks=()):
-        self.shares, self.blocks = tuple(shares), tuple(blocks)
+    def __init__(self, gate=(), up=(), blocks=()):
+        self.gate, self.up, self.blocks = tuple(gate), tuple(up), tuple(blocks)
 
     def shapes(self, cols, wide):
-        out = [pltpu.VMEM((cols, wide), BF16)] * (2 * len(self.shares))
+        out = [pltpu.VMEM((len(s) * cols, wide), BF16) for s in (self.gate, self.up) if s]
         return out + [pltpu.VMEM((wide, cols), BF16) for _ in self.blocks]
 
     def count(self):
-        return 2 * len(self.shares) + len(self.blocks)
+        return len(self.gate) + len(self.up) + len(self.blocks)
 
     def outs(self):
-        return 2 * len(self.shares) + len(self.blocks)
-
-    def ins(self):
-        return 3 if self.blocks else 2 if self.shares else 0
+        return (len(self.gate) > 0) + (len(self.up) > 0) + len(self.blocks)
+
+    def keep(self, outs, store):
+        outs = list(outs)
+        if self.gate:
+            store["gate", self.gate] = outs.pop(0)
+        if self.up:
+            store["up", self.up] = outs.pop(0)
+        for block in self.blocks:
+            store["down", block] = outs.pop(0)
 
     def start(self, owners, weights, outs, sems):
-        pairs = []
-        if self.shares:
-            gate, up = weights[:2]
-            cols = outs[0].shape[0]
-            for share in self.shares:
-                at = pl.ds(pl.multiple_of(owners[share] * cols, cols), cols)
-                pairs += [(gate.at[at], outs[0]), (up.at[at], outs[1])]
-                outs = outs[2:]
-        for block, out in zip(self.blocks, outs):
+        pairs, outs = [], list(outs)
+        for ref, shares in ((weights[0], self.gate), (weights[1], self.up)):
+            if shares:
+                out = outs.pop(0)
+                cols = out.shape[0] // len(shares)
+                for i, share in enumerate(shares):
+                    at = pl.ds(pl.multiple_of(owners[share] * cols, cols), cols)
+                    pairs.append((ref.at[at], out.at[pl.ds(i * cols, cols)]))
+        for block in self.blocks:
+            out = outs.pop(0)
             cols = out.shape[1]
-            pairs.append((weights[2].at[:, pl.ds(pl.multiple_of(owners[block] * cols, HD), cols)], out))
+            at = pl.ds(pl.multiple_of(owners[block] * cols, HD), cols)
+            pairs.append((weights[2].at[:, at], out))
         return copies(pairs, sems)
 
 
 def fetch_kernel(fetch, owners, *rest):
-    for c in fetch.start(owners, rest[: fetch.ins()], rest[fetch.ins() : -1], rest[-1]):
+    for c in fetch.start(owners, rest[:3], rest[3:-1], rest[-1]):
         c.wait()
 
 
@@ -237,13 +245,13 @@
     return pl.pallas_call(
         functools.partial(fetch_kernel, fetch),
         out_shape=shapes,
-        in_specs=[SMEM] + [HBM] * fetch.ins(),
+        in_specs=[SMEM] + [HBM] * 3,
         out_specs=[VMEM] * len(shapes),
         scratch_shapes=[pltpu.SemaphoreType.DMA((fetch.count(),))],
         compiler_params=params(16),
         cost_estimate=STEP,
         name="fetch_weights",
-    )(owners, *[in_hbm(x) for x in weights[: fetch.ins()]])
+    )(owners, *[in_hbm(x) for x in weights])
 
 
 def project_kernel(n, rows, first, owners, *rest):
@@ -301,8 +309,8 @@
 
 
 def feed_kernel(lo, hi, shares, taken, fetch, owners, tenants_ref, gain_ref, *rest):
-    weights, rest = rest[: fetch.ins()], rest[fetch.ins() :]
-    w_refs, rest = rest[: 2 * len(shares)], rest[2 * len(shares) :]
+    weights, rest = rest[:3], rest[3:]
+    w_refs, rest = rest[:2], rest[2:]
     chunks = (len(rest) - 5 - fetch.outs() - 3 * taken) // len(shares)
     parts, rest = rest[: chunks * len(shares)], rest[chunks * len(shares) :]
     held, rest = (rest[:3], rest[3:]) if taken else (None, rest)
@@ -318,24 +326,22 @@
         scaled[:, i * cols : (i + 1) * cols] = x
     squares[lo:hi, :] = total
     for i, out in enumerate((gates, lifts)):
-        one = jnp.dot(scaled[:, :cols], w_refs[i][...], preferred_element_type=F32)
-        if len(shares) > 1:
-            one = one + jnp.dot(scaled[:, cols:], w_refs[2 + i][...], preferred_element_type=F32)
+        one = jnp.dot(scaled[...], w_refs[i][...], preferred_element_type=F32)
         out[lo:hi, :] = held[i][lo:hi, :] + one if taken else one
     for c in moving:
         c.wait()
 
 
-def feed(lo, hi, shares, owners, tenants, gain, weights, w, parts, held, fetch, grant):
+def feed(lo, hi, shares, owners, tenants, gain, weights, w, parts, held, fetch):
     m, wide = tenants.shape[0], w[0].shape[1]
     cols = parts[0].shape[1]
-    first = 3 + fetch.ins() + len(w) + len(parts)
+    first = 6 + len(w) + len(parts)
     fetched = fetch.shapes(cols, wide)
     sums = [jax.ShapeDtypeStruct((m, wide), F32)] * 2 + [jax.ShapeDtypeStruct((m, HD), F32)]
     return pl.pallas_call(
         functools.partial(feed_kernel, lo, hi, shares, len(held) > 0, fetch),
         out_shape=sums + fetched,
-        in_specs=[SMEM, VMEM, VMEM] + [HBM] * fetch.ins() + [VMEM] * (len(w) + len(parts) + len(held)),
+        in_specs=[SMEM, VMEM, VMEM] + [HBM] * 3 + [VMEM] * (len(w) + len(parts) + len(held)),
         out_specs=[VMEM] * (3 + len(fetched)),
         scratch_shapes=[
             pltpu.VMEM((hi - lo, cols * len(shares)), BF16),
@@ -345,7 +351,7 @@
         compiler_params=params(16),
         cost_estimate=STEP,
         name="gate_up_sum",
-    )(owners, tenants, gain, *[in_hbm(x) for x in weights[: fetch.ins()]], *w, *parts, *held)
+    )(owners, tenants, gain, *[in_hbm(x) for x in weights], *w, *parts, *held)
 
 
 def hidden_kernel(lo, hi, share, owners, tenants_ref, gain_ref, w_gate, w_up, part, gates, lifts, squares, out):
@@ -369,6 +375,32 @@
         cost_estimate=STEP,
         name="hidden",
     )(owners, tenants, gain, *w, part, *held)
+
+
+def assemble_kernel(n, rows, owners, hidden, w, fw, bw, own, top, out, block):
+    total = jnp.dot(hidden[...], w[...], preferred_element_type=F32)
+    total = total + fw[...].astype(F32) + bw[...].astype(F32) + own[...].astype(F32)
+    local = block.shape[0] // n
+    for b in range(n):
+        at = b * local
+        block[at : at + rows, :] = top[b * rows : (b + 1) * rows, :].astype(F32)
+        block[at + rows : at + 2 * rows, :] = total[b * rows : (b + 1) * rows, :]
+        block[at + 2 * rows : at + local, :] = total[n * rows + b : n * rows + b + 1, :]
+    out[...] = block[...].astype(BF16)
+
+
+def assemble(n, rows, owners, hidden, w, arrived, own, top):
+    shape = (n * (2 * rows + 1), top.shape[1])
+    return pl.pallas_call(
+        functools.partial(assemble_kernel, n, rows),
+        out_shape=jax.ShapeDtypeStruct(shape, BF16),
+        in_specs=[SMEM] + [VMEM] * 6,
+        out_specs=VMEM,
+        scratch_shapes=[pltpu.VMEM(shape, F32)],
+        compiler_params=params(16),
+        cost_estimate=STEP,
+        name="last_sum",
+    )(owners, hidden, w, *arrived, own, top)
 
 
 def down_kernel(flags, own, owners, hidden, *rest):
@@ -481,7 +513,7 @@
         self.own, self.step, self.arrived = own, 0, ()
 
     def call(self, blocks, flags, own=()):
-        weights = [self.blocks[-b % self.chain.n] for b in blocks]
+        weights = [self.blocks["down", -b % self.chain.n] for b in blocks]
         out = down(flags, self.run.after(), self.hidden, weights, self.arrived, own)
         self.run.mark(out[0])
         return out
@@ -550,6 +582,8 @@
     run.hop(keys)
     run.tick()
     run.hop(values)
+    tenants, gain = settle(tenants, norm_gain)
+    run.mark(*run.last, tenants, owners)
     while not keys.done():
         run.tick()
         run.hop(keys)
@@ -567,23 +601,28 @@
     b = chain(run.mark(attention(rows, rows, run.after(), pre_q, pre_segment, kv, (dec,))), "bw")
     run.hop(b)
     run.hop(a)
-    tenants, gain = settle(tenants, norm_gain)
-    run.mark(*run.last, tenants)
-    run.hop(b)
     weights = (w_gate, w_up, w_down)
     wide = w_gate.shape[1]
     far = [d for d in range(half - 1, half + 2)]
-    fetches = [Fetch([0]), Fetch([1]), Fetch([n - 1]), Fetch((), far)]
-    blocks, early = {}, {}
+    fetches = [
+        Fetch([0], [0]),
+        Fetch([1, n - 1]),
+        Fetch((), [1, n - 1]),
+        Fetch([half], [half]),
+    ]
+    fetches.insert(0, Fetch((), (), far))
+    store = {}
 
     def fetch_some():
         if fetches:
             fetch = fetches.pop(0)
             out = fetch_early(fetch, run.after(), weights, cols, wide)
             run.mark(out[0])
-            blocks.update(zip(fetch.blocks, out))
-            early.update({share: out for share in fetch.shares})
-
+            fetch.keep(out, store)
+
+    fetch_some()
+    run.hop(b)
+    fetch_some()
     while not a.done():
         run.hop(a)
         fetch_some()
@@ -601,52 +640,50 @@
     m_a, m = mixed_a.shape[0], tenants.shape[0]
     held = ()
 
-    def add(lo, hi, shares, parts, fetch, grant):
-        w = [x for share in shares for x in early[share]]
-        out = feed(lo, hi, shares, run.after(), tenants, gain, weights, w, parts, held, fetch, grant)
+    def add(lo, hi, shares, parts, fetch):
+        w = [store["gate", tuple(shares)], store["up", tuple(shares)]]
+        out = feed(lo, hi, shares, run.after(), tenants, gain, weights, w, parts, held, fetch)
         run.mark(out[2])
-        for i, share in enumerate(fetch.shares):
-            early[share] = out[3 + 2 * i : 5 + 2 * i]
-        blocks.update(zip(fetch.blocks, out[3 + 2 * len(fetch.shares) :]))
+        fetch.keep(out[3:], store)
         return out[:3]
 
     def arrived(i):
         return [g.ahead[i], h.ahead[i], g.behind[i], h.behind[i]]
 
-    held = add(0, m, [0], [mixed_a, mixed_b], Fetch([2, n - 2] if half > 2 else [half]), 24)
+    def pair(i):
+        return [i, n - i] if 1 < i < half else []
+
+    def missing(ds):
+        return [d for d in ds if ("down", d) not in store]
+
+    held = add(0, m, [0], [mixed_a, mixed_b], Fetch(pair(2)))
     run.hop(g)
     run.hop(h)
     for i in range(1, half - 1):
-        if i == 1:
-            fetch = Fetch((), [half - 2, half + 2])
-        else:
-            fetch = Fetch([i + 1, n - i - 1])
-        held = add(0, m, [i, n - i], arrived(i), fetch, 24)
+        more = missing([half - 2, half + 2]) if i == half - 2 else []
+        held = add(0, m, [i, n - i], arrived(i), Fetch(pair(i + 2), pair(i + 1), more))
         run.hop(g)
         run.hop(h)
     i = half - 1
-    held = add(0, m_a, [i, n - i], arrived(i)[::2], Fetch([half], [d for d in range(1, n) if d not in blocks]), 16)
+    held = add(0, m_a, [i, n - i], arrived(i)[::2], Fetch((), (), missing(range(1, n))))
+
+    last = [store["gate", (half,)], store["up", (half,)]]
 
     def finish(lo, hi, part):
-        return run.mark(hide(lo, hi, half, run.after(), tenants, gain, early[half], part, held))
+        return run.mark(hide(lo, hi, half, run.after(), tenants, gain, last, part, held))
 
     hid_a = finish(0, m_a, g.ahead[half])
-    sum_a = Sum(run, g, hid_a, blocks, mixed_a)
+    sum_a = Sum(run, g, hid_a, store, mixed_a)
     sum_a.hop()
-    held = add(m_a, m, [i, n - i], arrived(i)[1::2], Fetch((), [0]), 16)
+    held = add(m_a, m, [i, n - i], arrived(i)[1::2], Fetch((), (), [0]))
     hid_b = finish(m_a, m, h.behind[half])
-    sum_b = Sum(run, h, hid_b, blocks, mixed_b)
+    sum_b = Sum(run, h, hid_b, store, mixed_b)
     sum_b.hop()
     for _ in range(1, half):
         sum_a.hop()
         sum_b.hop()
     out_a = sum_a.finish()
-    out_b = sum_b.finish()
-
-    top = out_a.reshape(n, rows, cols)
-    low = out_b[: n * rows].reshape(n, rows, cols)
-    tail = out_b[n * rows : n * rows + n].reshape(n, 1, cols)
-    return jnp.concatenate([top, low, tail], axis=1).reshape(n * (local + 1), cols)
+    return assemble(n, rows, run.after(), hid_b, store["down", 0], sum_b.arrived, mixed_b, out_a)
 
 
 def solution(mesh):

time: 182 us -> 178 us (0.978)
  local copies, waits for them, and re-layouts: 3.28 us -> 1.35 us
    pallas_call x5, Pallas kernels: 26.9 us -> 23.9 us  [feed(): pl.pallas_call(functools.partial(feed_kernel, lo, hi, shares, len(held) >...]
    ppermute x21, starting transfers between devices: 32.7 us -> 35.5 us  [hop(): chain.ahead.append(lax.ppermute(f, 'tok', chain.fw))]
    ppermute x21, starting transfers between devices: 10.9 us -> 8.47 us  [hop(): chain.behind.append(lax.ppermute(b, 'tok', chain.bw))]
    pallas_call x4 -> x5, Pallas kernels: 10.5 us -> 12.7 us  [fetch_early(): pl.pallas_call(functools.partial(fetch_kernel, fetch), out_shape=shapes,...]
    pallas_call x10 -> x9, Pallas kernels: 13.8 us -> 12.6 us  [down(): pl.pallas_call(functools.partial(down_kernel, flags, len(own)), out_shape...]
  transfers between devices with their start and end apart: 59 -> 59, of which waited for: 31 -> 34; matrix products, arithmetic and copies ran while one was open for 1% -> 1% of each run, Pallas kernels for 38% -> 38%
where the time goes in v5:
time: 178 us
  Pallas kernels  71 us (40%)
  starting transfers between devices  60.7 us (34%)
  waiting for transfers between devices  43.2 us (24%)
    ppermute x21, starting transfers between devices, hop(): chain.ahead.append(lax.ppermute(f, 'tok', chain.fw))  35.5 us
    pallas_call x5, Pallas kernels, feed(): pl.pallas_call(functools.partial(feed_kernel, lo, hi, shares, len(held) >...  23.9 us
    ppermute x21, waiting for transfers between devices, hop(): chain.behind.append(lax.ppermute(b, 'tok', chain.bw))  14.7 us
    pallas_call x5, Pallas kernels, fetch_early(): pl.pallas_call(functools.partial(fetch_kernel, fetch), out_shape=shapes,...  12.7 us
    pallas_call x9, Pallas kernels, down(): pl.pallas_call(functools.partial(down_kernel, flags, len(own)), out_shape...  12.6 us
    ppermute x6, starting transfers between devices, hop(): lax.ppermute(out[0], 'tok', chain.fw)  10.8 us
    ppermute x6, waiting for transfers between devices, hop(): lax.ppermute(out[1], 'tok', chain.bw)  10.5 us
    ppermute x21, waiting for transfers between devices, hop(): chain.ahead.append(lax.ppermute(f, 'tok', chain.fw))  10.5 us
  transfers between devices with their start and end apart: 59, of which 34 were waited for; matrix products, arithmetic and copies ran while one was open for 1% of the time, Pallas kernels for 38%

profile of v5, /device:TPU:0, one launch (start us, length us, event | category | flops | bytes accessed | tf_op | source)
XLA Modules:
  0.0 178.0 jit_solution(14425759241303876051)
XLA Ops:
  1.1 3.1 %collective-permute-start = (bf16[544,128]{1,0:T(8,128)(2,1)S(1)}, bf16[544,128]{1,0:T(8,128)(2,1)S(1)}, u32[]{:S(2)}, u32[]{:S(2)}) collective-permute-start(bf16[544,128]{1,0:T(8,128)(2,1)S(1)} %get-tuple-element.157.rest_0_), channel_id=1, source_target_pairs={{0,2},{2,4},{4,6},{6,7},{7,5},{5,3},{3,1},{1,0},{8,10},{10,12},{12... | collective-permute-start | bytes 417800 | tf_op jit(solution)/shard_map/ppermute | solution.py:506
  4.2 2.0 %collective-permute-start.4 = (bf16[512,128]{1,0:T(8,128)(2,1)S(1)}, bf16[512,128]{1,0:T(8,128)(2,1)S(1)}, u32[]{:S(2)}, u32[]{:S(2)}) collective-permute-start(bf16[512,128]{1,0:T(8,128)(2,1)S(1)} %get-tuple-element.166.rest_8_), channel_id=1, source_target_pairs={{0,2},{2,4},{4,6},{6,7},{7,5},{5,3},{3,1},{1,0},{8,10},{10,12},{12... | collective-permute-start | bytes 393224 | tf_op jit(solution)/shard_map/ppermute | solution.py:506
  32.7 3.0 %prefill_attention.2.rest_0_ = bf16[1024,128]{1,0:T(8,128)(2,1)S(1)} custom-call(s32[9]{0:T(128)S(1)} %pad_add_fusion.1.owners, bf16[64,4096]{1,0:T(8,128)(2,1)S(1)} %copy-done.5, s32[1,512]{1,0:T(1,128)S(1)} %copy-done.6, bf16[544,128]{1,0:T(8,128)(2,1)S(1)} %get-tuple-element.157.rest_0_, bf16[544,128]{1,0:T(8,128)(2,1)S(1)} %collective-permute-done.rest_1_, ...), custom_call_target="tpu_custom_call" | custom-call | flops 500000000 | bytes 1000000 | tf_op jit(solution)/shard_map/prefill_attention/pallas_call | solution.py:114
  39.3 3.0 %prefill_attention.3.rest_0_ = bf16[1056,128]{1,0:T(8,128)(2,1)S(1)} custom-call(s32[9]{0:T(128)S(1)} %pad_add_fusion.1.owners, bf16[64,4096]{1,0:T(8,128)(2,1)S(1)} %copy-done.5, s32[1,512]{1,0:T(1,128)S(1)} %copy-done.6, bf16[544,128]{1,0:T(8,128)(2,1)S(1)} %get-tuple-element.157.rest_0_, bf16[544,128]{1,0:T(8,128)(2,1)S(1)} %collective-permute-done.rest_1_, ...), custom_call_target="tpu_custom_call" | custom-call | flops 500000000 | bytes 1000000 | tf_op jit(solution)/shard_map/prefill_attention/pallas_call | solution.py:114
  46.9 2.9 %fetch_weights.5 = (bf16[1536,512]{1,0:T(8,128)(2,1)S(1)}, bf16[1536,512]{1,0:T(8,128)(2,1)S(1)}, bf16[1536,512]{1,0:T(8,128)(2,1)S(1)}) custom-call(s32[9]{0:T(128)S(1)} %pad_add_fusion.1.owners, bf16[4096,1536]{1,0:T(8,128)(2,1)} %rest_0_.19, bf16[4096,1536]{1,0:T(8,128)(2,1)} %rest_1_.19, bf16[1536,4096]{1,0:T(8,128)(2,1)} %rest_2_.19), custom_call_target="tpu_custom_call" | custom-call | flops 500000000 | bytes 1000000 | tf_op jit(solution)/shard_map/fetch_weights/pallas_call | solution.py:245
  55.4 2.4 %fetch_weights.6 = (bf16[512,1536]{1,0:T(8,128)(2,1)S(1)}, bf16[512,1536]{1,0:T(8,128)(2,1)S(1)}) custom-call(s32[9]{0:T(128)S(1)} %pad_add_fusion.1.owners, bf16[4096,1536]{1,0:T(8,128)(2,1)} %rest_0_.19, bf16[4096,1536]{1,0:T(8,128)(2,1)} %rest_1_.19, bf16[1536,4096]{1,0:T(8,128)(2,1)} %rest_2_.19), custom_call_target="tpu_custom_call" | custom-call | flops 500000000 | bytes 1000000 | tf_op jit(solution)/shard_map/fetch_weights/pallas_call | solution.py:245
  61.0 2.4 %fetch_weights.7.rest_3_ = bf16[1024,1536]{1,0:T(8,128)(2,1)S(1)} custom-call(s32[9]{0:T(128)S(1)} %pad_add_fusion.1.owners, bf16[4096,1536]{1,0:T(8,128)(2,1)} %rest_0_.19, bf16[4096,1536]{1,0:T(8,128)(2,1)} %rest_1_.19, bf16[1536,4096]{1,0:T(8,128)(2,1)} %rest_2_.19), custom_call_target="tpu_custom_call" | custom-call | flops 500000000 | bytes 1000000 | tf_op jit(solution)/shard_map/fetch_weights/pallas_call | solution.py:245
  66.8 2.4 %fetch_weights.8.rest_4_ = bf16[1024,1536]{1,0:T(8,128)(2,1)S(1)} custom-call(s32[9]{0:T(128)S(1)} %pad_add_fusion.1.owners, bf16[4096,1536]{1,0:T(8,128)(2,1)} %rest_0_.19, bf16[4096,1536]{1,0:T(8,128)(2,1)} %rest_1_.19, bf16[1536,4096]{1,0:T(8,128)(2,1)} %rest_2_.19), custom_call_target="tpu_custom_call" | custom-call | flops 500000000 | bytes 1000000 | tf_op jit(solution)/shard_map/fetch_weights/pallas_call | solution.py:245
  71.9 2.4 %fetch_weights.9 = (bf16[512,1536]{1,0:T(8,128)(2,1)S(1)}, bf16[512,1536]{1,0:T(8,128)(2,1)S(1)}) custom-call(s32[9]{0:T(128)S(1)} %pad_add_fusion.1.owners, bf16[4096,1536]{1,0:T(8,128)(2,1)} %rest_0_.19, bf16[4096,1536]{1,0:T(8,128)(2,1)} %rest_1_.19, bf16[1536,4096]{1,0:T(8,128)(2,1)} %rest_2_.19), custom_call_target="tpu_custom_call" | custom-call | flops 500000000 | bytes 1000000 | tf_op jit(solution)/shard_map/fetch_weights/pallas_call | solution.py:245
  75.0 3.3 %collective-permute-done.27.rest_4_ = bf16[1024,128]{1,0:T(8,128)(2,1)S(1)} collective-permute-done((bf16[1024,128]{1,0:T(8,128)(2,1)S(1)}, bf16[1024,128]{1,0:T(8,128)(2,1)S(1)}, u32[]{:S(2)}, u32[]{:S(2)}) %collective-permute-start.27) | collective-permute-done | bytes 262176 | tf_op jit(solution)/shard_map/ppermute | solution.py:502
  78.3 2.2 %out_projection.2.rest_5_.rest_3_ = bf16[256,512]{1,0:T(8,128)(2,1)S(1)} custom-call(s32[9]{0:T(128)S(1)} %pad_add_fusion.1.owners, bf16[1024,128]{1,0:T(8,128)(2,1)S(1)} %prefill_attention.2.rest_0_, bf16[1024,128]{1,0:T(8,128)(2,1)S(1)} %collective-permute-done.14.rest_1_, bf16[1024,128]{1,0:T(8,128)(2,1)S(1)} %collective-permute-done.19.rest_2_, ...), custom_call_target="tpu_custom_call" | custom-call | flops 500000000 | bytes 1000000 | tf_op jit(solution)/shard_map/out_projection/pallas_call | solution.py:286
  82.6 2.3 %out_projection.3.rest_6_.own = bf16[272,512]{1,0:T(8,128)(2,1)S(1)} custom-call(s32[9]{0:T(128)S(1)} %pad_add_fusion.1.owners, bf16[1056,128]{1,0:T(8,128)(2,1)S(1)} %prefill_attention.3.rest_0_, bf16[1056,128]{1,0:T(8,128)(2,1)S(1)} %collective-permute-done.21.rest_1_, bf16[1056,128]{1,0:T(8,128)(2,1)S(1)} %collective-permute-done.25.rest_2_, ...), custom_call_target="tpu_custom_call" | custom-call | flops 500000000 | bytes 1000000 | tf_op jit(solution)/shard_map/out_projection/pallas_call | solution.py:286
  87.0 4.2 %gate_up_sum.5 = (f32[528,1536]{1,0:T(8,128)S(1)}, f32[528,1536]{1,0:T(8,128)S(1)}, f32[528,128]{1,0:T(8,128)S(1)}, bf16[1024,1536]{1,0:T(8,128)(2,1)S(1)}) custom-call(s32[9]{0:T(128)S(1)} %pad_add_fusion.1.owners, s32[528,1]{1,0:T(8,128)S(1)} %copy-done.1, f32[4,4096]{1,0:T(4,128)S(1)} %copy-done.2, bf16[4096,1536]{1,0:T(8,128)(2,1)} %rest_0_.19, ...), custom_call_target="tpu_custom_call" | custom-call | flops 500000000 | bytes 1000000 | tf_op jit(solution)/shard_map/gate_up_sum/pallas_call | solution.py:341
  98.5 5.4 %gate_up_sum.6 = (f32[528,1536]{1,0:T(8,128)S(1)}, f32[528,1536]{1,0:T(8,128)S(1)}, f32[528,128]{1,0:T(8,128)S(1)}, bf16[1024,1536]{1,0:T(8,128)(2,1)S(1)}, bf16[1024,1536]{1,0:T(8,128)(2,1)S(1)}) custom-call(s32[9]{0:T(128)S(1)} %pad_add_fusion.1.owners, s32[528,1]{1,0:T(8,128)S(1)} %copy-done.1, ...), custom_call_target="tpu_custom_call", output_to_operand_aliasing={{0}: (12, {}), {1}: (13, {}), {2}: (14, {})} | custom-call | flops 500000000 | bytes 1000000 | tf_op jit(solution)/shard_map/gate_up_sum/pallas_call | solution.py:341
  110.1 7.3 %gate_up_sum.7 = (f32[528,1536]{1,0:T(8,128)S(1)}, f32[528,1536]{1,0:T(8,128)S(1)}, f32[528,128]{1,0:T(8,128)S(1)}, bf16[1024,1536]{1,0:T(8,128)(2,1)S(1)}, bf16...) custom-call(s32[9]{0:T(128)S(1)} %pad_add_fusion.1.owners, ...), custom_call_target="tpu_custom_call", output_to_operand_aliasing={{0}: (12, {}), {1}: (13, {}), {2}: (14, {})} | custom-call | flops 500000000 | bytes 1000000 | tf_op jit(solution)/shard_map/gate_up_sum/pallas_call | solution.py:341
  119.5 4.3 %gate_up_sum.8 = (f32[528,1536]{1,0:T(8,128)S(1)}, f32[528,1536]{1,0:T(8,128)S(1)}, f32[528,128]{1,0:T(8,128)S(1)}, bf16[1536,512]{1,0:T(8,128)(2,1)S(1)}, bf16[1536,512]{1,0:T(8,128)(2,1)S(1)}) custom-call(s32[9]{0:T(128)S(1)} %pad_add_fusion.1.owners, s32[528,1]{1,0:T(8,128)S(1)} %copy-done.1, ...), custom_call_target="tpu_custom_call", output_to_operand_aliasing={{0}: (10, {}), {1}: (11, {}), {2}: (12, {})} | custom-call | flops 500000000 | bytes 1000000 | tf_op jit(solution)/shard_map/gate_up_sum/pallas_call | solution.py:341
  128.8 2.8 %gate_up_sum.9 = (f32[528,1536]{1,0:T(8,128)S(1)}, f32[528,1536]{1,0:T(8,128)S(1)}, f32[528,128]{1,0:T(8,128)S(1)}, bf16[1536,512]{1,0:T(8,128)(2,1)S(1)}) custom-call(s32[9]{0:T(128)S(1)} %pad_add_fusion.1.owners, s32[528,1]{1,0:T(8,128)S(1)} %copy-done.1, f32[4,4096]{1,0:T(4,128)S(1)} %copy-done.2, ...), custom_call_target="tpu_custom_call", output_to_operand_aliasing={{0}: (10, {}), {1}: (11, {}), {2}: (12, {})} | custom-call | flops 500000000 | bytes 1000000 | tf_op jit(solution)/shard_map/gate_up_sum/pallas_call | solution.py:341
  131.5 2.0 %hidden.3 = bf16[272,1536]{1,0:T(8,128)(2,1)S(1)} custom-call(s32[9]{0:T(128)S(1)} %pad_add_fusion.1.owners, s32[528,1]{1,0:T(8,128)S(1)} %copy-done.1, f32[4,4096]{1,0:T(4,128)S(1)} %copy-done.2, bf16[512,1536]{1,0:T(8,128)(2,1)S(1)} %get-tuple-element.226.w_gate, bf16[512,1536]{1,0:T(8,128)(2,1)S(1)} %get-tuple-element.261.w_up, ...), custom_call_target="tpu_custom_call" | custom-call | flops 500000000 | bytes 1000000 | tf_op jit(solution)/shard_map/hidden/pallas_call | solution.py:369
  138.7 3.4 %collective-permute-done.46.rest_2_ = bf16[272,512]{1,0:T(8,128)(2,1)S(1)} collective-permute-done((bf16[272,512]{1,0:T(8,128)(2,1)S(1)}, bf16[272,512]{1,0:T(8,128)(2,1)S(1)}, u32[]{:S(2)}, u32[]{:S(2)}) %collective-permute-start.46) | collective-permute-done | bytes 278560 | tf_op jit(solution)/shard_map/ppermute | solution.py:526
  151.6 2.1 %collective-permute-done.50.rest_3_ = bf16[272,512]{1,0:T(8,128)(2,1)S(1)} collective-permute-done((bf16[272,512]{1,0:T(8,128)(2,1)S(1)}, bf16[272,512]{1,0:T(8,128)(2,1)S(1)}, u32[]{:S(2)}, u32[]{:S(2)}) %collective-permute-start.50) | collective-permute-done | bytes 278560 | tf_op jit(solution)/shard_map/ppermute | solution.py:530
  167.4 2.0 %collective-permute-start.57 = (bf16[272,512]{1,0:T(8,128)(2,1)S(1)}, bf16[272,512]{1,0:T(8,128)(2,1)S(1)}, u32[]{:S(2)}, u32[]{:S(2)}) collective-permute-start(bf16[272,512]{1,0:T(8,128)(2,1)S(1)} %get-tuple-element.295), channel_id=1, source_target_pairs={{0,2},{2,4},{4,6},{6,7},{7,5},{5,3},{3,1},{1,0},{8,10},{10,12},{12... | collective-permute-start | bytes 835592 | tf_op jit(solution)/shard_map/ppermute | solution.py:530
  171.9 2.1 %collective-permute-done.57.fw = bf16[272,512]{1,0:T(8,128)(2,1)S(1)} collective-permute-done((bf16[272,512]{1,0:T(8,128)(2,1)S(1)}, bf16[272,512]{1,0:T(8,128)(2,1)S(1)}, u32[]{:S(2)}, u32[]{:S(2)}) %collective-permute-start.57) | collective-permute-done | bytes 278560 | tf_op jit(solution)/shard_map/ppermute | solution.py:530
  174.0 2.0 %collective-permute-done.58.bw = bf16[272,512]{1,0:T(8,128)(2,1)S(1)} collective-permute-done((bf16[272,512]{1,0:T(8,128)(2,1)S(1)}, bf16[272,512]{1,0:T(8,128)(2,1)S(1)}, u32[]{:S(2)}, u32[]{:S(2)}) %collective-permute-start.58) | collective-permute-done | bytes 278560 | tf_op jit(solution)/shard_map/ppermute | solution.py:530
  176.0 2.1 %last_sum.1 = bf16[520,512]{1,0:T(8,128)(2,1)} custom-call(s32[9]{0:T(128)S(1)} %pad_add_fusion.1.owners, bf16[272,1536]{1,0:T(8,128)(2,1)S(1)} %hidden.3, bf16[1536,512]{1,0:T(8,128)(2,1)S(1)} %get-tuple-element.297.rest_0_.w, bf16[272,512]{1,0:T(8,128)(2,1)S(1)} %collective-permute-done.57.fw, bf16[272,512]{1,0:T(8,128)(2,1)S(1)} %collective-permute-done.58.bw, ...), custom_call_target="tpu_custom_call" | custom-call | flops 500000000 | bytes 1000000 | tf_op jit(solution)/shard_map/last_sum/pallas_call | solution.py:394
  (151 shorter events, 105.9 us)
Async XLA Ops:
  42.3 9.5 %collective-permute-start.21 = (bf16[1056,128]{1,0:T(8,128)(2,1)S(1)}, bf16[1056,128]{1,0:T(8,128)(2,1)S(1)}, u32[]{:S(2)}, u32[]{:S(2)}) collective-permute-start(bf16[1056,128]{1,0:T(8,128)(2,1)S(1)} %prefill_attention.3.rest_0_), channel_id=1, source_target_pairs={{0,2},{2,4},{4,6},{6,7},{7,5},{5,3},{3,1},{1,0},{8,10},{10,12},{12... | collective-permute-start | bytes 811016 | tf_op jit(solution)/shard_map/ppermute | solution.py:506
  43.9 9.4 %collective-permute-start.22 = (bf16[1056,128]{1,0:T(8,128)(2,1)S(1)}, bf16[1056,128]{1,0:T(8,128)(2,1)S(1)}, u32[]{:S(2)}, u32[]{:S(2)}) collective-permute-start(bf16[1056,128]{1,0:T(8,128)(2,1)S(1)} %prefill_attention.3.rest_0_), channel_id=1, source_target_pairs={{2,0},{4,2},{6,4},{7,6},{5,7},{3,5},{1,3},{0,1},{10,8},{12,10},{14... | collective-permute-start | bytes 811016 | tf_op jit(solution)/shard_map/ppermute | solution.py:507
  44.9 12.9 %collective-permute-start.19 = (bf16[1024,128]{1,0:T(8,128)(2,1)S(1)}, bf16[1024,128]{1,0:T(8,128)(2,1)S(1)}, u32[]{:S(2)}, u32[]{:S(2)}) collective-permute-start(bf16[1024,128]{1,0:T(8,128)(2,1)S(1)} %collective-permute-done.14.rest_1_), channel_id=1, source_target_pairs={{0,2},{2,4},{4,6},{6,7},{7,5},{5,3},{3,1},{1,0},{8,10},{10,12},{12... | collective-permute-start | bytes 786440 | tf_op jit(solution)/shard_map/ppermute | solution.py:506
  46.5 12.4 %collective-permute-start.20 = (bf16[1024,128]{1,0:T(8,128)(2,1)S(1)}, bf16[1024,128]{1,0:T(8,128)(2,1)S(1)}, u32[]{:S(2)}, u32[]{:S(2)}) collective-permute-start(bf16[1024,128]{1,0:T(8,128)(2,1)S(1)} %collective-permute-done.15.rest_7_), channel_id=1, source_target_pairs={{2,0},{4,2},{6,4},{7,6},{5,7},{3,5},{1,3},{0,1},{10,8},{12,10},{14... | collective-permute-start | bytes 786440 | tf_op jit(solution)/shard_map/ppermute | solution.py:507
  53.3 10.1 %collective-permute-start.25 = (bf16[1056,128]{1,0:T(8,128)(2,1)S(1)}, bf16[1056,128]{1,0:T(8,128)(2,1)S(1)}, u32[]{:S(2)}, u32[]{:S(2)}) collective-permute-start(bf16[1056,128]{1,0:T(8,128)(2,1)S(1)} %collective-permute-done.21.rest_1_), channel_id=1, source_target_pairs={{0,2},{2,4},{4,6},{6,7},{7,5},{5,3},{3,1},{1,0},{8,10},{10,12},{12... | collective-permute-start | bytes 811016 | tf_op jit(solution)/shard_map/ppermute | solution.py:506
  54.9 9.9 %collective-permute-start.26 = (bf16[1056,128]{1,0:T(8,128)(2,1)S(1)}, bf16[1056,128]{1,0:T(8,128)(2,1)S(1)}, u32[]{:S(2)}, u32[]{:S(2)}) collective-permute-start(bf16[1056,128]{1,0:T(8,128)(2,1)S(1)} %collective-permute-done.22.rest_7_), channel_id=1, source_target_pairs={{2,0},{4,2},{6,4},{7,6},{5,7},{3,5},{1,3},{0,1},{10,8},{12,10},{14... | collective-permute-start | bytes 811016 | tf_op jit(solution)/shard_map/ppermute | solution.py:507
  58.9 10.3 %collective-permute-start.23 = (bf16[1024,128]{1,0:T(8,128)(2,1)S(1)}, bf16[1024,128]{1,0:T(8,128)(2,1)S(1)}, u32[]{:S(2)}, u32[]{:S(2)}) collective-permute-start(bf16[1024,128]{1,0:T(8,128)(2,1)S(1)} %collective-permute-done.19.rest_2_), channel_id=1, source_target_pairs={{0,2},{2,4},{4,6},{6,7},{7,5},{5,3},{3,1},{1,0},{8,10},{10,12},{12... | collective-permute-start | bytes 786440 | tf_op jit(solution)/shard_map/ppermute | solution.py:506
  60.5 9.9 %collective-permute-start.24 = (bf16[1024,128]{1,0:T(8,128)(2,1)S(1)}, bf16[1024,128]{1,0:T(8,128)(2,1)S(1)}, u32[]{:S(2)}, u32[]{:S(2)}) collective-permute-start(bf16[1024,128]{1,0:T(8,128)(2,1)S(1)} %collective-permute-done.20.rest_6_), channel_id=1, source_target_pairs={{2,0},{4,2},{6,4},{7,6},{5,7},{3,5},{1,3},{0,1},{10,8},{12,10},{14... | collective-permute-start | bytes 786440 | tf_op jit(solution)/shard_map/ppermute | solution.py:507
  64.7 9.8 %collective-permute-start.28 = (bf16[1056,128]{1,0:T(8,128)(2,1)S(1)}, bf16[1056,128]{1,0:T(8,128)(2,1)S(1)}, u32[]{:S(2)}, u32[]{:S(2)}) collective-permute-start(bf16[1056,128]{1,0:T(8,128)(2,1)S(1)} %collective-permute-done.25.rest_2_), channel_id=1, source_target_pairs={{0,2},{2,4},{4,6},{6,7},{7,5},{5,3},{3,1},{1,0},{8,10},{10,12},{12... | collective-permute-start | bytes 811016 | tf_op jit(solution)/shard_map/ppermute | solution.py:506
  80.5 10.7 %collective-permute-start.33 = (bf16[256,512]{1,0:T(8,128)(2,1)S(1)}, bf16[256,512]{1,0:T(8,128)(2,1)S(1)}, u32[]{:S(2)}, u32[]{:S(2)}) collective-permute-start(bf16[256,512]{1,0:T(8,128)(2,1)S(1)} %out_projection.2.rest_5_.rest_3_), channel_id=1, source_target_pairs={{0,2},{2,4},{4,6},{6,7},{7,5},{5,3},{3,1},{1,0},{8,10},{10,12},{12... | collective-permute-start | bytes 786440 | tf_op jit(solution)/shard_map/ppermute | solution.py:506
  84.9 9.8 %collective-permute-start.31 = (bf16[272,512]{1,0:T(8,128)(2,1)S(1)}, bf16[272,512]{1,0:T(8,128)(2,1)S(1)}, u32[]{:S(2)}, u32[]{:S(2)}) collective-permute-start(bf16[272,512]{1,0:T(8,128)(2,1)S(1)} %out_projection.3.rest_6_.own), channel_id=1, source_target_pairs={{0,2},{2,4},{4,6},{6,7},{7,5},{5,3},{3,1},{1,0},{8,10},{10,12},{12... | collective-permute-start | bytes 835592 | tf_op jit(solution)/shard_map/ppermute | solution.py:506
  86.6 9.9 %collective-permute-start.32 = (bf16[272,512]{1,0:T(8,128)(2,1)S(1)}, bf16[272,512]{1,0:T(8,128)(2,1)S(1)}, u32[]{:S(2)}, u32[]{:S(2)}) collective-permute-start(bf16[272,512]{1,0:T(8,128)(2,1)S(1)} %out_projection.3.rest_6_.own), channel_id=1, source_target_pairs={{2,0},{4,2},{6,4},{7,6},{5,7},{3,5},{1,3},{0,1},{10,8},{12,10},{14... | collective-permute-start | bytes 835592 | tf_op jit(solution)/shard_map/ppermute | solution.py:507
  91.2 12.7 %collective-permute-start.37 = (bf16[256,512]{1,0:T(8,128)(2,1)S(1)}, bf16[256,512]{1,0:T(8,128)(2,1)S(1)}, u32[]{:S(2)}, u32[]{:S(2)}) collective-permute-start(bf16[256,512]{1,0:T(8,128)(2,1)S(1)} %collective-permute-done.33.rest_5_), channel_id=1, source_target_pairs={{0,2},{2,4},{4,6},{6,7},{7,5},{5,3},{3,1},{1,0},{8,10},{10,12},{12... | collective-permute-start | bytes 786440 | tf_op jit(solution)/shard_map/ppermute | solution.py:506
  92.8 11.1 %collective-permute-start.38 = (bf16[256,512]{1,0:T(8,128)(2,1)S(1)}, bf16[256,512]{1,0:T(8,128)(2,1)S(1)}, u32[]{:S(2)}, u32[]{:S(2)}) collective-permute-start(bf16[256,512]{1,0:T(8,128)(2,1)S(1)} %collective-permute-done.34.rest_7_), channel_id=1, source_target_pairs={{2,0},{4,2},{6,4},{7,6},{5,7},{3,5},{1,3},{0,1},{10,8},{12,10},{14... | collective-permute-start | bytes 786440 | tf_op jit(solution)/shard_map/ppermute | solution.py:507
  96.5 10.0 %collective-permute-start.35 = (bf16[272,512]{1,0:T(8,128)(2,1)S(1)}, bf16[272,512]{1,0:T(8,128)(2,1)S(1)}, u32[]{:S(2)}, u32[]{:S(2)}) collective-permute-start(bf16[272,512]{1,0:T(8,128)(2,1)S(1)} %collective-permute-done.31.rest_6_), channel_id=1, source_target_pairs={{0,2},{2,4},{4,6},{6,7},{7,5},{5,3},{3,1},{1,0},{8,10},{10,12},{12... | collective-permute-start | bytes 835592 | tf_op jit(solution)/shard_map/ppermute | solution.py:506
  98.0 10.0 %collective-permute-start.36 = (bf16[272,512]{1,0:T(8,128)(2,1)S(1)}, bf16[272,512]{1,0:T(8,128)(2,1)S(1)}, u32[]{:S(2)}, u32[]{:S(2)}) collective-permute-start(bf16[272,512]{1,0:T(8,128)(2,1)S(1)} %collective-permute-done.32.rest_8_), channel_id=1, source_target_pairs={{2,0},{4,2},{6,4},{7,6},{5,7},{3,5},{1,3},{0,1},{10,8},{12,10},{14... | collective-permute-start | bytes 835592 | tf_op jit(solution)/shard_map/ppermute | solution.py:507
  103.9 13.5 %collective-permute-start.39 = (bf16[256,512]{1,0:T(8,128)(2,1)S(1)}, bf16[256,512]{1,0:T(8,128)(2,1)S(1)}, u32[]{:S(2)}, u32[]{:S(2)}) collective-permute-start(bf16[256,512]{1,0:T(8,128)(2,1)S(1)} %collective-permute-done.37.rest_5_), channel_id=1, source_target_pairs={{0,2},{2,4},{4,6},{6,7},{7,5},{5,3},{3,1},{1,0},{8,10},{10,12},{12... | collective-permute-start | bytes 786440 | tf_op jit(solution)/shard_map/ppermute | solution.py:506
  105.5 11.9 %collective-permute-start.40 = (bf16[256,512]{1,0:T(8,128)(2,1)S(1)}, bf16[256,512]{1,0:T(8,128)(2,1)S(1)}, u32[]{:S(2)}, u32[]{:S(2)}) collective-permute-start(bf16[256,512]{1,0:T(8,128)(2,1)S(1)} %collective-permute-done.38.rest_7_), channel_id=1, source_target_pairs={{2,0},{4,2},{6,4},{7,6},{5,7},{3,5},{1,3},{0,1},{10,8},{12,10},{14... | collective-permute-start | bytes 786440 | tf_op jit(solution)/shard_map/ppermute | solution.py:507
  108.0 11.1 %collective-permute-start.42 = (bf16[272,512]{1,0:T(8,128)(2,1)S(1)}, bf16[272,512]{1,0:T(8,128)(2,1)S(1)}, u32[]{:S(2)}, u32[]{:S(2)}) collective-permute-start(bf16[272,512]{1,0:T(8,128)(2,1)S(1)} %collective-permute-done.35.rest_6_), channel_id=1, source_target_pairs={{0,2},{2,4},{4,6},{6,7},{7,5},{5,3},{3,1},{1,0},{8,10},{10,12},{12... | collective-permute-start | bytes 835592 | tf_op jit(solution)/shard_map/ppermute | solution.py:506
  109.7 9.4 %collective-permute-start.43 = (bf16[272,512]{1,0:T(8,128)(2,1)S(1)}, bf16[272,512]{1,0:T(8,128)(2,1)S(1)}, u32[]{:S(2)}, u32[]{:S(2)}) collective-permute-start(bf16[272,512]{1,0:T(8,128)(2,1)S(1)} %collective-permute-done.36.rest_8_), channel_id=1, source_target_pairs={{2,0},{4,2},{6,4},{7,6},{5,7},{3,5},{1,3},{0,1},{10,8},{12,10},{14... | collective-permute-start | bytes 835592 | tf_op jit(solution)/shard_map/ppermute | solution.py:507
  119.1 12.4 %collective-permute-start.44 = (bf16[272,512]{1,0:T(8,128)(2,1)S(1)}, bf16[272,512]{1,0:T(8,128)(2,1)S(1)}, u32[]{:S(2)}, u32[]{:S(2)}) collective-permute-start(bf16[272,512]{1,0:T(8,128)(2,1)S(1)} %collective-permute-done.43.rest_6_), channel_id=1, source_target_pairs={{2,0},{4,2},{6,4},{7,6},{5,7},{3,5},{1,3},{0,1},{10,8},{12,10},{14... | collective-permute-start | bytes 835592 | tf_op jit(solution)/shard_map/ppermute | solution.py:504
  138.3 9.4 %collective-permute-start.48 = (bf16[256,512]{1,0:T(8,128)(2,1)S(1)}, bf16[256,512]{1,0:T(8,128)(2,1)S(1)}, u32[]{:S(2)}, u32[]{:S(2)}) collective-permute-start(bf16[256,512]{1,0:T(8,128)(2,1)S(1)} %get-tuple-element.283), channel_id=1, source_target_pairs={{2,0},{4,2},{6,4},{7,6},{5,7},{3,5},{1,3},{0,1},{10,8},{12,10},{14... | collective-permute-start | bytes 786440 | tf_op jit(solution)/shard_map/ppermute | solution.py:530
  149.3 9.2 %collective-permute-start.51 = (bf16[256,512]{1,0:T(8,128)(2,1)S(1)}, bf16[256,512]{1,0:T(8,128)(2,1)S(1)}, u32[]{:S(2)}, u32[]{:S(2)}) collective-permute-start(bf16[256,512]{1,0:T(8,128)(2,1)S(1)} %get-tuple-element.284), channel_id=1, source_target_pairs={{0,2},{2,4},{4,6},{6,7},{7,5},{5,3},{3,1},{1,0},{8,10},{10,12},{12... | collective-permute-start | bytes 786440 | tf_op jit(solution)/shard_map/ppermute | solution.py:530
  151.2 9.2 %collective-permute-start.52 = (bf16[256,512]{1,0:T(8,128)(2,1)S(1)}, bf16[256,512]{1,0:T(8,128)(2,1)S(1)}, u32[]{:S(2)}, u32[]{:S(2)}) collective-permute-start(bf16[256,512]{1,0:T(8,128)(2,1)S(1)} %get-tuple-element.291), channel_id=1, source_target_pairs={{2,0},{4,2},{6,4},{7,6},{5,7},{3,5},{1,3},{0,1},{10,8},{12,10},{14... | collective-permute-start | bytes 786440 | tf_op jit(solution)/shard_map/ppermute | solution.py:530
  (43 other events, 406.3 us)

commit v6 on v5

--- a/solution.py
+++ b/solution.py
@@ -377,30 +377,52 @@
     )(owners, tenants, gain, *w, part, *held)
 
 
-def assemble_kernel(n, rows, owners, hidden, w, fw, bw, own, top, out, block):
+def last_block(hidden, w, fw, bw, own):
     total = jnp.dot(hidden[...], w[...], preferred_element_type=F32)
-    total = total + fw[...].astype(F32) + bw[...].astype(F32) + own[...].astype(F32)
+    return total + fw[...].astype(F32) + bw[...].astype(F32) + own[...].astype(F32)
+
+
+def place_kernel(n, rows, owners, hidden, w, fw, bw, own, hidden_b, own_b, block, part):
+    part[...] = jnp.dot(hidden_b[...], w[...], preferred_element_type=F32) + own_b[...].astype(F32)
+    total = last_block(hidden, w, fw, bw, own)
     local = block.shape[0] // n
     for b in range(n):
-        at = b * local
-        block[at : at + rows, :] = top[b * rows : (b + 1) * rows, :].astype(F32)
-        block[at + rows : at + 2 * rows, :] = total[b * rows : (b + 1) * rows, :]
-        block[at + 2 * rows : at + local, :] = total[n * rows + b : n * rows + b + 1, :]
+        block[b * local : b * local + rows, :] = total[b * rows : (b + 1) * rows, :]
+
+
+def put_rows(n, rows, owners, hidden, w, arrived, own, hidden_b, own_b):
+    return pl.pallas_call(
+        functools.partial(place_kernel, n, rows),
+        out_shape=[pltpu.VMEM((n * (2 * rows + 1), own.shape[1]), F32), pltpu.VMEM(own_b.shape, F32)],
+        in_specs=[SMEM] + [VMEM] * 7,
+        out_specs=[VMEM, VMEM],
+        compiler_params=params(16),
+        cost_estimate=STEP,
+        name="place_sum",
+    )(owners, hidden, w, *arrived, own, hidden_b, own_b)
+
+
+def assemble_kernel(n, rows, owners, fw, bw, part, placed, out, block):
+    total = part[...] + fw[...].astype(F32) + bw[...].astype(F32)
+    local = block.shape[0] // n
+    for b in range(n):
+        at = b * local + rows
+        block[at : at + rows, :] = total[b * rows : (b + 1) * rows, :]
+        block[at + rows : at + rows + 1, :] = total[n * rows + b : n * rows + b + 1, :]
     out[...] = block[...].astype(BF16)
 
 
-def assemble(n, rows, owners, hidden, w, arrived, own, top):
-    shape = (n * (2 * rows + 1), top.shape[1])
+def assemble(n, rows, owners, arrived, part, placed):
     return pl.pallas_call(
         functools.partial(assemble_kernel, n, rows),
-        out_shape=jax.ShapeDtypeStruct(shape, BF16),
-        in_specs=[SMEM] + [VMEM] * 6,
-        out_specs=VMEM,
-        scratch_shapes=[pltpu.VMEM(shape, F32)],
+        out_shape=[jax.ShapeDtypeStruct(placed.shape, BF16), pltpu.VMEM(placed.shape, F32)],
+        in_specs=[SMEM] + [VMEM] * 4,
+        out_specs=[VMEM, VMEM],
+        input_output_aliases={4: 1},
         compiler_params=params(16),
         cost_estimate=STEP,
         name="last_sum",
-    )(owners, hidden, w, *arrived, own, top)
+    )(owners, *arrived, part, placed)[0]
 
 
 def down_kernel(flags, own, owners, hidden, *rest):
@@ -682,8 +704,11 @@
     for _ in range(1, half):
         sum_a.hop()
         sum_b.hop()
-    out_a = sum_a.finish()
-    return assemble(n, rows, run.after(), hid_b, store["down", 0], sum_b.arrived, mixed_b, out_a)
+    out_a, part_b = put_rows(
+        n, rows, run.after(), hid_a, store["down", 0], sum_a.arrived, mixed_a, hid_b, mixed_b
+    )
+    run.mark(out_a)
+    return assemble(n, rows, run.after(), sum_b.arrived, part_b, out_a)
 
 
 def solution(mesh):

time: 178 us -> 178 us (level)
    pallas_call x9 -> x8, Pallas kernels: 12.6 us -> 11.5 us  [down(): pl.pallas_call(functools.partial(down_kernel, flags, len(own)), out_shape...]
where the time goes in v6:
time: 178 us
  Pallas kernels  70.9 us (40%)
  starting transfers between devices  60.7 us (34%)
  waiting for transfers between devices  42.6 us (24%)
    ppermute x21, starting transfers between devices, hop(): chain.ahead.append(lax.ppermute(f, 'tok', chain.fw))  35.5 us
    pallas_call x5, Pallas kernels, feed(): pl.pallas_call(functools.partial(feed_kernel, lo, hi, shares, len(held) >...  23.9 us
    ppermute x21, waiting for transfers between devices, hop(): chain.behind.append(lax.ppermute(b, 'tok', chain.bw))  14.7 us
    pallas_call x5, Pallas kernels, fetch_early(): pl.pallas_call(functools.partial(fetch_kernel, fetch), out_shape=shapes,...  12.7 us
    pallas_call x8, Pallas kernels, down(): pl.pallas_call(functools.partial(down_kernel, flags, len(own)), out_shape...  11.5 us
    ppermute x6, starting transfers between devices, hop(): lax.ppermute(out[0], 'tok', chain.fw)  10.6 us
    ppermute x6, waiting for transfers between devices, hop(): lax.ppermute(out[1], 'tok', chain.bw)  10.5 us
    ppermute x21, waiting for transfers between devices, hop(): chain.ahead.append(lax.ppermute(f, 'tok', chain.fw))  10.4 us
  transfers between devices with their start and end apart: 59, of which 34 were waited for; matrix products, arithmetic and copies ran while one was open for 1% of the time, Pallas kernels for 38%

profile of v6, /device:TPU:0, one launch (start us, length us, event | category | flops | bytes accessed | tf_op | source)
XLA Modules:
  0.0 177.5 jit_solution(6344145407374408382)
XLA Ops:
  1.1 3.1 %collective-permute-start = (bf16[544,128]{1,0:T(8,128)(2,1)S(1)}, bf16[544,128]{1,0:T(8,128)(2,1)S(1)}, u32[]{:S(2)}, u32[]{:S(2)}) collective-permute-start(bf16[544,128]{1,0:T(8,128)(2,1)S(1)} %get-tuple-element.160.rest_0_), channel_id=1, source_target_pairs={{0,2},{2,4},{4,6},{6,7},{7,5},{5,3},{3,1},{1,0},{8,10},{10,12},{12... | collective-permute-start | bytes 417800 | tf_op jit(solution)/shard_map/ppermute | solution.py:528
  4.2 2.0 %collective-permute-start.4 = (bf16[512,128]{1,0:T(8,128)(2,1)S(1)}, bf16[512,128]{1,0:T(8,128)(2,1)S(1)}, u32[]{:S(2)}, u32[]{:S(2)}) collective-permute-start(bf16[512,128]{1,0:T(8,128)(2,1)S(1)} %get-tuple-element.169.rest_8_), channel_id=1, source_target_pairs={{0,2},{2,4},{4,6},{6,7},{7,5},{5,3},{3,1},{1,0},{8,10},{10,12},{12... | collective-permute-start | bytes 393224 | tf_op jit(solution)/shard_map/ppermute | solution.py:528
  32.7 3.0 %prefill_attention.2.rest_0_ = bf16[1024,128]{1,0:T(8,128)(2,1)S(1)} custom-call(s32[9]{0:T(128)S(1)} %pad_add_fusion.1.owners, bf16[64,4096]{1,0:T(8,128)(2,1)S(1)} %copy-done.5, s32[1,512]{1,0:T(1,128)S(1)} %copy-done.6, bf16[544,128]{1,0:T(8,128)(2,1)S(1)} %get-tuple-element.160.rest_0_, bf16[544,128]{1,0:T(8,128)(2,1)S(1)} %collective-permute-done.rest_1_, ...), custom_call_target="tpu_custom_call" | custom-call | flops 500000000 | bytes 1000000 | tf_op jit(solution)/shard_map/prefill_attention/pallas_call | solution.py:114
  39.3 3.0 %prefill_attention.3.rest_0_ = bf16[1056,128]{1,0:T(8,128)(2,1)S(1)} custom-call(s32[9]{0:T(128)S(1)} %pad_add_fusion.1.owners, bf16[64,4096]{1,0:T(8,128)(2,1)S(1)} %copy-done.5, s32[1,512]{1,0:T(1,128)S(1)} %copy-done.6, bf16[544,128]{1,0:T(8,128)(2,1)S(1)} %get-tuple-element.160.rest_0_, bf16[544,128]{1,0:T(8,128)(2,1)S(1)} %collective-permute-done.rest_1_, ...), custom_call_target="tpu_custom_call" | custom-call | flops 500000000 | bytes 1000000 | tf_op jit(solution)/shard_map/prefill_attention/pallas_call | solution.py:114
  46.9 2.9 %fetch_weights.5 = (bf16[1536,512]{1,0:T(8,128)(2,1)S(1)}, bf16[1536,512]{1,0:T(8,128)(2,1)S(1)}, bf16[1536,512]{1,0:T(8,128)(2,1)S(1)}) custom-call(s32[9]{0:T(128)S(1)} %pad_add_fusion.1.owners, bf16[4096,1536]{1,0:T(8,128)(2,1)} %rest_0_.19, bf16[4096,1536]{1,0:T(8,128)(2,1)} %rest_1_.19, bf16[1536,4096]{1,0:T(8,128)(2,1)} %rest_2_.19), custom_call_target="tpu_custom_call" | custom-call | flops 500000000 | bytes 1000000 | tf_op jit(solution)/shard_map/fetch_weights/pallas_call | solution.py:245
  55.4 2.4 %fetch_weights.6 = (bf16[512,1536]{1,0:T(8,128)(2,1)S(1)}, bf16[512,1536]{1,0:T(8,128)(2,1)S(1)}) custom-call(s32[9]{0:T(128)S(1)} %pad_add_fusion.1.owners, bf16[4096,1536]{1,0:T(8,128)(2,1)} %rest_0_.19, bf16[4096,1536]{1,0:T(8,128)(2,1)} %rest_1_.19, bf16[1536,4096]{1,0:T(8,128)(2,1)} %rest_2_.19), custom_call_target="tpu_custom_call" | custom-call | flops 500000000 | bytes 1000000 | tf_op jit(solution)/shard_map/fetch_weights/pallas_call | solution.py:245
  61.0 2.4 %fetch_weights.7.rest_3_ = bf16[1024,1536]{1,0:T(8,128)(2,1)S(1)} custom-call(s32[9]{0:T(128)S(1)} %pad_add_fusion.1.owners, bf16[4096,1536]{1,0:T(8,128)(2,1)} %rest_0_.19, bf16[4096,1536]{1,0:T(8,128)(2,1)} %rest_1_.19, bf16[1536,4096]{1,0:T(8,128)(2,1)} %rest_2_.19), custom_call_target="tpu_custom_call" | custom-call | flops 500000000 | bytes 1000000 | tf_op jit(solution)/shard_map/fetch_weights/pallas_call | solution.py:245
  66.8 2.4 %fetch_weights.8.rest_4_ = bf16[1024,1536]{1,0:T(8,128)(2,1)S(1)} custom-call(s32[9]{0:T(128)S(1)} %pad_add_fusion.1.owners, bf16[4096,1536]{1,0:T(8,128)(2,1)} %rest_0_.19, bf16[4096,1536]{1,0:T(8,128)(2,1)} %rest_1_.19, bf16[1536,4096]{1,0:T(8,128)(2,1)} %rest_2_.19), custom_call_target="tpu_custom_call" | custom-call | flops 500000000 | bytes 1000000 | tf_op jit(solution)/shard_map/fetch_weights/pallas_call | solution.py:245
  72.0 2.4 %fetch_weights.9 = (bf16[512,1536]{1,0:T(8,128)(2,1)S(1)}, bf16[512,1536]{1,0:T(8,128)(2,1)S(1)}) custom-call(s32[9]{0:T(128)S(1)} %pad_add_fusion.1.owners, bf16[4096,1536]{1,0:T(8,128)(2,1)} %rest_0_.19, bf16[4096,1536]{1,0:T(8,128)(2,1)} %rest_1_.19, bf16[1536,4096]{1,0:T(8,128)(2,1)} %rest_2_.19), custom_call_target="tpu_custom_call" | custom-call | flops 500000000 | bytes 1000000 | tf_op jit(solution)/shard_map/fetch_weights/pallas_call | solution.py:245
  75.0 3.3 %collective-permute-done.27.rest_4_ = bf16[1024,128]{1,0:T(8,128)(2,1)S(1)} collective-permute-done((bf16[1024,128]{1,0:T(8,128)(2,1)S(1)}, bf16[1024,128]{1,0:T(8,128)(2,1)S(1)}, u32[]{:S(2)}, u32[]{:S(2)}) %collective-permute-start.27) | collective-permute-done | bytes 262176 | tf_op jit(solution)/shard_map/ppermute | solution.py:524
  78.3 2.2 %out_projection.2.rest_5_.own = bf16[256,512]{1,0:T(8,128)(2,1)S(1)} custom-call(s32[9]{0:T(128)S(1)} %pad_add_fusion.1.owners, bf16[1024,128]{1,0:T(8,128)(2,1)S(1)} %prefill_attention.2.rest_0_, bf16[1024,128]{1,0:T(8,128)(2,1)S(1)} %collective-permute-done.14.rest_1_, bf16[1024,128]{1,0:T(8,128)(2,1)S(1)} %collective-permute-done.19.rest_2_, ...), custom_call_target="tpu_custom_call" | custom-call | flops 500000000 | bytes 1000000 | tf_op jit(solution)/shard_map/out_projection/pallas_call | solution.py:286
  82.6 2.3 %out_projection.3.rest_6_.own_b = bf16[272,512]{1,0:T(8,128)(2,1)S(1)} custom-call(s32[9]{0:T(128)S(1)} %pad_add_fusion.1.owners, bf16[1056,128]{1,0:T(8,128)(2,1)S(1)} %prefill_attention.3.rest_0_, bf16[1056,128]{1,0:T(8,128)(2,1)S(1)} %collective-permute-done.21.rest_1_, bf16[1056,128]{1,0:T(8,128)(2,1)S(1)} %collective-permute-done.25.rest_2_, ...), custom_call_target="tpu_custom_call" | custom-call | flops 500000000 | bytes 1000000 | tf_op jit(solution)/shard_map/out_projection/pallas_call | solution.py:286
  87.0 4.2 %gate_up_sum.5 = (f32[528,1536]{1,0:T(8,128)S(1)}, f32[528,1536]{1,0:T(8,128)S(1)}, f32[528,128]{1,0:T(8,128)S(1)}, bf16[1024,1536]{1,0:T(8,128)(2,1)S(1)}) custom-call(s32[9]{0:T(128)S(1)} %pad_add_fusion.1.owners, s32[528,1]{1,0:T(8,128)S(1)} %copy-done.1, f32[4,4096]{1,0:T(4,128)S(1)} %copy-done.2, bf16[4096,1536]{1,0:T(8,128)(2,1)} %rest_0_.19, ...), custom_call_target="tpu_custom_call" | custom-call | flops 500000000 | bytes 1000000 | tf_op jit(solution)/shard_map/gate_up_sum/pallas_call | solution.py:341
  98.5 5.4 %gate_up_sum.6 = (f32[528,1536]{1,0:T(8,128)S(1)}, f32[528,1536]{1,0:T(8,128)S(1)}, f32[528,128]{1,0:T(8,128)S(1)}, bf16[1024,1536]{1,0:T(8,128)(2,1)S(1)}, bf16[1024,1536]{1,0:T(8,128)(2,1)S(1)}) custom-call(s32[9]{0:T(128)S(1)} %pad_add_fusion.1.owners, s32[528,1]{1,0:T(8,128)S(1)} %copy-done.1, ...), custom_call_target="tpu_custom_call", output_to_operand_aliasing={{0}: (12, {}), {1}: (13, {}), {2}: (14, {})} | custom-call | flops 500000000 | bytes 1000000 | tf_op jit(solution)/shard_map/gate_up_sum/pallas_call | solution.py:341
  110.1 7.3 %gate_up_sum.7 = (f32[528,1536]{1,0:T(8,128)S(1)}, f32[528,1536]{1,0:T(8,128)S(1)}, f32[528,128]{1,0:T(8,128)S(1)}, bf16[1024,1536]{1,0:T(8,128)(2,1)S(1)}, bf16...) custom-call(s32[9]{0:T(128)S(1)} %pad_add_fusion.1.owners, ...), custom_call_target="tpu_custom_call", output_to_operand_aliasing={{0}: (12, {}), {1}: (13, {}), {2}: (14, {})} | custom-call | flops 500000000 | bytes 1000000 | tf_op jit(solution)/shard_map/gate_up_sum/pallas_call | solution.py:341
  119.5 4.3 %gate_up_sum.8 = (f32[528,1536]{1,0:T(8,128)S(1)}, f32[528,1536]{1,0:T(8,128)S(1)}, f32[528,128]{1,0:T(8,128)S(1)}, bf16[1536,512]{1,0:T(8,128)(2,1)S(1)}, bf16[1536,512]{1,0:T(8,128)(2,1)S(1)}) custom-call(s32[9]{0:T(128)S(1)} %pad_add_fusion.1.owners, s32[528,1]{1,0:T(8,128)S(1)} %copy-done.1, ...), custom_call_target="tpu_custom_call", output_to_operand_aliasing={{0}: (10, {}), {1}: (11, {}), {2}: (12, {})} | custom-call | flops 500000000 | bytes 1000000 | tf_op jit(solution)/shard_map/gate_up_sum/pallas_call | solution.py:341
  128.7 2.8 %gate_up_sum.9 = (f32[528,1536]{1,0:T(8,128)S(1)}, f32[528,1536]{1,0:T(8,128)S(1)}, f32[528,128]{1,0:T(8,128)S(1)}, bf16[1536,512]{1,0:T(8,128)(2,1)S(1)}) custom-call(s32[9]{0:T(128)S(1)} %pad_add_fusion.1.owners, s32[528,1]{1,0:T(8,128)S(1)} %copy-done.1, f32[4,4096]{1,0:T(4,128)S(1)} %copy-done.2, ...), custom_call_target="tpu_custom_call", output_to_operand_aliasing={{0}: (10, {}), {1}: (11, {}), {2}: (12, {})} | custom-call | flops 500000000 | bytes 1000000 | tf_op jit(solution)/shard_map/gate_up_sum/pallas_call | solution.py:341
  131.5 2.0 %hidden.3.hidden_b = bf16[272,1536]{1,0:T(8,128)(2,1)S(1)} custom-call(s32[9]{0:T(128)S(1)} %pad_add_fusion.1.owners, s32[528,1]{1,0:T(8,128)S(1)} %copy-done.1, f32[4,4096]{1,0:T(4,128)S(1)} %copy-done.2, bf16[512,1536]{1,0:T(8,128)(2,1)S(1)} %get-tuple-element.229.w_gate, bf16[512,1536]{1,0:T(8,128)(2,1)S(1)} %get-tuple-element.264.w_up, ...), custom_call_target="tpu_custom_call" | custom-call | flops 500000000 | bytes 1000000 | tf_op jit(solution)/shard_map/hidden/pallas_call | solution.py:369
  138.7 3.4 %collective-permute-done.46.rest_2_ = bf16[272,512]{1,0:T(8,128)(2,1)S(1)} collective-permute-done((bf16[272,512]{1,0:T(8,128)(2,1)S(1)}, bf16[272,512]{1,0:T(8,128)(2,1)S(1)}, u32[]{:S(2)}, u32[]{:S(2)}) %collective-permute-start.46) | collective-permute-done | bytes 278560 | tf_op jit(solution)/shard_map/ppermute | solution.py:548
  143.7 1.9 %collective-permute-start.49 = (bf16[272,512]{1,0:T(8,128)(2,1)S(1)}, bf16[272,512]{1,0:T(8,128)(2,1)S(1)}, u32[]{:S(2)}, u32[]{:S(2)}) collective-permute-start(bf16[272,512]{1,0:T(8,128)(2,1)S(1)} %get-tuple-element.282), channel_id=1, source_target_pairs={{0,2},{2,4},{4,6},{6,7},{7,5},{5,3},{3,1},{1,0},{8,10},{10,12},{12... | collective-permute-start | bytes 835592 | tf_op jit(solution)/shard_map/ppermute | solution.py:552
  149.2 1.9 %collective-permute-start.51 = (bf16[256,512]{1,0:T(8,128)(2,1)S(1)}, bf16[256,512]{1,0:T(8,128)(2,1)S(1)}, u32[]{:S(2)}, u32[]{:S(2)}) collective-permute-start(bf16[256,512]{1,0:T(8,128)(2,1)S(1)} %get-tuple-element.287), channel_id=1, source_target_pairs={{0,2},{2,4},{4,6},{6,7},{7,5},{5,3},{3,1},{1,0},{8,10},{10,12},{12... | collective-permute-start | bytes 786440 | tf_op jit(solution)/shard_map/ppermute | solution.py:552
  151.6 2.1 %collective-permute-done.50.rest_3_ = bf16[272,512]{1,0:T(8,128)(2,1)S(1)} collective-permute-done((bf16[272,512]{1,0:T(8,128)(2,1)S(1)}, bf16[272,512]{1,0:T(8,128)(2,1)S(1)}, u32[]{:S(2)}, u32[]{:S(2)}) %collective-permute-start.50) | collective-permute-done | bytes 278560 | tf_op jit(solution)/shard_map/ppermute | solution.py:552
  158.5 1.9 %collective-permute-done.52.rest_3_ = bf16[256,512]{1,0:T(8,128)(2,1)S(1)} collective-permute-done((bf16[256,512]{1,0:T(8,128)(2,1)S(1)}, bf16[256,512]{1,0:T(8,128)(2,1)S(1)}, u32[]{:S(2)}, u32[]{:S(2)}) %collective-permute-start.52) | collective-permute-done | bytes 262176 | tf_op jit(solution)/shard_map/ppermute | solution.py:552
  167.4 2.0 %collective-permute-start.57 = (bf16[272,512]{1,0:T(8,128)(2,1)S(1)}, bf16[272,512]{1,0:T(8,128)(2,1)S(1)}, u32[]{:S(2)}, u32[]{:S(2)}) collective-permute-start(bf16[272,512]{1,0:T(8,128)(2,1)S(1)} %get-tuple-element.298), channel_id=1, source_target_pairs={{0,2},{2,4},{4,6},{6,7},{7,5},{5,3},{3,1},{1,0},{8,10},{10,12},{12... | collective-permute-start | bytes 835592 | tf_op jit(solution)/shard_map/ppermute | solution.py:552
  (151 shorter events, 105.8 us)
Async XLA Ops:
  42.3 9.5 %collective-permute-start.21 = (bf16[1056,128]{1,0:T(8,128)(2,1)S(1)}, bf16[1056,128]{1,0:T(8,128)(2,1)S(1)}, u32[]{:S(2)}, u32[]{:S(2)}) collective-permute-start(bf16[1056,128]{1,0:T(8,128)(2,1)S(1)} %prefill_attention.3.rest_0_), channel_id=1, source_target_pairs={{0,2},{2,4},{4,6},{6,7},{7,5},{5,3},{3,1},{1,0},{8,10},{10,12},{12... | collective-permute-start | bytes 811016 | tf_op jit(solution)/shard_map/ppermute | solution.py:528
  43.9 9.4 %collective-permute-start.22 = (bf16[1056,128]{1,0:T(8,128)(2,1)S(1)}, bf16[1056,128]{1,0:T(8,128)(2,1)S(1)}, u32[]{:S(2)}, u32[]{:S(2)}) collective-permute-start(bf16[1056,128]{1,0:T(8,128)(2,1)S(1)} %prefill_attention.3.rest_0_), channel_id=1, source_target_pairs={{2,0},{4,2},{6,4},{7,6},{5,7},{3,5},{1,3},{0,1},{10,8},{12,10},{14... | collective-permute-start | bytes 811016 | tf_op jit(solution)/shard_map/ppermute | solution.py:529
  44.9 12.9 %collective-permute-start.19 = (bf16[1024,128]{1,0:T(8,128)(2,1)S(1)}, bf16[1024,128]{1,0:T(8,128)(2,1)S(1)}, u32[]{:S(2)}, u32[]{:S(2)}) collective-permute-start(bf16[1024,128]{1,0:T(8,128)(2,1)S(1)} %collective-permute-done.14.rest_1_), channel_id=1, source_target_pairs={{0,2},{2,4},{4,6},{6,7},{7,5},{5,3},{3,1},{1,0},{8,10},{10,12},{12... | collective-permute-start | bytes 786440 | tf_op jit(solution)/shard_map/ppermute | solution.py:528
  46.5 12.4 %collective-permute-start.20 = (bf16[1024,128]{1,0:T(8,128)(2,1)S(1)}, bf16[1024,128]{1,0:T(8,128)(2,1)S(1)}, u32[]{:S(2)}, u32[]{:S(2)}) collective-permute-start(bf16[1024,128]{1,0:T(8,128)(2,1)S(1)} %collective-permute-done.15.rest_7_), channel_id=1, source_target_pairs={{2,0},{4,2},{6,4},{7,6},{5,7},{3,5},{1,3},{0,1},{10,8},{12,10},{14... | collective-permute-start | bytes 786440 | tf_op jit(solution)/shard_map/ppermute | solution.py:529
  53.3 10.1 %collective-permute-start.25 = (bf16[1056,128]{1,0:T(8,128)(2,1)S(1)}, bf16[1056,128]{1,0:T(8,128)(2,1)S(1)}, u32[]{:S(2)}, u32[]{:S(2)}) collective-permute-start(bf16[1056,128]{1,0:T(8,128)(2,1)S(1)} %collective-permute-done.21.rest_1_), channel_id=1, source_target_pairs={{0,2},{2,4},{4,6},{6,7},{7,5},{5,3},{3,1},{1,0},{8,10},{10,12},{12... | collective-permute-start | bytes 811016 | tf_op jit(solution)/shard_map/ppermute | solution.py:528
  54.9 9.8 %collective-permute-start.26 = (bf16[1056,128]{1,0:T(8,128)(2,1)S(1)}, bf16[1056,128]{1,0:T(8,128)(2,1)S(1)}, u32[]{:S(2)}, u32[]{:S(2)}) collective-permute-start(bf16[1056,128]{1,0:T(8,128)(2,1)S(1)} %collective-permute-done.22.rest_7_), channel_id=1, source_target_pairs={{2,0},{4,2},{6,4},{7,6},{5,7},{3,5},{1,3},{0,1},{10,8},{12,10},{14... | collective-permute-start | bytes 811016 | tf_op jit(solution)/shard_map/ppermute | solution.py:529
  58.9 10.3 %collective-permute-start.23 = (bf16[1024,128]{1,0:T(8,128)(2,1)S(1)}, bf16[1024,128]{1,0:T(8,128)(2,1)S(1)}, u32[]{:S(2)}, u32[]{:S(2)}) collective-permute-start(bf16[1024,128]{1,0:T(8,128)(2,1)S(1)} %collective-permute-done.19.rest_2_), channel_id=1, source_target_pairs={{0,2},{2,4},{4,6},{6,7},{7,5},{5,3},{3,1},{1,0},{8,10},{10,12},{12... | collective-permute-start | bytes 786440 | tf_op jit(solution)/shard_map/ppermute | solution.py:528
  60.5 9.8 %collective-permute-start.24 = (bf16[1024,128]{1,0:T(8,128)(2,1)S(1)}, bf16[1024,128]{1,0:T(8,128)(2,1)S(1)}, u32[]{:S(2)}, u32[]{:S(2)}) collective-permute-start(bf16[1024,128]{1,0:T(8,128)(2,1)S(1)} %collective-permute-done.20.rest_6_), channel_id=1, source_target_pairs={{2,0},{4,2},{6,4},{7,6},{5,7},{3,5},{1,3},{0,1},{10,8},{12,10},{14... | collective-permute-start | bytes 786440 | tf_op jit(solution)/shard_map/ppermute | solution.py:529
  64.7 9.8 %collective-permute-start.28 = (bf16[1056,128]{1,0:T(8,128)(2,1)S(1)}, bf16[1056,128]{1,0:T(8,128)(2,1)S(1)}, u32[]{:S(2)}, u32[]{:S(2)}) collective-permute-start(bf16[1056,128]{1,0:T(8,128)(2,1)S(1)} %collective-permute-done.25.rest_2_), channel_id=1, source_target_pairs={{0,2},{2,4},{4,6},{6,7},{7,5},{5,3},{3,1},{1,0},{8,10},{10,12},{12... | collective-permute-start | bytes 811016 | tf_op jit(solution)/shard_map/ppermute | solution.py:528
  80.5 10.7 %collective-permute-start.33 = (bf16[256,512]{1,0:T(8,128)(2,1)S(1)}, bf16[256,512]{1,0:T(8,128)(2,1)S(1)}, u32[]{:S(2)}, u32[]{:S(2)}) collective-permute-start(bf16[256,512]{1,0:T(8,128)(2,1)S(1)} %out_projection.2.rest_5_.own), channel_id=1, source_target_pairs={{0,2},{2,4},{4,6},{6,7},{7,5},{5,3},{3,1},{1,0},{8,10},{10,12},{12... | collective-permute-start | bytes 786440 | tf_op jit(solution)/shard_map/ppermute | solution.py:528
  84.9 9.8 %collective-permute-start.31 = (bf16[272,512]{1,0:T(8,128)(2,1)S(1)}, bf16[272,512]{1,0:T(8,128)(2,1)S(1)}, u32[]{:S(2)}, u32[]{:S(2)}) collective-permute-start(bf16[272,512]{1,0:T(8,128)(2,1)S(1)} %out_projection.3.rest_6_.own_b), channel_id=1, source_target_pairs={{0,2},{2,4},{4,6},{6,7},{7,5},{5,3},{3,1},{1,0},{8,10},{10,12},{12... | collective-permute-start | bytes 835592 | tf_op jit(solution)/shard_map/ppermute | solution.py:528
  86.6 9.9 %collective-permute-start.32 = (bf16[272,512]{1,0:T(8,128)(2,1)S(1)}, bf16[272,512]{1,0:T(8,128)(2,1)S(1)}, u32[]{:S(2)}, u32[]{:S(2)}) collective-permute-start(bf16[272,512]{1,0:T(8,128)(2,1)S(1)} %out_projection.3.rest_6_.own_b), channel_id=1, source_target_pairs={{2,0},{4,2},{6,4},{7,6},{5,7},{3,5},{1,3},{0,1},{10,8},{12,10},{14... | collective-permute-start | bytes 835592 | tf_op jit(solution)/shard_map/ppermute | solution.py:529
  91.2 12.7 %collective-permute-start.37 = (bf16[256,512]{1,0:T(8,128)(2,1)S(1)}, bf16[256,512]{1,0:T(8,128)(2,1)S(1)}, u32[]{:S(2)}, u32[]{:S(2)}) collective-permute-start(bf16[256,512]{1,0:T(8,128)(2,1)S(1)} %collective-permute-done.33.rest_5_), channel_id=1, source_target_pairs={{0,2},{2,4},{4,6},{6,7},{7,5},{5,3},{3,1},{1,0},{8,10},{10,12},{12... | collective-permute-start | bytes 786440 | tf_op jit(solution)/shard_map/ppermute | solution.py:528
  92.8 11.1 %collective-permute-start.38 = (bf16[256,512]{1,0:T(8,128)(2,1)S(1)}, bf16[256,512]{1,0:T(8,128)(2,1)S(1)}, u32[]{:S(2)}, u32[]{:S(2)}) collective-permute-start(bf16[256,512]{1,0:T(8,128)(2,1)S(1)} %collective-permute-done.34.rest_7_), channel_id=1, source_target_pairs={{2,0},{4,2},{6,4},{7,6},{5,7},{3,5},{1,3},{0,1},{10,8},{12,10},{14... | collective-permute-start | bytes 786440 | tf_op jit(solution)/shard_map/ppermute | solution.py:529
  96.5 10.0 %collective-permute-start.35 = (bf16[272,512]{1,0:T(8,128)(2,1)S(1)}, bf16[272,512]{1,0:T(8,128)(2,1)S(1)}, u32[]{:S(2)}, u32[]{:S(2)}) collective-permute-start(bf16[272,512]{1,0:T(8,128)(2,1)S(1)} %collective-permute-done.31.rest_6_), channel_id=1, source_target_pairs={{0,2},{2,4},{4,6},{6,7},{7,5},{5,3},{3,1},{1,0},{8,10},{10,12},{12... | collective-permute-start | bytes 835592 | tf_op jit(solution)/shard_map/ppermute | solution.py:528
  98.0 10.0 %collective-permute-start.36 = (bf16[272,512]{1,0:T(8,128)(2,1)S(1)}, bf16[272,512]{1,0:T(8,128)(2,1)S(1)}, u32[]{:S(2)}, u32[]{:S(2)}) collective-permute-start(bf16[272,512]{1,0:T(8,128)(2,1)S(1)} %collective-permute-done.32.rest_8_), channel_id=1, source_target_pairs={{2,0},{4,2},{6,4},{7,6},{5,7},{3,5},{1,3},{0,1},{10,8},{12,10},{14... | collective-permute-start | bytes 835592 | tf_op jit(solution)/shard_map/ppermute | solution.py:529
  103.9 13.5 %collective-permute-start.39 = (bf16[256,512]{1,0:T(8,128)(2,1)S(1)}, bf16[256,512]{1,0:T(8,128)(2,1)S(1)}, u32[]{:S(2)}, u32[]{:S(2)}) collective-permute-start(bf16[256,512]{1,0:T(8,128)(2,1)S(1)} %collective-permute-done.37.rest_5_), channel_id=1, source_target_pairs={{0,2},{2,4},{4,6},{6,7},{7,5},{5,3},{3,1},{1,0},{8,10},{10,12},{12... | collective-permute-start | bytes 786440 | tf_op jit(solution)/shard_map/ppermute | solution.py:528
  105.5 11.9 %collective-permute-start.40 = (bf16[256,512]{1,0:T(8,128)(2,1)S(1)}, bf16[256,512]{1,0:T(8,128)(2,1)S(1)}, u32[]{:S(2)}, u32[]{:S(2)}) collective-permute-start(bf16[256,512]{1,0:T(8,128)(2,1)S(1)} %collective-permute-done.38.rest_7_), channel_id=1, source_target_pairs={{2,0},{4,2},{6,4},{7,6},{5,7},{3,5},{1,3},{0,1},{10,8},{12,10},{14... | collective-permute-start | bytes 786440 | tf_op jit(solution)/shard_map/ppermute | solution.py:529
  108.0 11.0 %collective-permute-start.42 = (bf16[272,512]{1,0:T(8,128)(2,1)S(1)}, bf16[272,512]{1,0:T(8,128)(2,1)S(1)}, u32[]{:S(2)}, u32[]{:S(2)}) collective-permute-start(bf16[272,512]{1,0:T(8,128)(2,1)S(1)} %collective-permute-done.35.rest_6_), channel_id=1, source_target_pairs={{0,2},{2,4},{4,6},{6,7},{7,5},{5,3},{3,1},{1,0},{8,10},{10,12},{12... | collective-permute-start | bytes 835592 | tf_op jit(solution)/shard_map/ppermute | solution.py:528
  109.6 9.4 %collective-permute-start.43 = (bf16[272,512]{1,0:T(8,128)(2,1)S(1)}, bf16[272,512]{1,0:T(8,128)(2,1)S(1)}, u32[]{:S(2)}, u32[]{:S(2)}) collective-permute-start(bf16[272,512]{1,0:T(8,128)(2,1)S(1)} %collective-permute-done.36.rest_8_), channel_id=1, source_target_pairs={{2,0},{4,2},{6,4},{7,6},{5,7},{3,5},{1,3},{0,1},{10,8},{12,10},{14... | collective-permute-start | bytes 835592 | tf_op jit(solution)/shard_map/ppermute | solution.py:529
  119.0 12.4 %collective-permute-start.44 = (bf16[272,512]{1,0:T(8,128)(2,1)S(1)}, bf16[272,512]{1,0:T(8,128)(2,1)S(1)}, u32[]{:S(2)}, u32[]{:S(2)}) collective-permute-start(bf16[272,512]{1,0:T(8,128)(2,1)S(1)} %collective-permute-done.43.rest_6_), channel_id=1, source_target_pairs={{2,0},{4,2},{6,4},{7,6},{5,7},{3,5},{1,3},{0,1},{10,8},{12,10},{14... | collective-permute-start | bytes 835592 | tf_op jit(solution)/shard_map/ppermute | solution.py:526
  138.3 9.5 %collective-permute-start.48 = (bf16[256,512]{1,0:T(8,128)(2,1)S(1)}, bf16[256,512]{1,0:T(8,128)(2,1)S(1)}, u32[]{:S(2)}, u32[]{:S(2)}) collective-permute-start(bf16[256,512]{1,0:T(8,128)(2,1)S(1)} %get-tuple-element.286), channel_id=1, source_target_pairs={{2,0},{4,2},{6,4},{7,6},{5,7},{3,5},{1,3},{0,1},{10,8},{12,10},{14... | collective-permute-start | bytes 786440 | tf_op jit(solution)/shard_map/ppermute | solution.py:552
  149.2 9.2 %collective-permute-start.51 = (bf16[256,512]{1,0:T(8,128)(2,1)S(1)}, bf16[256,512]{1,0:T(8,128)(2,1)S(1)}, u32[]{:S(2)}, u32[]{:S(2)}) collective-permute-start(bf16[256,512]{1,0:T(8,128)(2,1)S(1)} %get-tuple-element.287), channel_id=1, source_target_pairs={{0,2},{2,4},{4,6},{6,7},{7,5},{5,3},{3,1},{1,0},{8,10},{10,12},{12... | collective-permute-start | bytes 786440 | tf_op jit(solution)/shard_map/ppermute | solution.py:552
  151.2 9.2 %collective-permute-start.52 = (bf16[256,512]{1,0:T(8,128)(2,1)S(1)}, bf16[256,512]{1,0:T(8,128)(2,1)S(1)}, u32[]{:S(2)}, u32[]{:S(2)}) collective-permute-start(bf16[256,512]{1,0:T(8,128)(2,1)S(1)} %get-tuple-element.294), channel_id=1, source_target_pairs={{2,0},{4,2},{6,4},{7,6},{5,7},{3,5},{1,3},{0,1},{10,8},{12,10},{14... | collective-permute-start | bytes 786440 | tf_op jit(solution)/shard_map/ppermute | solution.py:552
  (43 other events, 406.3 us)
